TPU v7x, 512 devices: a whole 4x4x16 slice. The times are simulated.
512 devices in a mesh: ctx: 64 (over z_lo, y, core), head: 8 (over x, z_hi).
Axes of the slice: x: 4, y: 4, z: 16 (z_hi: 2, z_lo: 8; z = z_hi * 8 + z_lo), core: 2. Of those that a mesh axis runs over, the one named last changes fastest.
Arguments:
- query_states: bfloat16 [8192, 2048], P('ctx', 'head'), may hold values from -40 to 40
- key_states: bfloat16 [8192, 1024], P('ctx', 'head'), may hold values from -5 to 5
- value_states: bfloat16 [8192, 1024], P('ctx', 'head'), may hold values from -6 to 6
- out_weight: bfloat16 [4096, 2048], P(None, 'head'), may hold values from -0.125 to 0.125
- out_grad: bfloat16 [8192, 4096], P('ctx', 'head'), may hold values from -6 to 6
- doc_lengths: int32 [16], replicated, may hold values from 1 to 4096, 8192 in all
- block_order: int32 [128], replicated, may hold values from 0 to 127, each once
Outputs:
- projected: bfloat16 [8192, 4096], P('ctx', 'head')
- grad_query: bfloat16 [8192, 2048], P('ctx', 'head')
- grad_key: bfloat16 [8192, 1024], P('ctx', 'head')
- grad_value: bfloat16 [8192, 1024], P('ctx', 'head')
Inputs may be any that keep to these rules, and one draw needn't show every extreme that they name: `doc_lengths`: the lengths sum to 8192 and the longest is exactly 4096. `block_order`: each block number appears exactly once.
All inputs are finite; a program needn't handle non-finite values.
Results may differ from a plain program's by a relative error of at most 0.034.
Values may be sent and summed in bfloat16 or wider, within the bound.
No kernel may reach another device: no remote copies, remote signals or barrier semaphores. Data moves between devices by JAX's collectives and lax.ppermute only.
A program may use at most 64 MiB of HBM per device.

v0:
```python
import math

import jax
import jax.numpy as jnp
from jax import lax
from jax.sharding import PartitionSpec as P

HD = 128
BLOCK = 64


NEGATIVE = -1e30


def row_positions(block_order, first_row, count):
    blocks = lax.dynamic_slice_in_dim(block_order, first_row // BLOCK, count // BLOCK, 0)
    within = jnp.arange(BLOCK, dtype=jnp.int32)
    return (blocks[:, None] * BLOCK + within[None, :]).reshape(count)


def document_of(positions, doc_ends):
    return jnp.sum((positions[:, None] >= doc_ends[None, :]).astype(jnp.int32), axis=1)


def permitted(query_pos, query_doc, key_pos, key_doc):
    return (query_doc[:, None] == key_doc[None, :]) & (key_pos[None, :] <= query_pos[:, None])


def per_device(
    query_states, key_states, value_states, out_weight, out_grad, doc_lengths, block_order
):
    local_rows = query_states.shape[0]
    kv_heads = key_states.shape[1] // HD
    group_size = query_states.shape[1] // key_states.shape[1]
    score_scale = HD ** (-0.5)
    doc_ends = jnp.cumsum(doc_lengths)
    first_local = lax.axis_index("ctx") * local_rows
    query_pos = row_positions(block_order, first_local, local_rows)
    query_doc = document_of(query_pos, doc_ends)
    queries_local = query_states.reshape(local_rows, kv_heads, group_size, HD)
    keys_local = key_states.reshape(local_rows, kv_heads, HD)
    values_local = value_states.reshape(local_rows, kv_heads, HD)
    grad_attn = jnp.dot(
        lax.all_gather(out_grad, "head", axis=1, tiled=True),
        out_weight,
        preferred_element_type=jnp.float32,
    ).astype(jnp.bfloat16)
    grads_local = grad_attn.reshape(local_rows, kv_heads, group_size, HD)
    all_keys, all_values = (
        lax.all_gather(key_states, "ctx", axis=0, tiled=True),
        lax.all_gather(value_states, "ctx", axis=0, tiled=True),
    )
    total_rows = all_keys.shape[0]
    tile_rows = math.gcd(512, total_rows)
    tile_count = total_rows // tile_rows
    keys_whole = all_keys.reshape(total_rows, kv_heads, HD)
    values_whole = all_values.reshape(total_rows, kv_heads, HD)

    def key_tile(tile_index):
        tile_first = tile_index * tile_rows
        keys_tile = lax.dynamic_slice_in_dim(keys_whole, tile_first, tile_rows, 0)
        values_tile = lax.dynamic_slice_in_dim(values_whole, tile_first, tile_rows, 0)
        tile_pos = row_positions(block_order, tile_first, tile_rows)
        allowed = permitted(query_pos, query_doc, tile_pos, document_of(tile_pos, doc_ends))
        return (keys_tile, values_tile, allowed)

    def forward_step(tile_index, carried):
        keys_tile, values_tile, allowed = key_tile(tile_index)
        run_max, run_sum, weighted = carried
        scores = (
            jnp.einsum(
                "rkgd,nkd->kgrn", queries_local, keys_tile, preferred_element_type=jnp.float32
            )
            * score_scale
        )
        scores = jnp.where(allowed, scores, NEGATIVE)
        new_max = jnp.maximum(run_max, jnp.max(scores, axis=-1))
        factor = jnp.exp(run_max - new_max)
        weights = jnp.where(allowed, jnp.exp(scores - new_max[..., None]), 0.0)
        run_sum = run_sum * factor + jnp.sum(weights, axis=-1)
        weighted = weighted * factor[..., None] + jnp.einsum(
            "kgrn,nkd->kgrd",
            weights.astype(jnp.bfloat16),
            values_tile,
            preferred_element_type=jnp.float32,
        )
        return (new_max, run_sum, weighted)

    stat_shape = (kv_heads, group_size, local_rows)
    forward_start = (
        jnp.full(stat_shape, NEGATIVE, jnp.float32),
        jnp.zeros(stat_shape, jnp.float32),
        jnp.zeros(stat_shape + (HD,), jnp.float32),
    )
    run_max, run_sum, weighted = lax.fori_loop(0, tile_count, forward_step, forward_start)
    log_sums = run_max + jnp.log(run_sum)
    attn_four = (weighted / run_sum[..., None]).transpose(2, 0, 1, 3)
    attn_out = attn_four.reshape(local_rows, group_size * kv_heads * HD).astype(jnp.bfloat16)
    terms = jnp.einsum("rc,dc->rd", attn_out, out_weight, preferred_element_type=jnp.float32)
    projected = lax.psum_scatter(
        terms.astype(jnp.bfloat16), "head", scatter_dimension=1, tiled=True
    )
    attn_rows = attn_out.astype(jnp.float32).reshape(local_rows, kv_heads, group_size, HD)
    row_dots = jnp.sum(grads_local.astype(jnp.float32) * attn_rows, axis=-1).transpose(1, 2, 0)

    def query_step(tile_index, carried):
        keys_tile, values_tile, allowed = key_tile(tile_index)
        scores = (
            jnp.einsum(
                "rkgd,nkd->kgrn", queries_local, keys_tile, preferred_element_type=jnp.float32
            )
            * score_scale
        )
        scores = jnp.where(allowed, scores, NEGATIVE)
        normed = jnp.where(allowed, jnp.exp(scores - log_sums[..., None]), 0.0)
        grad_probs = jnp.einsum(
            "rkgd,nkd->kgrn", grads_local, values_tile, preferred_element_type=jnp.float32
        )
        grad_scores = (normed * (grad_probs - row_dots[..., None])).astype(jnp.bfloat16)
        return carried + jnp.einsum(
            "kgrn,nkd->rkgd", grad_scores, keys_tile, preferred_element_type=jnp.float32
        )

    query_accum = lax.fori_loop(
        0, tile_count, query_step, jnp.zeros((local_rows, kv_heads, group_size, HD), jnp.float32)
    )
    grad_query = (
        (query_accum * score_scale)
        .reshape(local_rows, group_size * kv_heads * HD)
        .astype(jnp.bfloat16)
    )
    sums_all, dots_all = (
        lax.all_gather(log_sums, "ctx", axis=2, tiled=True),
        lax.all_gather(row_dots, "ctx", axis=2, tiled=True),
    )
    empty_grads = jnp.zeros((local_rows, kv_heads, HD), jnp.float32)
    query_piece = lax.all_gather(query_states, "ctx", axis=0, tiled=True)
    piece_rows = query_piece.shape[0]
    inner_rows = math.gcd(512, piece_rows)
    query_rows = query_piece.reshape(piece_rows, kv_heads, group_size, HD)
    grad_rows = lax.all_gather(grad_attn, "ctx", axis=0, tiled=True).reshape(
        piece_rows, kv_heads, group_size, HD
    )

    def inner_step(inner_index, running):
        inner_first = inner_index * inner_rows
        query_tile = lax.dynamic_slice_in_dim(query_rows, inner_first, inner_rows, 0)
        grad_tile = lax.dynamic_slice_in_dim(grad_rows, inner_first, inner_rows, 0)
        tile_pos = row_positions(block_order, inner_first, inner_rows)
        allowed = permitted(tile_pos, document_of(tile_pos, doc_ends), query_pos, query_doc)
        sums_tile = lax.dynamic_slice_in_dim(sums_all, inner_first, inner_rows, 2)
        dots_tile = lax.dynamic_slice_in_dim(dots_all, inner_first, inner_rows, 2)
        grad_keys, grad_values = running
        scores = (
            jnp.einsum("nkgd,rkd->kgnr", query_tile, keys_local, preferred_element_type=jnp.float32)
            * score_scale
        )
        scores = jnp.where(allowed, scores, NEGATIVE)
        normed = jnp.where(allowed, jnp.exp(scores - sums_tile[..., None]), 0.0)
        grad_values = grad_values + jnp.einsum(
            "kgnr,nkgd->rkd",
            normed.astype(jnp.bfloat16),
            grad_tile,
            preferred_element_type=jnp.float32,
        )
        grad_probs = jnp.einsum(
            "nkgd,rkd->kgnr", grad_tile, values_local, preferred_element_type=jnp.float32
        )
        grad_scores = (normed * (grad_probs - dots_tile[..., None])).astype(jnp.bfloat16)
        grad_keys = grad_keys + jnp.einsum(
            "kgnr,nkgd->rkd", grad_scores, query_tile, preferred_element_type=jnp.float32
        )
        return (grad_keys, grad_values)

    grad_keys, grad_values = lax.fori_loop(
        0, piece_rows // inner_rows, inner_step, (empty_grads, empty_grads)
    )
    grad_key = (grad_keys * score_scale).reshape(local_rows, kv_heads * HD).astype(jnp.bfloat16)
    grad_value = grad_values.reshape(local_rows, kv_heads * HD).astype(jnp.bfloat16)
    return (projected, grad_query, grad_key, grad_value)


def solution(mesh):
    return jax.shard_map(
        per_device,
        mesh=mesh,
        in_specs=(
            P("ctx", "head"),
            P("ctx", "head"),
            P("ctx", "head"),
            P(None, "head"),
            P("ctx", "head"),
            P(),
            P(),
        ),
        out_specs=(P("ctx", "head"), P("ctx", "head"), P("ctx", "head"), P("ctx", "head")),
        check_vma=False,
    )
```

profile of v0, /device:TPU:24, one launch (start us, length us, event | category | flops | bytes accessed | tf_op | source)
XLA Modules:
  0.0 795.9 jit_solution(4067359919963549220)
XLA Ops:
  9.5 94.5 %all-gather.10.cloned.1.call-done = bf16[128,4096]{1,0:T(8,128)(2,1)} async-done(((bf16[128,512]{1,0:T(8,128)(2,1)}), bf16[128,4096]{1,0:T(8,128)(2,1)}) %all-gather.10.cloned.1.call-update) | async-done | bytes 1048592 | tf_op jit(solution)/shard_map/all_gather | solution.py:44
  104.0 2.3 convolution_convert_fusion.1
  109.8 105.8 %all-gather.6.cloned.1.call-done = bf16[8192,128]{1,0:T(8,128)(2,1)} async-done(((bf16[128,128]{1,0:T(8,128)(2,1)}), bf16[8192,128]{1,0:T(8,128)(2,1)}) %all-gather.6.cloned.1.call-update) | async-done | bytes 2097168 | tf_op jit(solution)/shard_map/all_gather | solution.py:50
  215.6 118.7 %all-gather.8.cloned.1.call-done = bf16[8192,128]{1,0:T(8,128)(2,1)} async-done(((bf16[128,128]{1,0:T(8,128)(2,1)}), bf16[8192,128]{1,0:T(8,128)(2,1)}) %all-gather.8.cloned.1.call-update) | async-done | bytes 2097168 | tf_op jit(solution)/shard_map/all_gather | solution.py:51
  334.3 52.9 %while.54 = (s32[]{:T(128)}, f32[1,2,128]{2,1,0:T(2,128)S(1)}, f32[1,2,128]{2,1,0:T(2,128)S(1)}, f32[1,2,128,128]{3,2,1,0:T(8,128)S(1)}, s32[128]{0:T(128)S(1)},...) while((s32[]{:T(128)}, f32[1,2,128]{2,1,0:T(2,128)S(1)}, ...), condition=%wide.region_6.7_spmd.clone, body=%wide.region_2.6_spmd.clone.sunk | while | flops 68609696 | bytes 2458706 | solution.py:95
  387.4 53.7 %while.55 = (s32[]{:T(128)}, f32[128,1,2,128]{0,3,2,1:T(8,128)S(1)}, bf16[8192,1,128]{2,0,1:T(8,128)(2,1)}, s32[128]{0:T(128)S(1)}, s32[128]{0:T(128)S(1)}, /*in...) while((s32[]{:T(128)}, ...), condition=%wide.region_11.12_spmd.clone, body=%wide.region_9.11_spmd.clone.sunk | while | flops 101867680 | bytes 1987155 | solution.py:124
  389.3 1.4 fusion.112
  392.6 1.4 fusion.112
  396.0 1.4 fusion.112
  399.3 1.4 fusion.112
  402.7 1.4 fusion.112
  406.1 1.4 fusion.112
  409.4 1.4 fusion.112
  412.8 1.4 fusion.112
  416.1 1.4 fusion.112
  419.5 1.4 fusion.112
  422.8 1.4 fusion.112
  426.2 1.4 fusion.112
  429.5 1.4 fusion.112
  432.9 1.4 fusion.112
  436.2 1.4 fusion.112
  439.6 1.4 fusion.112
  441.8 105.6 %all_gather.25 = f32[1,2,8192]{2,1,0:T(2,128)S(1)} all-gather(f32[1,2,128]{2,1,0:T(2,128)S(1)} %get-tuple-element.1619), channel_id=1, replica_groups=mesh['ctx'=64,'head'=8] {'ctx'}, dimensions={2}, use_global_device_ids=true | all-gather | bytes 66560 | tf_op jit(solution)/shard_map/all_gather | solution.py:133
  547.4 117.0 %all_gather.27 = f32[1,2,8192]{2,1,0:T(2,128)S(1)} all-gather(f32[1,2,128]{2,1,0:T(2,128)S(1)} %get-tuple-element.1616), channel_id=1, replica_groups=mesh['ctx'=64,'head'=8] {'ctx'}, dimensions={2}, use_global_device_ids=true | all-gather | bytes 66560 | tf_op jit(solution)/shard_map/all_gather | solution.py:134
  664.5 1.8 convolution_convert_fusion
  666.4 6.9 reshape.511
  673.3 78.3 %while.56 = (s32[]{:T(128)}, f32[128,1,128]{0,2,1:T(8,128)S(1)}, f32[128,1,128]{0,2,1:T(8,128)S(1)}, bf16[8192,1,2,128]{0,3,2,1:T(8,128)(2,1)}, s32[128]{0:T(128...) while((s32[]{:T(128)}, f32[128,1,128]{0,2,1:T(8,128)S(1)}, ...), condition=%wide.region_14.15_spmd.clone, body=%wide.region_12.14_spmd.clone.sunk | while | flops 135553184 | bytes 3646569 | solution.py:175
  705.9 1.4 fusion.119
  710.8 1.4 fusion.119
  740.2 1.4 fusion.119
  745.1 1.4 fusion.119
  753.1 36.0 %reduce-scatter.2.cloned.1.call-done = bf16[128,512]{1,0:T(8,128)(2,1)} async-done(((bf16[128,4096]{1,0:T(8,128)(2,1)}), bf16[128,512]{1,0:T(8,128)(2,1)}) %reduce-scatter.2.cloned.1.call-update) | async-done | bytes 131088 | tf_op jit(solution)/shard_map/reduce_scatter | solution.py:100
  (576 shorter events, 161.4 us)
Async XLA Ops:
  7.2 96.8 %copy-start = (bf16[4096,256]{1,0:T(8,128)(2,1)S(1)}, bf16[4096,256]{1,0:T(8,128)(2,1)}, u32[]{:S(2)}) copy-start(bf16[4096,256]{1,0:T(8,128)(2,1)} %param.16) | copy-start | bytes 6291460
  7.2 99.2 %copy-start.2 = (bf16[128,256]{1,0:T(8,128)(2,1)S(1)}, bf16[128,256]{1,0:T(8,128)(2,1)}, u32[]{:S(2)}) copy-start(bf16[128,256]{1,0:T(8,128)(2,1)} %param.13) | copy-start | bytes 196612
  7.2 100.1 %copy-start.5 = (s32[128]{0:T(128)S(1)}, s32[128]{0:T(128)}, u32[]{:S(2)}) copy-start(s32[128]{0:T(128)} %param.19) | copy-start | bytes 1540
  7.2 100.3 %copy-start.4 = (s32[16]{0:T(128)S(1)}, s32[16]{0:T(128)}, u32[]{:S(2)}) copy-start(s32[16]{0:T(128)} %param.18) | copy-start | bytes 196
  7.2 96.8 %all-gather.10.cloned.1.call-start = ((), (), s32[]{:S(2)}) async-start(), calls=%async_computation.4 | async-start | bytes 1179648 | tf_op jit(solution)/shard_map/all_gather | solution.py:44
  7.9 207.6 %all-gather.6.cloned.1.call-start = ((), (), s32[]{:S(2)}) async-start(), calls=%async_computation.1 | async-start | bytes 2129920 | tf_op jit(solution)/shard_map/all_gather | solution.py:50
  8.7 325.6 %all-gather.8.cloned.1.call-start = ((), (), s32[]{:S(2)}) async-start(), calls=%async_computation.2 | async-start | bytes 2129920 | tf_op jit(solution)/shard_map/all_gather | solution.py:51
  9.4 657.0 %all-gather.14.cloned.1.call-start = ((), (), s32[]{:S(2)}) async-start(), calls=%async_computation.6 | async-start | bytes 4259840 | tf_op jit(solution)/shard_map/all_gather | solution.py:141
  106.3 567.0 %all-gather.12.cloned.1.call-start = ((), (), s32[]{:S(2)}) async-start(), calls=%async_computation.5 | async-start | bytes 4259840 | tf_op jit(solution)/shard_map/all_gather | solution.py:137
  107.1 682.0 %reduce-scatter.2.cloned.1.call-start = ((), (), s32[]{:S(2)}) async-start(), calls=%async_computation.3 | async-start | bytes 1179648 | tf_op jit(solution)/shard_map/reduce_scatter | solution.py:100
  666.3 7.0 copy-start.1
  666.3 7.0 copy-start.3
Sparse Core Ops, SparseCore 0:
  11.1 92.8 all-gather.9
  106.1 109.3 all-gather.5
  217.7 116.4 all-gather.7
  336.3 119.3 all-gather.13
  457.6 122.2 all-gather.11
  666.5 122.5 reduce-scatter.1
where the time goes:
time: 799 us; the launch traced here: 796 us
  waiting for transfers between devices  357 us (45%)
  blocking collectives  223 us (28%)
  matrix products  133 us (17%)
  local copies, waits for them, and re-layouts  37.7 us (5%)
  other arithmetic  28.2 us (4%)
  between operations  14.3 us (2%)
    all_gather x1, waiting for transfers between devices, per_device(): lax.all_gather(value_states, 'ctx', axis=0, tiled=True)  119 us
    all_gather x1, blocking collectives, per_device(): lax.all_gather(row_dots, 'ctx', axis=2, tiled=True)  117 us
    all_gather x1, waiting for transfers between devices, per_device(): lax.all_gather(key_states, 'ctx', axis=0, tiled=True)  106 us
    all_gather x1, blocking collectives, per_device(): lax.all_gather(log_sums, 'ctx', axis=2, tiled=True)  106 us
    all_gather x1, waiting for transfers between devices, per_device(): lax.all_gather(out_grad, 'head', axis=1, tiled=True)  94.5 us
    reduce_scatter x1, waiting for transfers between devices, per_device(): lax.psum_scatter(terms.astype(jnp.bfloat16), 'head', scatter_dimension=1,...  36 us
    dot_general x16, matrix products, query_step(): jnp.einsum('kgrn,nkd->rkgd', grad_scores, keys_tile, preferred_element_ty...  22.9 us
    dot_general x16, matrix products, inner_step(): jnp.einsum('kgnr,nkgd->rkd', grad_scores, query_tile, preferred_element_t...  22.6 us
  transfers between devices with their start and end apart: 6, of which 4 were waited for; matrix products, arithmetic and copies ran while one was open for 25% of the time, Pallas kernels for 0%

commit v1 on v0

v1 whole, which is shorter than its diff:
```python
import functools
import math

import jax
import jax.numpy as jnp
from jax import lax
from jax.experimental import pallas as pl
from jax.experimental.pallas import tpu as pltpu
from jax.sharding import Mesh
from jax.sharding import PartitionSpec as P

HD = 128
BLOCK = 64
ROWS = 128
WIDE = 2 * HD
EXTRA = 16
CHUNK = 256
CHUNKS = 8
DOCS = 16
NEGATIVE = -1e30
SCALE = HD ** (-0.5)
SCALE2 = SCALE * math.log2(math.e)
VMEM = 40 * 1024 * 1024

NT = (((1,), (1,)), ((), ()))
NN = (((1,), (0,)), ((), ()))


def mm(a, b, dims):
    return lax.dot_general(a, b, dims, preferred_element_type=jnp.float32)


def heads_down(x):
    return jnp.concatenate([x[:, :HD], x[:, HD:]], axis=0)


def heads_across(x):
    return jnp.concatenate([x[:ROWS], x[ROWS:]], axis=1)


def split3(x):
    hi = x.astype(jnp.bfloat16)
    rest = x - hi.astype(jnp.float32)
    mid = rest.astype(jnp.bfloat16)
    low = (rest - mid.astype(jnp.float32)).astype(jnp.bfloat16)
    return hi, mid, low


def join3(rows, at):
    return rows[at : at + 1] + rows[at + 1 : at + 2] + rows[at + 2 : at + 3]


def query_rows(at_ref, order_ref, lengths_ref, t):
    z_lo, core = at_ref[0], at_ref[2]
    ctx = (z_lo * 4 + t) * 2 + core
    lane = lax.broadcasted_iota(jnp.int32, (1, WIDE), 1)
    row = lax.rem(lane, ROWS)
    first, second = order_ref[2 * ctx] * BLOCK, order_ref[2 * ctx + 1] * BLOCK
    pos = jnp.where(row < BLOCK, first + row, second + row - BLOCK)
    start = jnp.zeros_like(pos)
    end = 0
    for d in range(DOCS):
        end = end + lengths_ref[d]
        start = jnp.where(pos >= end, end, start)
    return pos, start


def key_base(at_ref, order_ref, block):
    z_lo, y, core = at_ref[0], at_ref[1], at_ref[2]
    part, z10, half = block // 8, (block // 2) % 4, block % 2
    z2 = z_lo // 4
    z2 = (1 - z2) if part % 2 else z2
    core = (1 - core) if part // 2 else core
    ctx = ((z2 * 4 + z10) * 4 + y) * 2 + core
    return order_ref[2 * ctx + half] * BLOCK


def allowed(pos, start, base):
    row = lax.broadcasted_iota(jnp.int32, (BLOCK, WIDE), 0)
    return (row >= start - base) & (row <= pos - base)


def kv_chunk(kv_refs, c, which):
    ref = kv_refs[c // 2]
    first = 2 * (c % 2)
    columns = slice(which * HD, (which + 1) * HD)
    return jnp.concatenate([ref[first, :, columns], ref[first + 1, :, columns]], axis=0)


def forward_kernel(
    at_ref, order_ref, lengths_ref, q_ref, kv0, kv1, kv2, kv3, out_ref, scores, v_t
):
    kv_refs = (kv0, kv1, kv2, kv3)
    for c in range(CHUNKS):
        v_t[:, c * CHUNK : (c + 1) * CHUNK] = kv_chunk(kv_refs, c, 1).T

    def tile(t, carried):
        queries = heads_down(q_ref[t])
        pos, start = query_rows(at_ref, order_ref, lengths_ref, t)
        top = jnp.full((1, WIDE), NEGATIVE, jnp.float32)
        for c in range(CHUNKS):
            s = mm(kv_chunk(kv_refs, c, 0), queries, NT)
            for b in range(CHUNK // BLOCK):
                base = key_base(at_ref, order_ref, c * 4 + b)
                part = jnp.where(
                    allowed(pos, start, base), s[b * BLOCK : (b + 1) * BLOCK], NEGATIVE
                )
                scores[pl.ds(c * CHUNK + b * BLOCK, BLOCK), :] = part
                top = jnp.maximum(top, jnp.max(part, axis=0, keepdims=True))
        top = jnp.maximum(top, 0.1 * NEGATIVE)
        total = jnp.zeros((1, WIDE), jnp.float32)
        acc = jnp.zeros((HD, WIDE), jnp.float32)
        for c in range(CHUNKS):
            e = jnp.exp2((scores[pl.ds(c * CHUNK, CHUNK), :] - top) * SCALE2)
            total = total + jnp.sum(e, axis=0, keepdims=True)
            acc = acc + mm(v_t[:, c * CHUNK : (c + 1) * CHUNK], e.astype(jnp.bfloat16), NN)
        some = total > 0
        safe = jnp.where(some, total, 1.0)
        out = (acc * (1.0 / safe)).T
        out_ref[t, :ROWS, :] = heads_across(out).astype(jnp.bfloat16)
        log_sum = jnp.where(some, top * SCALE2 + jnp.log2(safe), NEGATIVE)
        pad = jnp.zeros((EXTRA - 3, WIDE), jnp.float32)
        hi, mid, low = (v.astype(jnp.float32) for v in split3(log_sum))
        out_ref[t, ROWS:, :] = jnp.concatenate([hi, mid, low, pad], axis=0).astype(jnp.bfloat16)
        return carried

    lax.fori_loop(0, 4, tile, 0)


def combine_kernel(parts_ref, grad_ref, attn_ref, send_ref):
    sums = [join3(parts_ref[j, ROWS:, :].astype(jnp.float32), 0) for j in range(4)]
    top = functools.reduce(jnp.maximum, sums)
    weights = [jnp.exp2(s - top) for s in sums]
    total = functools.reduce(jnp.add, weights)
    log_sum = top + jnp.log2(total)
    inverse = 1.0 / total
    flat = []
    for w in weights:
        w = w * inverse
        flat += [w[:, :HD], w[:, HD:]]
    columns = jnp.concatenate(flat + [jnp.zeros((HD - 8, HD), jnp.float32)], axis=0).T
    halves, dots = [], []
    for h in range(2):
        lanes = slice(h * HD, (h + 1) * HD)
        acc = jnp.zeros((ROWS, HD), jnp.float32)
        for j in range(4):
            acc = acc + columns[:, 2 * j + h : 2 * j + h + 1] * parts_ref[
                j, :ROWS, lanes
            ].astype(jnp.float32)
        half = acc.astype(jnp.bfloat16)
        halves.append(half)
        dot = jnp.sum(
            half.astype(jnp.float32) * grad_ref[:, lanes].astype(jnp.float32),
            axis=1,
            keepdims=True,
        )
        dots.append(jnp.broadcast_to(dot, (ROWS, HD)).T[0:1])
    attn_ref[...] = jnp.concatenate(halves, axis=1)
    row_dots = jnp.concatenate(dots, axis=1)
    rows = [v.astype(jnp.float32) for v in split3(log_sum) + split3(row_dots)]
    extra = jnp.concatenate(rows + [jnp.zeros((EXTRA - 6, WIDE), jnp.float32)], axis=0)
    for j in range(4):
        send_ref[j, :ROWS, :] = grad_ref[...]
        send_ref[j, ROWS:, :] = extra.astype(jnp.bfloat16)


def backward_kernel(
    at_ref,
    order_ref,
    lengths_ref,
    q_ref,
    grad_ref,
    kv0,
    kv1,
    kv2,
    kv3,
    dq_ref,
    own_ref,
    far_ref,
    dk_acc,
    dv_acc,
    k_t,
):
    kv_refs = (kv0, kv1, kv2, kv3)
    for c in range(CHUNKS):
        k_t[:, c * CHUNK : (c + 1) * CHUNK] = kv_chunk(kv_refs, c, 0).T
    dk_acc[...] = jnp.zeros_like(dk_acc)
    dv_acc[...] = jnp.zeros_like(dv_acc)

    def tile(t, carried):
        queries = heads_down(q_ref[t])
        grads = heads_down(grad_ref[t, :ROWS, :])
        extra = grad_ref[t, ROWS:, :].astype(jnp.float32)
        log_sum, row_dots = join3(extra, 0), join3(extra, 3)
        pos, start = query_rows(at_ref, order_ref, lengths_ref, t)
        dq = jnp.zeros((HD, WIDE), jnp.float32)
        for c in range(CHUNKS):
            rows = pl.ds(c * CHUNK, CHUNK)
            s = mm(kv_chunk(kv_refs, c, 0), queries, NT)
            dp = mm(kv_chunk(kv_refs, c, 1), grads, NT)
            parts = []
            for b in range(CHUNK // BLOCK):
                base = key_base(at_ref, order_ref, c * 4 + b)
                raised = jnp.exp2(s[b * BLOCK : (b + 1) * BLOCK] * SCALE2 - log_sum)
                parts.append(jnp.where(allowed(pos, start, base), raised, 0.0))
            p = jnp.concatenate(parts, axis=0)
            ds = (p * (dp - row_dots)).astype(jnp.bfloat16)
            dv_acc[rows, :] += mm(p.astype(jnp.bfloat16), grads, NN)
            dk_acc[rows, :] += mm(ds, queries, NN)
            dq = dq + mm(k_t[:, c * CHUNK : (c + 1) * CHUNK], ds, NN)
        dq_ref[t] = heads_across((dq * SCALE).T).astype(jnp.bfloat16)
        return carried

    lax.fori_loop(0, 4, tile, 0)
    for part in range(4):
        ref = far_ref if part // 2 else own_ref
        for z10 in range(4):
            rows = pl.ds((part * 4 + z10) * ROWS, ROWS)
            ref[z10, part % 2, :, :HD] = (dk_acc[rows, :] * SCALE).astype(jnp.bfloat16)
            ref[z10, part % 2, :, HD:] = dv_acc[rows, :].astype(jnp.bfloat16)


def call(kernel, outs, scratch, smem, vmem, flops):
    specs = [pl.BlockSpec(memory_space=pltpu.SMEM)] * len(smem)
    specs += [pl.BlockSpec(memory_space=pltpu.VMEM)] * len(vmem)
    out_specs = [pl.BlockSpec(memory_space=pltpu.VMEM)] * len(outs)
    return pl.pallas_call(
        kernel,
        out_shape=[jax.ShapeDtypeStruct(o, jnp.bfloat16) for o in outs],
        in_specs=specs,
        out_specs=out_specs,
        scratch_shapes=scratch,
        compiler_params=pltpu.CompilerParams(vmem_limit_bytes=VMEM),
        cost_estimate=pl.CostEstimate(flops=flops, bytes_accessed=1 << 21, transcendentals=1 << 21),
    )(*smem, *vmem)


def spread(x, axis, n):
    return lax.all_to_all(jnp.broadcast_to(x, (n,) + x.shape), axis, 0, 0)


def swap(x, axis):
    return lax.ppermute(x, axis, [(0, 1), (1, 0)])


def per_device(
    query_states, key_states, value_states, out_weight, out_grad, doc_lengths, block_order
):
    z_hi = lax.axis_index("z_hi")
    z_lo = lax.axis_index("z2") * 4 + lax.axis_index("z10")
    at = jnp.stack([z_lo, lax.axis_index("y"), lax.axis_index("core")]).astype(jnp.int32)
    smem = (at, block_order, doc_lengths)

    other_grad = swap(out_grad, "z_hi")
    kv = jnp.concatenate([key_states, value_states], axis=1)
    kv_near = spread(kv, "z10", 4)
    kv_far = swap(kv_near, "z2")
    kv_near_core = swap(kv_near, "core")
    queries = spread(query_states, "y", 4)
    first, second = (
        jnp.where(z_hi == 0, out_grad, other_grad),
        jnp.where(z_hi == 0, other_grad, out_grad),
    )
    all_grad = spread(jnp.concatenate([first, second], axis=1), "x", 4)
    kv_far_core = swap(kv_far, "core")
    keys_values = (kv_near, kv_far, kv_near_core, kv_far_core)
    grad_attn = jnp.einsum(
        "xrd,xdc->rc",
        all_grad,
        out_weight.reshape(4, 1024, WIDE),
        preferred_element_type=jnp.float32,
    ).astype(jnp.bfloat16)

    (partial_out,) = call(
        forward_kernel,
        [(4, ROWS + EXTRA, WIDE)],
        [pltpu.VMEM((2048, WIDE), jnp.float32), pltpu.VMEM((HD, 2048), jnp.bfloat16)],
        smem,
        (queries,) + keys_values,
        1 << 30,
    )
    parts = lax.all_to_all(partial_out, "y", 0, 0)
    attn_out, send = call(
        combine_kernel,
        [(ROWS, WIDE), (4, ROWS + EXTRA, WIDE)],
        [],
        (),
        (parts, grad_attn),
        1 << 20,
    )
    grads = lax.all_to_all(send, "y", 0, 0)
    terms = jnp.einsum(
        "rc,xdc->xrd",
        attn_out,
        out_weight.reshape(4, 1024, WIDE),
        preferred_element_type=jnp.float32,
    ).astype(jnp.bfloat16)
    terms = lax.all_to_all(terms, "x", 0, 0)
    terms = jnp.sum(terms.astype(jnp.float32), axis=0)
    keep = jnp.where(z_hi == 0, terms[:, :512], terms[:, 512:])
    give = jnp.where(z_hi == 0, terms[:, 512:], terms[:, :512]).astype(jnp.bfloat16)
    got = swap(give, "z_hi")
    projected = (keep + got.astype(jnp.float32)).astype(jnp.bfloat16)

    dq, own, far = call(
        backward_kernel,
        [(4, ROWS, WIDE), (4, 2, ROWS, WIDE), (4, 2, ROWS, WIDE)],
        [
            pltpu.VMEM((2048, HD), jnp.float32),
            pltpu.VMEM((2048, HD), jnp.float32),
            pltpu.VMEM((HD, 2048), jnp.bfloat16),
        ],
        smem,
        (queries, grads) + keys_values,
        1 << 31,
    )
    far = swap(far, "core")
    both = (own.astype(jnp.float32) + far.astype(jnp.float32)).astype(jnp.bfloat16)
    both = jnp.sum(lax.all_to_all(both, "z10", 0, 0).astype(jnp.float32), axis=0)
    late = swap(both[1].astype(jnp.bfloat16), "z2")
    dq = jnp.sum(lax.all_to_all(dq, "y", 0, 0).astype(jnp.float32), axis=0)
    grad_query = dq.astype(jnp.bfloat16)
    grad_kv = (both[0] + late.astype(jnp.float32)).astype(jnp.bfloat16)
    return projected, grad_query, grad_kv[:, :HD], grad_kv[:, HD:]


def solution(mesh):
    fine = Mesh(
        mesh.devices.reshape(2, 4, 4, 2, 4, 2), ("z2", "z10", "y", "core", "x", "z_hi")
    )
    ctx, head = ("z2", "z10", "y", "core"), ("x", "z_hi")
    both = P(ctx, head)
    return jax.shard_map(
        per_device,
        mesh=fine,
        in_specs=(both, both, both, P(None, head), both, P(), P()),
        out_specs=(both, both, both, both),
        check_vma=False,
    )
```

time: 799 us -> 188 us (0.24)
  waiting for transfers between devices: 357 us -> 50.8 us
  blocking collectives: 223 us -> 9.22 us
  matrix products: 133 us -> 3.47 us
  starting transfers between devices: 0.24 us -> 91.2 us
  local copies, waits for them, and re-layouts: 37.7 us -> 5.03 us
  other arithmetic: 28.2 us -> 6.61 us
  Pallas kernels: 0 us -> 19 us
  between operations: 14.3 us -> 0.82 us
    all_gather x5 -> x0, waiting for transfers between devices: 319 us -> none  [the longest x1 119 us: per_device(): lax.all_gather(value_states, 'ctx', axis=0, tiled=True)]
    all_gather x2 -> x0, blocking collectives: 223 us -> none  [the longest x1 117 us: per_device(): lax.all_gather(row_dots, 'ctx', axis=2, tiled=True)]
    dot_general x114 -> x2, matrix products: 133 us -> 3.47 us  [the longest x1 1.8 us: per_device(): jnp.einsum('rc,xdc->xrd', attn_out, out_weight.reshape(4, 1024, WIDE), pr...]
    ppermute x0 -> x7, starting transfers between devices: none -> 55.6 us  [swap(): return lax.ppermute(x, axis, [(0, 1), (1, 0)])]
    reduce_scatter x1 -> x0, waiting for transfers between devices: 36 us -> none  [per_device(): lax.psum_scatter(terms.astype(jnp.bfloat16), 'head', scatter_dimension=1,...]
    all_to_all x0 -> x7, starting transfers between devices: none -> 35.6 us  [the longest x3 16.7 us: spread(): return lax.all_to_all(jnp.broadcast_to(x, (n,) + x.shape), axis, 0, 0)]
    ppermute x0 -> x7, waiting for transfers between devices: none -> 26.6 us  [swap(): return lax.ppermute(x, axis, [(0, 1), (1, 0)])]
    all_to_all x0 -> x7, waiting for transfers between devices: none -> 24.2 us  [the longest x1 14 us: per_device(): terms = lax.all_to_all(terms, 'x', 0, 0)]
  transfers between devices with their start and end apart: 6 -> 14, of which waited for: 4 -> 9; matrix products, arithmetic and copies ran while one was open for 25% -> 5% of each run, Pallas kernels for 0% -> 4%
where the time goes in v1:
time: 188 us; the launch traced here: 186 us
  starting transfers between devices  91.2 us (49%)
  waiting for transfers between devices  50.8 us (27%)
  Pallas kernels  19 us (10%)
  blocking collectives  9.22 us (5%)
  other arithmetic  6.61 us (4%)
  local copies, waits for them, and re-layouts  5.03 us (3%)
  matrix products  3.47 us (2%)
    ppermute x7, starting transfers between devices, swap(): return lax.ppermute(x, axis, [(0, 1), (1, 0)])  55.6 us
    ppermute x7, waiting for transfers between devices, swap(): return lax.ppermute(x, axis, [(0, 1), (1, 0)])  26.6 us
    pallas_call x3, Pallas kernels, call(): pl.pallas_call(kernel, out_shape=[jax.ShapeDtypeStruct(o, jnp.bfloat16) f...  19 us
    all_to_all x3, starting transfers between devices, spread(): return lax.all_to_all(jnp.broadcast_to(x, (n,) + x.shape), axis, 0, 0)  16.7 us
    all_to_all x1, waiting for transfers between devices, per_device(): terms = lax.all_to_all(terms, 'x', 0, 0)  14 us
    all_to_all x1, blocking collectives, per_device(): grads = lax.all_to_all(send, 'y', 0, 0)  9.22 us
    all_to_all x1, starting transfers between devices, per_device(): parts = lax.all_to_all(partial_out, 'y', 0, 0)  5.55 us
    all_to_all x1, starting transfers between devices, per_device(): dq = jnp.sum(lax.all_to_all(dq, 'y', 0, 0).astype(jnp.float32), axis=0)  5.43 us
  transfers between devices with their start and end apart: 14, of which 9 were waited for; matrix products, arithmetic and copies ran while one was open for 5% of the time, Pallas kernels for 4%

profile of v1, /device:TPU:24, one launch (start us, length us, event | category | flops | bytes accessed | tf_op | source)
XLA Modules:
  0.0 186.2 jit_solution(10044917764173721102)
XLA Ops:
  0.6 1.7 broadcast_in_dim.9
  2.4 9.0 %all-to-all-start = ((bf16[4,128,256]{2,1,0:T(8,128)(2,1)}), bf16[4,128,256]{2,1,0:T(8,128)(2,1)S(1)}, u32[]{:S(2)}, u32[]{:S(2)}) async-start(bf16[4,128,256]{2,1,0:T(8,128)(2,1)} %broadcast_in_dim.9), calls=%async_computation | async-start | bytes 524288 | tf_op jit(solution)/shard_map/all_to_all | solution.py:239
  12.1 3.8 %all-to-all-done.q_ref = bf16[4,128,256]{2,1,0:T(8,128)(2,1)S(1)} async-done(((bf16[4,128,256]{2,1,0:T(8,128)(2,1)}), bf16[4,128,256]{2,1,0:T(8,128)(2,1)S(1)}, u32[]{:S(2)}, u32[]{:S(2)}) %all-to-all-start) | async-done | bytes 262176 | tf_op jit(solution)/shard_map/all_to_all | solution.py:239
  16.7 3.4 %all-to-all-start.1 = ((bf16[4,128,256]{2,1,0:T(8,128)(2,1)}), bf16[4,128,256]{2,1,0:T(8,128)(2,1)S(1)}, u32[]{:S(2)}, u32[]{:S(2)}) async-start(bf16[4,128,256]{2,1,0:T(8,128)(2,1)} %broadcast_in_dim.10), calls=%async_computation.1 | async-start | bytes 524288 | tf_op jit(solution)/shard_map/all_to_all | solution.py:239
  20.1 11.4 %collective-permute-start.3 = (bf16[128,512]{1,0:T(8,128)(2,1)}, bf16[128,512]{1,0:T(8,128)(2,1)S(1)}, u32[]{:S(2)}, u32[]{:S(2)}) collective-permute-start(bf16[128,512]{1,0:T(8,128)(2,1)} %param.11), channel_id=1, source_target_pairs={{0,1},{1,0},{2,3},{3,2},{4,5},{5,4},{6,7},{7,6},{8,9},{9,8},{10,11... | collective-permute-start | bytes 393224 | tf_op jit(solution)/shard_map/ppermute | solution.py:243
  31.5 4.8 %collective-permute-done.3 = bf16[128,512]{1,0:T(8,128)(2,1)S(1)} collective-permute-done((bf16[128,512]{1,0:T(8,128)(2,1)}, bf16[128,512]{1,0:T(8,128)(2,1)S(1)}, u32[]{:S(2)}, u32[]{:S(2)}) %collective-permute-start.3) | collective-permute-done | bytes 131104 | tf_op jit(solution)/shard_map/ppermute | solution.py:243
  36.3 0.9 broadcast_select_fusion.1
  37.3 1.1 broadcast_in_dim.11
  38.4 4.3 %all-to-all-start.3 = ((bf16[4,128,1024]{2,1,0:T(8,128)(2,1)}), bf16[4,128,1024]{2,1,0:T(8,128)(2,1)}, u32[]{:S(2)}, u32[]{:S(2)}) async-start(bf16[4,128,1024]{2,1,0:T(8,128)(2,1)} %broadcast_in_dim.11), calls=%async_computation.3 | async-start | bytes 2097152 | tf_op jit(solution)/shard_map/all_to_all | solution.py:239
  42.7 8.9 %collective-permute-start = (bf16[4,128,256]{2,1,0:T(8,128)(2,1)S(1)}, bf16[4,128,256]{2,1,0:T(8,128)(2,1)S(1)}, u32[]{:S(2)}, u32[]{:S(2)}) collective-permute-start(bf16[4,128,256]{2,1,0:T(8,128)(2,1)S(1)} %all-to-all-done.1.kv0), channel_id=1, source_target_pairs={{0,256},{256,0},{1,257},{257,1},{2,258},{258,2},{3,259},{259,3},{4... | collective-permute-start | bytes 786440 | tf_op jit(solution)/shard_map/ppermute | solution.py:243
  51.7 1.9 %collective-permute-start.1 = (bf16[4,128,256]{2,1,0:T(8,128)(2,1)S(1)}, bf16[4,128,256]{2,1,0:T(8,128)(2,1)S(1)}, u32[]{:S(2)}, u32[]{:S(2)}) collective-permute-start(bf16[4,128,256]{2,1,0:T(8,128)(2,1)S(1)} %all-to-all-done.1.kv0), channel_id=1, source_target_pairs={{0,8},{8,0},{1,9},{9,1},{2,10},{10,2},{3,11},{11,3},{4,12},{12,4},... | collective-permute-start | bytes 786440 | tf_op jit(solution)/shard_map/ppermute | solution.py:243
  53.6 19.8 %collective-permute-done.kv1 = bf16[4,128,256]{2,1,0:T(8,128)(2,1)S(1)} collective-permute-done((bf16[4,128,256]{2,1,0:T(8,128)(2,1)S(1)}, bf16[4,128,256]{2,1,0:T(8,128)(2,1)S(1)}, u32[]{:S(2)}, u32[]{:S(2)}) %collective-permute-start) | collective-permute-done | bytes 262176 | tf_op jit(solution)/shard_map/ppermute | solution.py:243
  73.4 1.9 %collective-permute-start.2 = (bf16[4,128,256]{2,1,0:T(8,128)(2,1)S(1)}, bf16[4,128,256]{2,1,0:T(8,128)(2,1)S(1)}, u32[]{:S(2)}, u32[]{:S(2)}) collective-permute-start(bf16[4,128,256]{2,1,0:T(8,128)(2,1)S(1)} %collective-permute-done.kv1), channel_id=1, source_target_pairs={{0,8},{8,0},{1,9},{9,1},{2,10},{10,2},{3,11},{11,3},{4,12},{12,4},... | collective-permute-start | bytes 786440 | tf_op jit(solution)/shard_map/ppermute | solution.py:243
  75.4 1.4 collective-permute-done.2.kv3
  76.8 7.8 %shard_map.102 = bf16[4,144,256]{2,1,0:T(8,128)(2,1)} custom-call(s32[3]{0:T(128)S(1)} %pad_add_fusion.at_ref, s32[128]{0:T(128)S(1)} %copy-done.6, s32[16]{0:T(128)S(1)} %copy-done.7, bf16[4,128,256]{2,1,0:T(8,128)(2,1)S(1)} %all-to-all-done.q_ref, bf16[4,128,256]{2,1,0:T(8,128)(2,1)S(1)} %all-to-all-done.1.kv0, ...), custom_call_target="tpu_custom_call" | custom-call | flops 1073741824 | bytes 2097152 | tf_op jit(solution)/shard_map/pallas_call | solution.py:227
  84.6 5.6 %all-to-all-start.2 = ((bf16[4,144,256]{2,1,0:T(8,128)(2,1)}), bf16[4,144,256]{2,1,0:T(8,128)(2,1)S(1)}, u32[]{:S(2)}, u32[]{:S(2)}) async-start(bf16[4,144,256]{2,1,0:T(8,128)(2,1)} %shard_map.102), calls=%async_computation.2 | async-start | bytes 589824 | tf_op jit(solution)/shard_map/all_to_all | solution.py:282
  90.2 1.7 fusion.1.grad_ref
  91.9 3.9 %all-to-all-done.2.parts_ref = bf16[4,144,256]{2,1,0:T(8,128)(2,1)S(1)} async-done(((bf16[4,144,256]{2,1,0:T(8,128)(2,1)}), bf16[4,144,256]{2,1,0:T(8,128)(2,1)S(1)}, u32[]{:S(2)}, u32[]{:S(2)}) %all-to-all-start.2) | async-done | bytes 294944 | tf_op jit(solution)/shard_map/all_to_all | solution.py:282
  96.4 9.2 %all_to_all.40.grad_ref = bf16[4,144,256]{2,1,0:T(8,128)(2,1)S(1)} all-to-all(bf16[4,144,256]{2,1,0:T(8,128)(2,1)S(1)} %get-tuple-element.10), channel_id=1, replica_groups=mesh['z2'=2,'z10'=4,'y'=4,'core'=2,'x'=4,'z_hi'=2] {'y'}, dimensions={0} | all-to-all | bytes 589824 | tf_op jit(solution)/shard_map/all_to_all | solution.py:291
  105.6 10.6 %shard_map.104 = (bf16[4,128,256]{2,1,0:T(8,128)(2,1)}, bf16[4,2,128,256]{3,2,1,0:T(8,128)(2,1)S(1)}, bf16[4,2,128,256]{3,2,1,0:T(8,128)(2,1)S(1)}) custom-call(s32[3]{0:T(128)S(1)} %pad_add_fusion.at_ref, s32[128]{0:T(128)S(1)} %copy-done.6, s32[16]{0:T(128)S(1)} %copy-done.7, bf16[4,128,256]{2,1,0:T(8,128)(2,1)S(1)} %all-to-all-done.q_ref, ...), custom_call_target="tpu_custom_call" | custom-call | flops 2147483648 | bytes 2097152 | tf_op jit(solution)/shard_map/pallas_call | solution.py:227
  117.0 5.4 %all-to-all-start.6 = ((bf16[4,128,256]{2,1,0:T(8,128)(2,1)}), bf16[4,128,256]{2,1,0:T(8,128)(2,1)S(1)}, u32[]{:S(2)}, u32[]{:S(2)}) async-start(bf16[4,128,256]{2,1,0:T(8,128)(2,1)} %get-tuple-element.11), calls=%async_computation.6 | async-start | bytes 524288 | tf_op jit(solution)/shard_map/all_to_all | solution.py:321
  122.4 1.9 %collective-permute-start.5 = (bf16[4,2,128,256]{3,2,1,0:T(8,128)(2,1)}, bf16[4,2,128,256]{3,2,1,0:T(8,128)(2,1)S(1)}, u32[]{:S(2)}, u32[]{:S(2)}) collective-permute-start(bf16[4,2,128,256]{3,2,1,0:T(8,128)(2,1)} %copy-done.1), channel_id=1, source_target_pairs={{0,8},{8,0},{1,9},{9,1},{2,10},{10,2},{3,11},{11,3},{4,12},{12,4},... | collective-permute-start | bytes 1572872 | tf_op jit(solution)/shard_map/ppermute | solution.py:243
  124.3 1.8 fusion
  127.0 4.5 %all-to-all-start.4 = ((bf16[4,128,1024]{2,1,0:T(8,128)(2,1)}), bf16[4,128,1024]{2,1,0:T(8,128)(2,1)}, u32[]{:S(2)}, u32[]{:S(2)}) async-start(bf16[4,128,1024]{2,1,0:T(8,128)(2,1)} %fusion), calls=%async_computation.4 | async-start | bytes 2097152 | tf_op jit(solution)/shard_map/all_to_all | solution.py:298
  131.5 0.9 add_convert_fusion
  132.4 14.0 %all-to-all-done.4 = bf16[4,128,1024]{2,1,0:T(8,128)(2,1)} async-done(((bf16[4,128,1024]{2,1,0:T(8,128)(2,1)}), bf16[4,128,1024]{2,1,0:T(8,128)(2,1)}, u32[]{:S(2)}, u32[]{:S(2)}) %all-to-all-start.4) | async-done | bytes 1048608 | tf_op jit(solution)/shard_map/all_to_all | solution.py:298
  146.5 3.5 %all-to-all-start.7 = ((bf16[4,2,128,256]{3,2,1,0:T(8,128)(2,1)}), bf16[4,2,128,256]{3,2,1,0:T(8,128)(2,1)S(1)}, u32[]{:S(2)}, u32[]{:S(2)}) async-start(bf16[4,2,128,256]{3,2,1,0:T(8,128)(2,1)} %add_convert_fusion), calls=%async_computation.7 | async-start | bytes 1048576 | tf_op jit(solution)/shard_map/all_to_all | solution.py:319
  150.6 1.5 convert_reduce_fusion
  152.1 9.6 %collective-permute-start.4 = (bf16[128,512]{1,0:T(8,128)(2,1)S(1)}, bf16[128,512]{1,0:T(8,128)(2,1)}, u32[]{:S(2)}, u32[]{:S(2)}) collective-permute-start(bf16[128,512]{1,0:T(8,128)(2,1)S(1)} %select_convert_fusion), channel_id=1, source_target_pairs={{0,1},{1,0},{2,3},{3,2},{4,5},{5,4},{6,7},{7,6},{8,9},{9,8},{10,11... | collective-permute-start | bytes 393224 | tf_op jit(solution)/shard_map/ppermute | solution.py:243
  161.8 1.6 all-to-all-done.7
  163.4 19.9 %collective-permute-start.6 = (bf16[128,256]{1,0:T(8,128)(2,1)S(1)}, bf16[128,256]{1,0:T(8,128)(2,1)S(1)}, u32[]{:S(2)}, u32[]{:S(2)}) collective-permute-start(bf16[128,256]{1,0:T(8,128)(2,1)S(1)} %fusion.4), channel_id=1, source_target_pairs={{0,256},{256,0},{1,257},{257,1},{2,258},{258,2},{3,259},{259,3},{4... | collective-permute-start | bytes 196616 | tf_op jit(solution)/shard_map/ppermute | solution.py:243
  183.3 1.6 add_convert_fusion.1
  (34 shorter events, 6.0 us)
Async XLA Ops:
  0.6 89.6 %copy-start = (bf16[4096,256]{1,0:T(8,128)(2,1)S(1)}, bf16[4096,256]{1,0:T(8,128)(2,1)}, u32[]{:S(2)}) copy-start(bf16[4096,256]{1,0:T(8,128)(2,1)} %param.10) | copy-start | bytes 6291460
  2.4 13.6 %all-to-all-start = ((bf16[4,128,256]{2,1,0:T(8,128)(2,1)}), bf16[4,128,256]{2,1,0:T(8,128)(2,1)S(1)}, u32[]{:S(2)}, u32[]{:S(2)}) async-start(bf16[4,128,256]{2,1,0:T(8,128)(2,1)} %broadcast_in_dim.9), calls=%async_computation | async-start | bytes 524288 | tf_op jit(solution)/shard_map/all_to_all | solution.py:239
  16.7 20.6 %all-to-all-start.1 = ((bf16[4,128,256]{2,1,0:T(8,128)(2,1)}), bf16[4,128,256]{2,1,0:T(8,128)(2,1)S(1)}, u32[]{:S(2)}, u32[]{:S(2)}) async-start(bf16[4,128,256]{2,1,0:T(8,128)(2,1)} %broadcast_in_dim.10), calls=%async_computation.1 | async-start | bytes 524288 | tf_op jit(solution)/shard_map/all_to_all | solution.py:239
  20.1 16.3 %collective-permute-start.3 = (bf16[128,512]{1,0:T(8,128)(2,1)}, bf16[128,512]{1,0:T(8,128)(2,1)S(1)}, u32[]{:S(2)}, u32[]{:S(2)}) collective-permute-start(bf16[128,512]{1,0:T(8,128)(2,1)} %param.11), channel_id=1, source_target_pairs={{0,1},{1,0},{2,3},{3,2},{4,5},{5,4},{6,7},{7,6},{8,9},{9,8},{10,11... | collective-permute-start | bytes 393224 | tf_op jit(solution)/shard_map/ppermute | solution.py:243
  37.3 39.5 %copy-start.6 = (s32[128]{0:T(128)S(1)}, s32[128]{0:T(128)}, u32[]{:S(2)}) copy-start(s32[128]{0:T(128)} %order_ref.3) | copy-start | bytes 1540
  37.3 39.5 %copy-start.7 = (s32[16]{0:T(128)S(1)}, s32[16]{0:T(128)}, u32[]{:S(2)}) copy-start(s32[16]{0:T(128)} %lengths_ref.3) | copy-start | bytes 196
  38.4 46.2 %all-to-all-start.3 = ((bf16[4,128,1024]{2,1,0:T(8,128)(2,1)}), bf16[4,128,1024]{2,1,0:T(8,128)(2,1)}, u32[]{:S(2)}, u32[]{:S(2)}) async-start(bf16[4,128,1024]{2,1,0:T(8,128)(2,1)} %broadcast_in_dim.11), calls=%async_computation.3 | async-start | bytes 2097152 | tf_op jit(solution)/shard_map/all_to_all | solution.py:239
  42.7 30.7 %collective-permute-start = (bf16[4,128,256]{2,1,0:T(8,128)(2,1)S(1)}, bf16[4,128,256]{2,1,0:T(8,128)(2,1)S(1)}, u32[]{:S(2)}, u32[]{:S(2)}) collective-permute-start(bf16[4,128,256]{2,1,0:T(8,128)(2,1)S(1)} %all-to-all-done.1.kv0), channel_id=1, source_target_pairs={{0,256},{256,0},{1,257},{257,1},{2,258},{258,2},{3,259},{259,3},{4... | collective-permute-start | bytes 786440 | tf_op jit(solution)/shard_map/ppermute | solution.py:243
  51.7 23.7 %collective-permute-start.1 = (bf16[4,128,256]{2,1,0:T(8,128)(2,1)S(1)}, bf16[4,128,256]{2,1,0:T(8,128)(2,1)S(1)}, u32[]{:S(2)}, u32[]{:S(2)}) collective-permute-start(bf16[4,128,256]{2,1,0:T(8,128)(2,1)S(1)} %all-to-all-done.1.kv0), channel_id=1, source_target_pairs={{0,8},{8,0},{1,9},{9,1},{2,10},{10,2},{3,11},{11,3},{4,12},{12,4},... | collective-permute-start | bytes 786440 | tf_op jit(solution)/shard_map/ppermute | solution.py:243
  73.4 3.4 %collective-permute-start.2 = (bf16[4,128,256]{2,1,0:T(8,128)(2,1)S(1)}, bf16[4,128,256]{2,1,0:T(8,128)(2,1)S(1)}, u32[]{:S(2)}, u32[]{:S(2)}) collective-permute-start(bf16[4,128,256]{2,1,0:T(8,128)(2,1)S(1)} %collective-permute-done.kv1), channel_id=1, source_target_pairs={{0,8},{8,0},{1,9},{9,1},{2,10},{10,2},{3,11},{11,3},{4,12},{12,4},... | collective-permute-start | bytes 786440 | tf_op jit(solution)/shard_map/ppermute | solution.py:243
  75.4 9.2 %copy-start.2 = (bf16[4,128,256]{2,1,0:T(8,128)(2,1)}, bf16[4,128,256]{2,1,0:T(8,128)(2,1)S(1)}, u32[]{:S(2)}) copy-start(bf16[4,128,256]{2,1,0:T(8,128)(2,1)S(1)} %collective-permute-done.1.kv2) | copy-start | bytes 786436
  76.8 7.8 %copy-start.4 = (bf16[4,128,256]{2,1,0:T(8,128)(2,1)}, bf16[4,128,256]{2,1,0:T(8,128)(2,1)S(1)}, u32[]{:S(2)}) copy-start(bf16[4,128,256]{2,1,0:T(8,128)(2,1)S(1)} %collective-permute-done.2.kv3) | copy-start | bytes 786436
  84.6 11.1 %all-to-all-start.2 = ((bf16[4,144,256]{2,1,0:T(8,128)(2,1)}), bf16[4,144,256]{2,1,0:T(8,128)(2,1)S(1)}, u32[]{:S(2)}, u32[]{:S(2)}) async-start(bf16[4,144,256]{2,1,0:T(8,128)(2,1)} %shard_map.102), calls=%async_computation.2 | async-start | bytes 589824 | tf_op jit(solution)/shard_map/all_to_all | solution.py:282
  95.7 9.9 %copy-start.3 = (bf16[4,128,256]{2,1,0:T(8,128)(2,1)S(1)}, bf16[4,128,256]{2,1,0:T(8,128)(2,1)}, u32[]{:S(2)}) copy-start(bf16[4,128,256]{2,1,0:T(8,128)(2,1)} %copy-done.2) | copy-start | bytes 786436
  95.7 9.9 %copy-start.5 = (bf16[4,128,256]{2,1,0:T(8,128)(2,1)S(1)}, bf16[4,128,256]{2,1,0:T(8,128)(2,1)}, u32[]{:S(2)}) copy-start(bf16[4,128,256]{2,1,0:T(8,128)(2,1)} %copy-done.4) | copy-start | bytes 786436
  116.2 0.8 copy-start.1
  117.0 10.0 %all-to-all-start.6 = ((bf16[4,128,256]{2,1,0:T(8,128)(2,1)}), bf16[4,128,256]{2,1,0:T(8,128)(2,1)S(1)}, u32[]{:S(2)}, u32[]{:S(2)}) async-start(bf16[4,128,256]{2,1,0:T(8,128)(2,1)} %get-tuple-element.11), calls=%async_computation.6 | async-start | bytes 524288 | tf_op jit(solution)/shard_map/all_to_all | solution.py:321
  122.4 9.1 %collective-permute-start.5 = (bf16[4,2,128,256]{3,2,1,0:T(8,128)(2,1)}, bf16[4,2,128,256]{3,2,1,0:T(8,128)(2,1)S(1)}, u32[]{:S(2)}, u32[]{:S(2)}) collective-permute-start(bf16[4,2,128,256]{3,2,1,0:T(8,128)(2,1)} %copy-done.1), channel_id=1, source_target_pairs={{0,8},{8,0},{1,9},{9,1},{2,10},{10,2},{3,11},{11,3},{4,12},{12,4},... | collective-permute-start | bytes 1572872 | tf_op jit(solution)/shard_map/ppermute | solution.py:243
  127.0 19.5 %all-to-all-start.4 = ((bf16[4,128,1024]{2,1,0:T(8,128)(2,1)}), bf16[4,128,1024]{2,1,0:T(8,128)(2,1)}, u32[]{:S(2)}, u32[]{:S(2)}) async-start(bf16[4,128,1024]{2,1,0:T(8,128)(2,1)} %fusion), calls=%async_computation.4 | async-start | bytes 2097152 | tf_op jit(solution)/shard_map/all_to_all | solution.py:298
  146.5 16.9 %all-to-all-start.7 = ((bf16[4,2,128,256]{3,2,1,0:T(8,128)(2,1)}), bf16[4,2,128,256]{3,2,1,0:T(8,128)(2,1)S(1)}, u32[]{:S(2)}, u32[]{:S(2)}) async-start(bf16[4,2,128,256]{3,2,1,0:T(8,128)(2,1)} %add_convert_fusion), calls=%async_computation.7 | async-start | bytes 1048576 | tf_op jit(solution)/shard_map/all_to_all | solution.py:319
  152.1 31.2 %collective-permute-start.4 = (bf16[128,512]{1,0:T(8,128)(2,1)S(1)}, bf16[128,512]{1,0:T(8,128)(2,1)}, u32[]{:S(2)}, u32[]{:S(2)}) collective-permute-start(bf16[128,512]{1,0:T(8,128)(2,1)S(1)} %select_convert_fusion), channel_id=1, source_target_pairs={{0,1},{1,0},{2,3},{3,2},{4,5},{5,4},{6,7},{7,6},{8,9},{9,8},{10,11... | collective-permute-start | bytes 393224 | tf_op jit(solution)/shard_map/ppermute | solution.py:243
  163.4 22.1 %collective-permute-start.6 = (bf16[128,256]{1,0:T(8,128)(2,1)S(1)}, bf16[128,256]{1,0:T(8,128)(2,1)S(1)}, u32[]{:S(2)}, u32[]{:S(2)}) collective-permute-start(bf16[128,256]{1,0:T(8,128)(2,1)S(1)} %fusion.4), channel_id=1, source_target_pairs={{0,256},{256,0},{1,257},{257,1},{2,258},{258,2},{3,259},{259,3},{4... | collective-permute-start | bytes 196616 | tf_op jit(solution)/shard_map/ppermute | solution.py:243

commit v2 on v1

v2 whole, which is shorter than its diff:
```python
import functools
import math

import jax
import jax.numpy as jnp
from jax import lax
from jax.experimental import pallas as pl
from jax.experimental.pallas import tpu as pltpu
from jax.sharding import Mesh
from jax.sharding import PartitionSpec as P

HD = 128
BLOCK = 64
ROWS = 128
WIDE = 2 * HD
EXTRA = 32
CHUNK = 256
CHUNKS = 8
DOCS = 16
NEGATIVE = -1e30
SCALE = HD ** (-0.5)
SCALE2 = SCALE * math.log2(math.e)
VMEM = 40 * 1024 * 1024

NT = (((1,), (1,)), ((), ()))
NN = (((1,), (0,)), ((), ()))


def mm(a, b, dims):
    return lax.dot_general(a, b, dims, preferred_element_type=jnp.float32)


def heads_down(x):
    return jnp.concatenate([x[:, :HD], x[:, HD:]], axis=0)


def heads_across(x):
    return jnp.concatenate([x[:ROWS], x[ROWS:]], axis=1)


def split3(x):
    hi = x.astype(jnp.bfloat16)
    rest = x - hi.astype(jnp.float32)
    mid = rest.astype(jnp.bfloat16)
    low = (rest - mid.astype(jnp.float32)).astype(jnp.bfloat16)
    return hi, mid, low


def join3(rows, at):
    return rows[at : at + 1] + rows[at + 1 : at + 2] + rows[at + 2 : at + 3]


def query_rows(at_ref, order_ref, lengths_ref, t):
    z_lo, core = at_ref[0], at_ref[2]
    ctx = (z_lo * 4 + t) * 2 + core
    lane = lax.broadcasted_iota(jnp.int32, (1, WIDE), 1)
    row = lax.rem(lane, ROWS)
    first, second = order_ref[2 * ctx] * BLOCK, order_ref[2 * ctx + 1] * BLOCK
    pos = jnp.where(row < BLOCK, first + row, second + row - BLOCK)
    start = jnp.zeros_like(pos)
    end = 0
    for d in range(DOCS):
        end = end + lengths_ref[d]
        start = jnp.where(pos >= end, end, start)
    return pos, start


def key_base(at_ref, order_ref, block):
    z_lo, y, core = at_ref[0], at_ref[1], at_ref[2]
    half, flips = block % 2, (block // 2) % 4 * 2
    flips = (flips & 2) * 2 + (flips & 4) // 2 + (block // 8) % 2
    z_lo = jnp.bitwise_xor(z_lo, flips)
    core = (1 - core) if block // 16 else core
    ctx = (z_lo * 4 + y) * 2 + core
    return order_ref[2 * ctx + half] * BLOCK


def allowed(pos, start, base):
    row = lax.broadcasted_iota(jnp.int32, (BLOCK, WIDE), 0)
    return (row >= start - base) & (row <= pos - base)


def kv_chunk(kv_refs, c, which):
    ref = kv_refs[c // 2]
    first = 2 * (c % 2)
    columns = slice(which * HD, (which + 1) * HD)
    return jnp.concatenate([ref[first, :, columns], ref[first + 1, :, columns]], axis=0)


def forward_kernel(
    at_ref, order_ref, lengths_ref, q_ref, kv0, kv1, kv2, kv3, out_ref, sums_ref, scores, v_t
):
    kv_refs = (kv0, kv1, kv2, kv3)
    for c in range(CHUNKS):
        v_t[:, c * CHUNK : (c + 1) * CHUNK] = kv_chunk(kv_refs, c, 1).T

    def tile(t, carried):
        queries = heads_down(q_ref[t])
        pos, start = query_rows(at_ref, order_ref, lengths_ref, t)
        top = jnp.full((1, WIDE), NEGATIVE, jnp.float32)
        for c in range(CHUNKS):
            s = mm(kv_chunk(kv_refs, c, 0), queries, NT)
            for b in range(CHUNK // BLOCK):
                base = key_base(at_ref, order_ref, c * 4 + b)
                part = jnp.where(
                    allowed(pos, start, base), s[b * BLOCK : (b + 1) * BLOCK], NEGATIVE
                )
                scores[pl.ds(c * CHUNK + b * BLOCK, BLOCK), :] = part
                top = jnp.maximum(top, jnp.max(part, axis=0, keepdims=True))
        top = jnp.maximum(top, 0.1 * NEGATIVE)
        total = jnp.zeros((1, WIDE), jnp.float32)
        acc = jnp.zeros((HD, WIDE), jnp.float32)
        for c in range(CHUNKS):
            e = jnp.exp2((scores[pl.ds(c * CHUNK, CHUNK), :] - top) * SCALE2)
            total = total + jnp.sum(e, axis=0, keepdims=True)
            acc = acc + mm(v_t[:, c * CHUNK : (c + 1) * CHUNK], e.astype(jnp.bfloat16), NN)
        some = total > 0
        safe = jnp.where(some, total, 1.0)
        out_ref[t] = heads_across((acc * (1.0 / safe)).T).astype(jnp.bfloat16)
        sums_ref[t] = jnp.where(some, top * SCALE2 + jnp.log2(safe), NEGATIVE)
        return carried

    lax.fori_loop(0, 4, tile, 0)


def pack_kernel(out_ref, sums_ref, grad_ref, send_ref):
    rows = []
    for t in range(4):
        dots = []
        for h in range(2):
            lanes = slice(h * HD, (h + 1) * HD)
            product = out_ref[t, :, lanes].astype(jnp.float32) * grad_ref[
                t, :, lanes
            ].astype(jnp.float32)
            dot = jnp.sum(product, axis=1, keepdims=True)
            dots.append(jnp.broadcast_to(dot, (ROWS, HD)).T[0:1])
        pieces = split3(sums_ref[t]) + split3(jnp.concatenate(dots, axis=1))
        rows += [v.astype(jnp.float32) for v in pieces]
        rows.append(jnp.zeros((2, WIDE), jnp.float32))
    extra = jnp.concatenate(rows, axis=0).astype(jnp.bfloat16)
    for t in range(4):
        send_ref[t, :ROWS, :] = out_ref[t]
        send_ref[t, ROWS:, :] = extra


def joined(log_sums):
    top = functools.reduce(jnp.maximum, log_sums)
    weights = [jnp.exp2(s - top) for s in log_sums]
    total = functools.reduce(jnp.add, weights)
    inverse = 1.0 / total
    return top + jnp.log2(total), [w * inverse for w in weights]


def combine_kernel(at_ref, parts_ref, weight_ref, terms_ref, sums):
    for j in range(4):
        extra = parts_ref[j, ROWS:, :].astype(jnp.float32)
        for t in range(4):
            sums[t, j : j + 1, :] = join3(extra, 8 * t)
    mine = sums[at_ref[1]]
    log_sum, weights = joined([mine[j : j + 1] for j in range(4)])
    flat = []
    for w in weights:
        flat += [w[:, :HD], w[:, HD:]]
    columns = jnp.concatenate(flat + [jnp.zeros((HD - 8, HD), jnp.float32)], axis=0).T
    halves = []
    for h in range(2):
        lanes = slice(h * HD, (h + 1) * HD)
        acc = jnp.zeros((ROWS, HD), jnp.float32)
        for j in range(4):
            acc = acc + columns[:, 2 * j + h : 2 * j + h + 1] * parts_ref[
                j, :ROWS, lanes
            ].astype(jnp.float32)
        halves.append(acc.astype(jnp.bfloat16))
    attn_out = jnp.concatenate(halves, axis=1)
    for x in range(4):
        for c in range(4):
            part = mm(attn_out, weight_ref[x, pl.ds(c * WIDE, WIDE), :], NT)
            terms_ref[x, :, c * WIDE : (c + 1) * WIDE] = part.astype(jnp.bfloat16)


def backward_kernel(
    at_ref,
    order_ref,
    lengths_ref,
    q_ref,
    grad_ref,
    parts_ref,
    terms_ref,
    kv0,
    kv1,
    kv2,
    kv3,
    dq_ref,
    own_ref,
    far_ref,
    dk_acc,
    dv_acc,
    k_t,
    stats,
):
    kv_refs = (kv0, kv1, kv2, kv3)
    for c in range(CHUNKS):
        k_t[:, c * CHUNK : (c + 1) * CHUNK] = kv_chunk(kv_refs, c, 0).T
    dk_acc[...] = jnp.zeros_like(dk_acc)
    dv_acc[...] = jnp.zeros_like(dv_acc)
    extras = [parts_ref[j, ROWS:, :].astype(jnp.float32) for j in range(4)]
    for t in range(4):
        log_sum, weights = joined([join3(e, 8 * t) for e in extras])
        dots = [w * join3(e, 8 * t + 3) for w, e in zip(weights, extras)]
        stats[t, 0:1, :] = log_sum
        stats[t, 1:2, :] = functools.reduce(jnp.add, dots)

    def tile(t, carried):
        queries = heads_down(q_ref[t])
        grads = heads_down(grad_ref[t])
        log_sum, row_dots = stats[t, 0:1, :], stats[t, 1:2, :]
        pos, start = query_rows(at_ref, order_ref, lengths_ref, t)
        dq = jnp.zeros((HD, WIDE), jnp.float32)
        for c in range(CHUNKS):
            rows = pl.ds(c * CHUNK, CHUNK)
            s = mm(kv_chunk(kv_refs, c, 0), queries, NT)
            dp = mm(kv_chunk(kv_refs, c, 1), grads, NT)
            parts = []
            for b in range(CHUNK // BLOCK):
                base = key_base(at_ref, order_ref, c * 4 + b)
                raised = jnp.exp2(s[b * BLOCK : (b + 1) * BLOCK] * SCALE2 - log_sum)
                parts.append(jnp.where(allowed(pos, start, base), raised, 0.0))
            p = jnp.concatenate(parts, axis=0)
            ds = (p * (dp - row_dots)).astype(jnp.bfloat16)
            dv_acc[rows, :] += mm(p.astype(jnp.bfloat16), grads, NN)
            dk_acc[rows, :] += mm(ds, queries, NN)
            dq = dq + mm(k_t[:, c * CHUNK : (c + 1) * CHUNK], ds, NN)
        dq_ref[t] = heads_across((dq * SCALE).T).astype(jnp.bfloat16)
        return carried

    lax.fori_loop(0, 4, tile, 0)
    for part in range(4):
        ref = far_ref if part // 2 else own_ref
        for k in range(4):
            rows = pl.ds((part * 4 + k) * ROWS, ROWS)
            z10 = jnp.bitwise_xor(at_ref[0] % 4, (k // 2) * 2 + part % 2)
            ref[z10, k % 2, :, :HD] = (dk_acc[rows, :] * SCALE).astype(jnp.bfloat16)
            ref[z10, k % 2, :, HD:] = dv_acc[rows, :].astype(jnp.bfloat16)


def call(kernel, outs, scratch, smem, vmem, flops, unread=0):
    specs = [pl.BlockSpec(memory_space=pltpu.SMEM)] * len(smem)
    specs += [pl.BlockSpec(memory_space=pltpu.VMEM)] * len(vmem)
    if unread:
        specs[unread] = pl.BlockSpec(memory_space=pl.ANY)
    out_specs = [pl.BlockSpec(memory_space=pltpu.VMEM)] * len(outs)
    return pl.pallas_call(
        kernel,
        out_shape=[jax.ShapeDtypeStruct(*o) for o in outs],
        in_specs=specs,
        out_specs=out_specs,
        scratch_shapes=scratch,
        compiler_params=pltpu.CompilerParams(vmem_limit_bytes=VMEM),
        cost_estimate=pl.CostEstimate(flops=flops, bytes_accessed=1 << 21, transcendentals=1 << 21),
    )(*smem, *vmem)


def spread(x, axis, n):
    return lax.all_to_all(jnp.broadcast_to(x, (n,) + x.shape), axis, 0, 0)


def swap(x, axis):
    return lax.ppermute(x, axis, [(0, 1), (1, 0)])


def per_device(
    query_states, key_states, value_states, out_weight, out_grad, doc_lengths, block_order
):
    z_hi = lax.axis_index("z_hi")
    z_lo = lax.axis_index("z2") * 4 + lax.axis_index("z1") * 2 + lax.axis_index("z0")
    at = jnp.stack([z_lo, lax.axis_index("y"), lax.axis_index("core")]).astype(jnp.int32)
    smem = (at, block_order, doc_lengths)

    other_grad = swap(out_grad, "z_hi")
    kv = jnp.concatenate([key_states, value_states], axis=1)
    kv = jnp.stack([kv, swap(kv, "z2")])
    queries = spread(query_states, "y", 4)
    out_grad, other_grad, kv, queries = lax.optimization_barrier(
        (out_grad, other_grad, kv, queries)
    )
    first, second = (
        jnp.where(z_hi == 0, out_grad, other_grad),
        jnp.where(z_hi == 0, other_grad, out_grad),
    )
    all_grad = spread(jnp.concatenate([first, second], axis=1), "x", 4)
    kv_near = jnp.concatenate([kv, swap(kv, "z1")], axis=0)
    kv_far = swap(kv_near, "z0")
    kv_near_core = swap(kv_near, "core")
    kv_far_core = swap(kv_far, "core")
    keys_values = (kv_near, kv_far, kv_near_core, kv_far_core)
    weight = out_weight.reshape(4, 1024, WIDE)
    grad_attn = jnp.einsum(
        "xrd,xdc->rc", all_grad, weight, preferred_element_type=jnp.float32
    ).astype(jnp.bfloat16)
    grads = spread(grad_attn, "y", 4)

    bf16, f32 = jnp.bfloat16, jnp.float32
    partial_out, partial_sums = call(
        forward_kernel,
        [((4, ROWS, WIDE), bf16), ((4, 1, WIDE), f32)],
        [pltpu.VMEM((2048, WIDE), f32), pltpu.VMEM((HD, 2048), bf16)],
        smem,
        (queries,) + keys_values,
        8 * 10**9,
    )
    (send,) = call(
        pack_kernel,
        [((4, ROWS + EXTRA, WIDE), bf16)],
        [],
        (),
        (partial_out, partial_sums, grads),
        10**9,
    )
    parts = lax.all_to_all(send, "y", 0, 0)
    (terms,) = call(
        combine_kernel,
        [((4, ROWS, 1024), bf16)],
        [pltpu.VMEM((4, 8, WIDE), f32)],
        (at,),
        (parts, weight),
        10**9,
    )
    all_terms = lax.all_to_all(terms, "x", 0, 0)
    dq, own, far = call(
        backward_kernel,
        [((4, ROWS, WIDE), bf16), ((4, 2, ROWS, WIDE), bf16), ((4, 2, ROWS, WIDE), bf16)],
        [
            pltpu.VMEM((2048, HD), f32),
            pltpu.VMEM((2048, HD), f32),
            pltpu.VMEM((HD, 2048), bf16),
            pltpu.VMEM((4, 8, WIDE), f32),
        ],
        smem,
        (queries, grads, parts, terms) + keys_values,
        12 * 10**9,
        unread=6,
    )
    dq, own, far, all_terms = lax.optimization_barrier((dq, own, far, all_terms))
    all_terms = jnp.sum(all_terms.astype(f32), axis=0)
    keep = jnp.where(z_hi == 0, all_terms[:, :512], all_terms[:, 512:])
    give = jnp.where(z_hi == 0, all_terms[:, 512:], all_terms[:, :512]).astype(bf16)
    got = swap(give, "z_hi")
    projected = (keep + got.astype(f32)).astype(bf16)
    far = swap(far, "core")
    both = (own.astype(f32) + far.astype(f32)).astype(bf16)
    both = lax.all_to_all(both, ("z1", "z0"), 0, 0)
    both, dq = lax.optimization_barrier((both, dq))
    both = jnp.sum(both.astype(f32), axis=0)
    late = swap(both[1].astype(bf16), "z2")
    grad_kv = (both[0] + late.astype(f32)).astype(bf16)
    dq = jnp.sum(lax.all_to_all(dq, "y", 0, 0).astype(f32), axis=0)
    grad_query = dq.astype(bf16)
    return projected, grad_query, grad_kv[:, :HD], grad_kv[:, HD:]


def solution(mesh):
    fine = Mesh(
        mesh.devices.reshape(2, 2, 2, 4, 2, 4, 2),
        ("z2", "z1", "z0", "y", "core", "x", "z_hi"),
    )
    ctx, head = ("z2", "z1", "z0", "y", "core"), ("x", "z_hi")
    both = P(ctx, head)
    return jax.shard_map(
        per_device,
        mesh=fine,
        in_specs=(both, both, both, P(None, head), both, P(), P()),
        out_specs=(both, both, both, both),
        check_vma=False,
    )
```

time: 188 us -> 169 us (0.90)
  the two profiles are of different devices: /device:TPU:24 before, /device:TPU:64 now
where the time goes in v2:
time: 169 us; the launch traced here: 167 us
  starting transfers between devices  72.3 us (43%)
  waiting for transfers between devices  46.7 us (28%)
  Pallas kernels  21.6 us (13%)
  blocking collectives  12.1 us (7%)
  local copies, waits for them, and re-layouts  7.22 us (4%)
  other arithmetic  4.92 us (3%)
    ppermute x9, starting transfers between devices, swap(): return lax.ppermute(x, axis, [(0, 1), (1, 0)])  45.9 us
    ppermute x9, waiting for transfers between devices, swap(): return lax.ppermute(x, axis, [(0, 1), (1, 0)])  24.2 us
    pallas_call x4, Pallas kernels, call(): pl.pallas_call(kernel, out_shape=[jax.ShapeDtypeStruct(*o) for o in outs]...  21.6 us
    all_to_all x3, starting transfers between devices, spread(): return lax.all_to_all(jnp.broadcast_to(x, (n,) + x.shape), axis, 0, 0)  13.2 us
    all_to_all x1, waiting for transfers between devices, per_device(): both = lax.all_to_all(both, ('z1', 'z0'), 0, 0)  13.2 us
    all_to_all x1, blocking collectives, per_device(): parts = lax.all_to_all(send, 'y', 0, 0)  12.1 us
    all_to_all x1, waiting for transfers between devices, per_device(): dq = jnp.sum(lax.all_to_all(dq, 'y', 0, 0).astype(f32), axis=0)  6.03 us
    all_to_all x1, starting transfers between devices, per_device(): both = lax.all_to_all(both, ('z1', 'z0'), 0, 0)  5.36 us
  transfers between devices with their start and end apart: 15, of which 9 were waited for; matrix products, arithmetic and copies ran while one was open for 4% of the time, Pallas kernels for 11%

profile of v2, /device:TPU:64, one launch (start us, length us, event | category | flops | bytes accessed | tf_op | source)
XLA Modules:
  0.0 167.4 jit_solution(5252548095446544311)
XLA Ops:
  0.6 1.6 broadcast_in_dim.9
  2.2 4.5 %all-to-all-start = ((bf16[4,128,256]{2,1,0:T(8,128)(2,1)}), bf16[4,128,256]{2,1,0:T(8,128)(2,1)S(1)}, u32[]{:S(2)}, u32[]{:S(2)}) async-start(bf16[4,128,256]{2,1,0:T(8,128)(2,1)} %broadcast_in_dim.9), calls=%async_computation | async-start | bytes 524288 | tf_op jit(solution)/shard_map/all_to_all | solution.py:264
  8.2 9.1 %collective-permute-start.1 = (bf16[128,256]{1,0:T(8,128)(2,1)S(1)}, bf16[128,256]{1,0:T(8,128)(2,1)S(1)}, u32[]{:S(2)}, u32[]{:S(2)}) collective-permute-start(bf16[128,256]{1,0:T(8,128)(2,1)S(1)} %constant_dynamic-update-slice_fusion), channel_id=1, source_target_pairs={{0,256},{256,0},{1,257},{257,1},{2,258},{258,2},{3,259},{259,3},{4... | collective-permute-start | bytes 196616 | tf_op jit(solution)/shard_map/ppermute | solution.py:268
  17.3 9.1 %collective-permute-start = (bf16[128,512]{1,0:T(8,128)(2,1)}, bf16[128,512]{1,0:T(8,128)(2,1)S(1)}, u32[]{:S(2)}, u32[]{:S(2)}) collective-permute-start(bf16[128,512]{1,0:T(8,128)(2,1)} %param.11), channel_id=1, source_target_pairs={{0,1},{1,0},{2,3},{3,2},{4,5},{5,4},{6,7},{7,6},{8,9},{9,8},{10,11... | collective-permute-start | bytes 393224 | tf_op jit(solution)/shard_map/ppermute | solution.py:268
  26.4 8.4 %collective-permute-done = bf16[128,512]{1,0:T(8,128)(2,1)S(1)} collective-permute-done((bf16[128,512]{1,0:T(8,128)(2,1)}, bf16[128,512]{1,0:T(8,128)(2,1)S(1)}, u32[]{:S(2)}, u32[]{:S(2)}) %collective-permute-start) | collective-permute-done | bytes 131104 | tf_op jit(solution)/shard_map/ppermute | solution.py:268
  35.9 1.1 broadcast_in_dim.10
  36.9 4.3 %all-to-all-start.1 = ((bf16[4,128,1024]{2,1,0:T(8,128)(2,1)}), bf16[4,128,1024]{2,1,0:T(8,128)(2,1)}, u32[]{:S(2)}, u32[]{:S(2)}) async-start(bf16[4,128,1024]{2,1,0:T(8,128)(2,1)} %broadcast_in_dim.10), calls=%async_computation.1 | async-start | bytes 2097152 | tf_op jit(solution)/shard_map/all_to_all | solution.py:264
  41.2 1.9 %collective-permute-start.2 = (bf16[2,128,256]{2,1,0:T(8,128)(2,1)S(1)}, bf16[2,128,256]{2,1,0:T(8,128)(2,1)S(1)}, u32[]{:S(2)}, u32[]{:S(2)}) collective-permute-start(bf16[2,128,256]{2,1,0:T(8,128)(2,1)S(1)} %pad_maximum_fusion.1), channel_id=1, source_target_pairs={{0,128},{128,0},{1,129},{129,1},{2,130},{130,2},{3,131},{131,3},{4... | collective-permute-start | bytes 393224 | tf_op jit(solution)/shard_map/ppermute | solution.py:268
  43.2 5.8 %collective-permute-done.2 = bf16[2,128,256]{2,1,0:T(8,128)(2,1)S(1)} collective-permute-done((bf16[2,128,256]{2,1,0:T(8,128)(2,1)S(1)}, bf16[2,128,256]{2,1,0:T(8,128)(2,1)S(1)}, u32[]{:S(2)}, u32[]{:S(2)}) %collective-permute-start.2) | collective-permute-done | bytes 131104 | tf_op jit(solution)/shard_map/ppermute | solution.py:268
  49.0 11.5 %collective-permute-start.3 = (bf16[4,128,256]{2,1,0:T(8,128)(2,1)S(1)}, bf16[4,128,256]{2,1,0:T(8,128)(2,1)S(1)}, u32[]{:S(2)}, u32[]{:S(2)}) collective-permute-start(bf16[4,128,256]{2,1,0:T(8,128)(2,1)S(1)} %constant_dynamic-update-slice_fusion.2.kv0), channel_id=1, source_target_pairs={{0,64},{64,0},{1,65},{65,1},{2,66},{66,2},{3,67},{67,3},{4,68},{68... | collective-permute-start | bytes 786440 | tf_op jit(solution)/shard_map/ppermute | solution.py:268
  60.7 1.9 %collective-permute-start.4 = (bf16[4,128,256]{2,1,0:T(8,128)(2,1)S(1)}, bf16[4,128,256]{2,1,0:T(8,128)(2,1)S(1)}, u32[]{:S(2)}, u32[]{:S(2)}) collective-permute-start(bf16[4,128,256]{2,1,0:T(8,128)(2,1)S(1)} %constant_dynamic-update-slice_fusion.2.kv0), channel_id=1, source_target_pairs={{0,8},{8,0},{1,9},{9,1},{2,10},{10,2},{3,11},{11,3},{4,12},{12,4},... | collective-permute-start | bytes 786440 | tf_op jit(solution)/shard_map/ppermute | solution.py:268
  62.6 3.7 %collective-permute-done.3.kv1 = bf16[4,128,256]{2,1,0:T(8,128)(2,1)S(1)} collective-permute-done((bf16[4,128,256]{2,1,0:T(8,128)(2,1)S(1)}, bf16[4,128,256]{2,1,0:T(8,128)(2,1)S(1)}, u32[]{:S(2)}, u32[]{:S(2)}) %collective-permute-start.3) | collective-permute-done | bytes 262176 | tf_op jit(solution)/shard_map/ppermute | solution.py:268
  66.3 1.9 %collective-permute-start.5 = (bf16[4,128,256]{2,1,0:T(8,128)(2,1)S(1)}, bf16[4,128,256]{2,1,0:T(8,128)(2,1)}, u32[]{:S(2)}, u32[]{:S(2)}) collective-permute-start(bf16[4,128,256]{2,1,0:T(8,128)(2,1)S(1)} %collective-permute-done.3.kv1), channel_id=1, source_target_pairs={{0,8},{8,0},{1,9},{9,1},{2,10},{10,2},{3,11},{11,3},{4,12},{12,4},... | collective-permute-start | bytes 786440 | tf_op jit(solution)/shard_map/ppermute | solution.py:268
  68.2 1.7 fusion
  70.6 4.5 %all-to-all-start.2 = ((bf16[4,128,256]{2,1,0:T(8,128)(2,1)}), bf16[4,128,256]{2,1,0:T(8,128)(2,1)S(1)}, u32[]{:S(2)}, u32[]{:S(2)}) async-start(bf16[4,128,256]{2,1,0:T(8,128)(2,1)} %broadcast_in_dim.11), calls=%async_computation.2 | async-start | bytes 524288 | tf_op jit(solution)/shard_map/all_to_all | solution.py:264
  75.1 7.5 %shard_map.102 = (bf16[4,128,256]{2,1,0:T(8,128)(2,1)S(1)}, f32[4,1,256]{2,1,0:T(1,128)S(1)}) custom-call(s32[3]{0:T(128)S(1)} %pad_add_fusion.at_ref, s32[128]{0:T(128)S(1)} %copy-done.3, s32[16]{0:T(128)S(1)} %copy-done.4, bf16[4,128,256]{2,1,0:T(8,128)(2,1)S(1)} %all-to-all-done.q_ref, bf16[4,128,256]{2,1,0:T(8,128)(2,1)S(1)} %constant_dynamic-update-slice_fusion.2.kv0, ...), custom_call_target="tpu_custom_call" | custom-call | flops 8000000000 | bytes 2097152 | tf_op jit(solution)/shard_map/pallas_call | solution.py:252
  83.3 0.9 copy-done.6
  84.6 12.1 %all_to_all.35.parts_ref = bf16[4,160,256]{2,1,0:T(8,128)(2,1)S(1)} all-to-all(bf16[4,160,256]{2,1,0:T(8,128)(2,1)S(1)} %shard_map.103), channel_id=1, replica_groups=mesh['z2'=2,'z1'=2,'z0'=2,'y'=4,'core'=2,'x'=4,'z_hi'=2] {'y'}, dimensions={0} | all-to-all | bytes 655360 | tf_op jit(solution)/shard_map/all_to_all | solution.py:319
  96.7 2.6 %shard_map.104.terms_ref = bf16[4,128,1024]{2,1,0:T(8,128)(2,1)} custom-call(s32[3]{0:T(128)S(1)} %pad_add_fusion.at_ref, bf16[4,160,256]{2,1,0:T(8,128)(2,1)S(1)} %all_to_all.35.parts_ref, bf16[4,1024,256]{2,1,0:T(8,128)(2,1)S(1)} %bitcast.21), custom_call_target="tpu_custom_call" | custom-call | flops 1000000000 | bytes 2097152 | tf_op jit(solution)/shard_map/pallas_call | solution.py:252
  99.3 4.4 %all-to-all-start.4 = ((bf16[4,128,1024]{2,1,0:T(8,128)(2,1)}), bf16[4,128,1024]{2,1,0:T(8,128)(2,1)}, u32[]{:S(2)}, u32[]{:S(2)}) async-start(bf16[4,128,1024]{2,1,0:T(8,128)(2,1)} %shard_map.104.terms_ref), calls=%async_computation.4 | async-start | bytes 2097152 | tf_op jit(solution)/shard_map/all_to_all | solution.py:328
  103.7 11.1 %shard_map.105 = (bf16[4,128,256]{2,1,0:T(8,128)(2,1)}, bf16[4,2,128,256]{3,2,1,0:T(8,128)(2,1)S(1)}, bf16[4,2,128,256]{3,2,1,0:T(8,128)(2,1)S(1)}) custom-call(s32[3]{0:T(128)S(1)} %pad_add_fusion.at_ref, s32[128]{0:T(128)S(1)} %copy-done.3, s32[16]{0:T(128)S(1)} %copy-done.4, bf16[4,128,256]{2,1,0:T(8,128)(2,1)S(1)} %all-to-all-done.q_ref, ...), custom_call_target="tpu_custom_call" | custom-call | flops 12000000000 | bytes 2097152 | tf_op jit(solution)/shard_map/pallas_call | solution.py:252
  114.8 3.3 %all-to-all-done.4 = bf16[4,128,1024]{2,1,0:T(8,128)(2,1)} async-done(((bf16[4,128,1024]{2,1,0:T(8,128)(2,1)}), bf16[4,128,1024]{2,1,0:T(8,128)(2,1)}, u32[]{:S(2)}, u32[]{:S(2)}) %all-to-all-start.4) | async-done | bytes 1048608 | tf_op jit(solution)/shard_map/all_to_all | solution.py:328
  118.1 1.9 %collective-permute-start.7 = (bf16[4,2,128,256]{3,2,1,0:T(8,128)(2,1)S(1)}, bf16[4,2,128,256]{3,2,1,0:T(8,128)(2,1)S(1)}, u32[]{:S(2)}, u32[]{:S(2)}) collective-permute-start(bf16[4,2,128,256]{3,2,1,0:T(8,128)(2,1)S(1)} %get-tuple-element.30), channel_id=1, source_target_pairs={{0,8},{8,0},{1,9},{9,1},{2,10},{10,2},{3,11},{11,3},{4,12},{12,4},... | collective-permute-start | bytes 1572872 | tf_op jit(solution)/shard_map/ppermute | solution.py:268
  120.0 1.9 %collective-permute-done.7 = bf16[4,2,128,256]{3,2,1,0:T(8,128)(2,1)S(1)} collective-permute-done((bf16[4,2,128,256]{3,2,1,0:T(8,128)(2,1)S(1)}, bf16[4,2,128,256]{3,2,1,0:T(8,128)(2,1)S(1)}, u32[]{:S(2)}, u32[]{:S(2)}) %collective-permute-start.7) | collective-permute-done | bytes 524320 | tf_op jit(solution)/shard_map/ppermute | solution.py:268
  122.8 5.4 %all-to-all-start.5 = ((bf16[4,2,128,256]{3,2,1,0:T(8,128)(2,1)}), bf16[4,2,128,256]{3,2,1,0:T(8,128)(2,1)S(1)}, u32[]{:S(2)}, u32[]{:S(2)}) async-start(bf16[4,2,128,256]{3,2,1,0:T(8,128)(2,1)} %add_convert_fusion), calls=%async_computation.5 | async-start | bytes 1048576 | tf_op jit(solution)/shard_map/all_to_all | solution.py:351
  128.2 1.5 convert_reduce_fusion
  129.7 6.7 %collective-permute-start.6 = (bf16[128,512]{1,0:T(8,128)(2,1)S(1)}, bf16[128,512]{1,0:T(8,128)(2,1)S(1)}, u32[]{:S(2)}, u32[]{:S(2)}) collective-permute-start(bf16[128,512]{1,0:T(8,128)(2,1)S(1)} %select_convert_fusion), channel_id=1, source_target_pairs={{0,1},{1,0},{2,3},{3,2},{4,5},{5,4},{6,7},{7,6},{8,9},{9,8},{10,11... | collective-permute-start | bytes 393224 | tf_op jit(solution)/shard_map/ppermute | solution.py:268
  136.3 13.2 %all-to-all-done.5 = bf16[4,2,128,256]{3,2,1,0:T(8,128)(2,1)S(1)} async-done(((bf16[4,2,128,256]{3,2,1,0:T(8,128)(2,1)}), bf16[4,2,128,256]{3,2,1,0:T(8,128)(2,1)S(1)}, u32[]{:S(2)}, u32[]{:S(2)}) %all-to-all-start.5) | async-done | bytes 524320 | tf_op jit(solution)/shard_map/all_to_all | solution.py:351
  149.6 1.9 %collective-permute-start.8 = (bf16[128,256]{1,0:T(8,128)(2,1)S(1)}, bf16[128,256]{1,0:T(8,128)(2,1)S(1)}, u32[]{:S(2)}, u32[]{:S(2)}) collective-permute-start(bf16[128,256]{1,0:T(8,128)(2,1)S(1)} %fusion.3), channel_id=1, source_target_pairs={{0,256},{256,0},{1,257},{257,1},{2,258},{258,2},{3,259},{259,3},{4... | collective-permute-start | bytes 196616 | tf_op jit(solution)/shard_map/ppermute | solution.py:268
  151.5 4.1 %collective-permute-done.6 = bf16[128,512]{1,0:T(8,128)(2,1)S(1)} collective-permute-done((bf16[128,512]{1,0:T(8,128)(2,1)S(1)}, bf16[128,512]{1,0:T(8,128)(2,1)S(1)}, u32[]{:S(2)}, u32[]{:S(2)}) %collective-permute-start.6) | collective-permute-done | bytes 131104 | tf_op jit(solution)/shard_map/ppermute | solution.py:268
  156.4 3.4 %all-to-all-start.6 = ((bf16[4,128,256]{2,1,0:T(8,128)(2,1)}), bf16[4,128,256]{2,1,0:T(8,128)(2,1)S(1)}, u32[]{:S(2)}, u32[]{:S(2)}) async-start(bf16[4,128,256]{2,1,0:T(8,128)(2,1)} %get-tuple-element.32), calls=%async_computation.6 | async-start | bytes 524288 | tf_op jit(solution)/shard_map/all_to_all | solution.py:356
  160.7 6.0 %all-to-all-done.6 = bf16[4,128,256]{2,1,0:T(8,128)(2,1)S(1)} async-done(((bf16[4,128,256]{2,1,0:T(8,128)(2,1)}), bf16[4,128,256]{2,1,0:T(8,128)(2,1)S(1)}, u32[]{:S(2)}, u32[]{:S(2)}) %all-to-all-start.6) | async-done | bytes 262176 | tf_op jit(solution)/shard_map/all_to_all | solution.py:356
  (38 shorter events, 7.8 us)
Async XLA Ops:
  2.2 32.7 %all-to-all-start = ((bf16[4,128,256]{2,1,0:T(8,128)(2,1)}), bf16[4,128,256]{2,1,0:T(8,128)(2,1)S(1)}, u32[]{:S(2)}, u32[]{:S(2)}) async-start(bf16[4,128,256]{2,1,0:T(8,128)(2,1)} %broadcast_in_dim.9), calls=%async_computation | async-start | bytes 524288 | tf_op jit(solution)/shard_map/all_to_all | solution.py:264
  8.2 18.2 %collective-permute-start.1 = (bf16[128,256]{1,0:T(8,128)(2,1)S(1)}, bf16[128,256]{1,0:T(8,128)(2,1)S(1)}, u32[]{:S(2)}, u32[]{:S(2)}) collective-permute-start(bf16[128,256]{1,0:T(8,128)(2,1)S(1)} %constant_dynamic-update-slice_fusion), channel_id=1, source_target_pairs={{0,256},{256,0},{1,257},{257,1},{2,258},{258,2},{3,259},{259,3},{4... | collective-permute-start | bytes 196616 | tf_op jit(solution)/shard_map/ppermute | solution.py:268
  17.3 17.6 %collective-permute-start = (bf16[128,512]{1,0:T(8,128)(2,1)}, bf16[128,512]{1,0:T(8,128)(2,1)S(1)}, u32[]{:S(2)}, u32[]{:S(2)}) collective-permute-start(bf16[128,512]{1,0:T(8,128)(2,1)} %param.11), channel_id=1, source_target_pairs={{0,1},{1,0},{2,3},{3,2},{4,5},{5,4},{6,7},{7,6},{8,9},{9,8},{10,11... | collective-permute-start | bytes 393224 | tf_op jit(solution)/shard_map/ppermute | solution.py:268
  35.8 32.4 %copy-start = (bf16[4096,256]{1,0:T(8,128)(2,1)S(1)}, bf16[4096,256]{1,0:T(8,128)(2,1)}, u32[]{:S(2)}) copy-start(bf16[4096,256]{1,0:T(8,128)(2,1)} %param.10) | copy-start | bytes 6291460
  36.9 31.2 %all-to-all-start.1 = ((bf16[4,128,1024]{2,1,0:T(8,128)(2,1)}), bf16[4,128,1024]{2,1,0:T(8,128)(2,1)}, u32[]{:S(2)}, u32[]{:S(2)}) async-start(bf16[4,128,1024]{2,1,0:T(8,128)(2,1)} %broadcast_in_dim.10), calls=%async_computation.1 | async-start | bytes 2097152 | tf_op jit(solution)/shard_map/all_to_all | solution.py:264
  41.2 7.8 %collective-permute-start.2 = (bf16[2,128,256]{2,1,0:T(8,128)(2,1)S(1)}, bf16[2,128,256]{2,1,0:T(8,128)(2,1)S(1)}, u32[]{:S(2)}, u32[]{:S(2)}) collective-permute-start(bf16[2,128,256]{2,1,0:T(8,128)(2,1)S(1)} %pad_maximum_fusion.1), channel_id=1, source_target_pairs={{0,128},{128,0},{1,129},{129,1},{2,130},{130,2},{3,131},{131,3},{4... | collective-permute-start | bytes 393224 | tf_op jit(solution)/shard_map/ppermute | solution.py:268
  49.0 26.0 %copy-start.3 = (s32[128]{0:T(128)S(1)}, s32[128]{0:T(128)}, u32[]{:S(2)}) copy-start(s32[128]{0:T(128)} %order_ref.3) | copy-start | bytes 1540
  49.0 26.0 %copy-start.4 = (s32[16]{0:T(128)S(1)}, s32[16]{0:T(128)}, u32[]{:S(2)}) copy-start(s32[16]{0:T(128)} %lengths_ref.3) | copy-start | bytes 196
  49.0 17.2 %collective-permute-start.3 = (bf16[4,128,256]{2,1,0:T(8,128)(2,1)S(1)}, bf16[4,128,256]{2,1,0:T(8,128)(2,1)S(1)}, u32[]{:S(2)}, u32[]{:S(2)}) collective-permute-start(bf16[4,128,256]{2,1,0:T(8,128)(2,1)S(1)} %constant_dynamic-update-slice_fusion.2.kv0), channel_id=1, source_target_pairs={{0,64},{64,0},{1,65},{65,1},{2,66},{66,2},{3,67},{67,3},{4,68},{68... | collective-permute-start | bytes 786440 | tf_op jit(solution)/shard_map/ppermute | solution.py:268
  60.7 14.4 %collective-permute-start.4 = (bf16[4,128,256]{2,1,0:T(8,128)(2,1)S(1)}, bf16[4,128,256]{2,1,0:T(8,128)(2,1)S(1)}, u32[]{:S(2)}, u32[]{:S(2)}) collective-permute-start(bf16[4,128,256]{2,1,0:T(8,128)(2,1)S(1)} %constant_dynamic-update-slice_fusion.2.kv0), channel_id=1, source_target_pairs={{0,8},{8,0},{1,9},{9,1},{2,10},{10,2},{3,11},{11,3},{4,12},{12,4},... | collective-permute-start | bytes 786440 | tf_op jit(solution)/shard_map/ppermute | solution.py:268
  66.3 8.8 %collective-permute-start.5 = (bf16[4,128,256]{2,1,0:T(8,128)(2,1)S(1)}, bf16[4,128,256]{2,1,0:T(8,128)(2,1)}, u32[]{:S(2)}, u32[]{:S(2)}) collective-permute-start(bf16[4,128,256]{2,1,0:T(8,128)(2,1)S(1)} %collective-permute-done.3.kv1), channel_id=1, source_target_pairs={{0,8},{8,0},{1,9},{9,1},{2,10},{10,2},{3,11},{11,3},{4,12},{12,4},... | collective-permute-start | bytes 786440 | tf_op jit(solution)/shard_map/ppermute | solution.py:268
  70.6 12.7 %all-to-all-start.2 = ((bf16[4,128,256]{2,1,0:T(8,128)(2,1)}), bf16[4,128,256]{2,1,0:T(8,128)(2,1)S(1)}, u32[]{:S(2)}, u32[]{:S(2)}) async-start(bf16[4,128,256]{2,1,0:T(8,128)(2,1)} %broadcast_in_dim.11), calls=%async_computation.2 | async-start | bytes 524288 | tf_op jit(solution)/shard_map/all_to_all | solution.py:264
  75.1 7.6 %copy-start.1 = (bf16[4,128,256]{2,1,0:T(8,128)(2,1)}, bf16[4,128,256]{2,1,0:T(8,128)(2,1)S(1)}, u32[]{:S(2)}) copy-start(bf16[4,128,256]{2,1,0:T(8,128)(2,1)S(1)} %collective-permute-done.4.kv2) | copy-start | bytes 786436
  82.6 0.7 copy-start.5
  83.3 1.0 copy-start.6
  99.3 4.4 %copy-start.2 = (bf16[4,128,256]{2,1,0:T(8,128)(2,1)S(1)}, bf16[4,128,256]{2,1,0:T(8,128)(2,1)}, u32[]{:S(2)}) copy-start(bf16[4,128,256]{2,1,0:T(8,128)(2,1)} %copy-done.1) | copy-start | bytes 786436
  99.3 18.7 %all-to-all-start.4 = ((bf16[4,128,1024]{2,1,0:T(8,128)(2,1)}), bf16[4,128,1024]{2,1,0:T(8,128)(2,1)}, u32[]{:S(2)}, u32[]{:S(2)}) async-start(bf16[4,128,1024]{2,1,0:T(8,128)(2,1)} %shard_map.104.terms_ref), calls=%async_computation.4 | async-start | bytes 2097152 | tf_op jit(solution)/shard_map/all_to_all | solution.py:328
  118.1 3.8 %collective-permute-start.7 = (bf16[4,2,128,256]{3,2,1,0:T(8,128)(2,1)S(1)}, bf16[4,2,128,256]{3,2,1,0:T(8,128)(2,1)S(1)}, u32[]{:S(2)}, u32[]{:S(2)}) collective-permute-start(bf16[4,2,128,256]{3,2,1,0:T(8,128)(2,1)S(1)} %get-tuple-element.30), channel_id=1, source_target_pairs={{0,8},{8,0},{1,9},{9,1},{2,10},{10,2},{3,11},{11,3},{4,12},{12,4},... | collective-permute-start | bytes 1572872 | tf_op jit(solution)/shard_map/ppermute | solution.py:268
  122.8 26.7 %all-to-all-start.5 = ((bf16[4,2,128,256]{3,2,1,0:T(8,128)(2,1)}), bf16[4,2,128,256]{3,2,1,0:T(8,128)(2,1)S(1)}, u32[]{:S(2)}, u32[]{:S(2)}) async-start(bf16[4,2,128,256]{3,2,1,0:T(8,128)(2,1)} %add_convert_fusion), calls=%async_computation.5 | async-start | bytes 1048576 | tf_op jit(solution)/shard_map/all_to_all | solution.py:351
  129.7 26.0 %collective-permute-start.6 = (bf16[128,512]{1,0:T(8,128)(2,1)S(1)}, bf16[128,512]{1,0:T(8,128)(2,1)S(1)}, u32[]{:S(2)}, u32[]{:S(2)}) collective-permute-start(bf16[128,512]{1,0:T(8,128)(2,1)S(1)} %select_convert_fusion), channel_id=1, source_target_pairs={{0,1},{1,0},{2,3},{3,2},{4,5},{5,4},{6,7},{7,6},{8,9},{9,8},{10,11... | collective-permute-start | bytes 393224 | tf_op jit(solution)/shard_map/ppermute | solution.py:268
  149.6 10.5 %collective-permute-start.8 = (bf16[128,256]{1,0:T(8,128)(2,1)S(1)}, bf16[128,256]{1,0:T(8,128)(2,1)S(1)}, u32[]{:S(2)}, u32[]{:S(2)}) collective-permute-start(bf16[128,256]{1,0:T(8,128)(2,1)S(1)} %fusion.3), channel_id=1, source_target_pairs={{0,256},{256,0},{1,257},{257,1},{2,258},{258,2},{3,259},{259,3},{4... | collective-permute-start | bytes 196616 | tf_op jit(solution)/shard_map/ppermute | solution.py:268
  156.4 10.4 %all-to-all-start.6 = ((bf16[4,128,256]{2,1,0:T(8,128)(2,1)}), bf16[4,128,256]{2,1,0:T(8,128)(2,1)S(1)}, u32[]{:S(2)}, u32[]{:S(2)}) async-start(bf16[4,128,256]{2,1,0:T(8,128)(2,1)} %get-tuple-element.32), calls=%async_computation.6 | async-start | bytes 524288 | tf_op jit(solution)/shard_map/all_to_all | solution.py:356

commit v3 on v2

v3 whole, which is shorter than its diff:
```python
import functools
import math

import jax
import jax.numpy as jnp
from jax import lax
from jax.experimental import pallas as pl
from jax.experimental.pallas import tpu as pltpu
from jax.sharding import Mesh
from jax.sharding import PartitionSpec as P

HD = 128
BLOCK = 64
ROWS = 128
WIDE = 2 * HD
EXTRA = 32
CHUNK = 256
CHUNKS = 8
DOCS = 16
NEGATIVE = -1e30
SCALE = HD ** (-0.5)
SCALE2 = SCALE * math.log2(math.e)
VMEM = 20 * 1024 * 1024

NT = (((1,), (1,)), ((), ()))
NN = (((1,), (0,)), ((), ()))


def mm(a, b, dims):
    return lax.dot_general(a, b, dims, preferred_element_type=jnp.float32)


def heads_down(x):
    return jnp.concatenate([x[:, :HD], x[:, HD:]], axis=0)


def heads_across(x):
    return jnp.concatenate([x[:ROWS], x[ROWS:]], axis=1)


def split3(x):
    hi = x.astype(jnp.bfloat16)
    rest = x - hi.astype(jnp.float32)
    mid = rest.astype(jnp.bfloat16)
    low = (rest - mid.astype(jnp.float32)).astype(jnp.bfloat16)
    return hi, mid, low


def join3(rows, at):
    return rows[at : at + 1] + rows[at + 1 : at + 2] + rows[at + 2 : at + 3]


K_RANK, K_BASE, Q_ORDER, Q_BASE, Q_RANK, Q_LOW, Q_RAW = 0, 32, 64, 72, 80, 88, 96


def key_base(at_ref, order_ref, block):
    half, k = block % 2, (block // 2) % 8
    z_lo = (k % 2) * 4 + (k // 2 % 2) * 2 + k // 4
    core = (1 - at_ref[2]) if block // 16 else at_ref[2]
    ctx = (z_lo * 4 + at_ref[1]) * 2 + core
    return order_ref[2 * ctx + half] * BLOCK


def plan_kernel(at_ref, order_ref, lengths_ref, plan_ref, raw):
    def rank(values, count, at, base_at):
        def one(b, carried):
            mine, place = values[b], 0
            for j in range(count):
                place = place + jnp.where(values[j] < mine, 1, 0)
            plan_ref[at + b] = place
            plan_ref[base_at + place] = mine
            return carried

        lax.fori_loop(0, count, one, 0)

    for b in range(32):
        raw[b] = key_base(at_ref, order_ref, b)
    rank(raw, 32, K_RANK, K_BASE)
    for b in range(8):
        ctx = (at_ref[0] * 4 + b // 2) * 2 + at_ref[2]
        raw[b] = order_ref[2 * ctx + b % 2] * BLOCK
    rank(raw, 8, Q_RANK, Q_BASE)
    for b in range(8):
        plan_ref[Q_ORDER + plan_ref[Q_RANK + b]] = b
    for b in range(8):
        first, low, end = plan_ref[Q_BASE + b], 0, 0
        for d in range(DOCS):
            end = end + lengths_ref[d]
            low = jnp.where(first >= end, end, low)
        plan_ref[Q_LOW + b] = low


def query_rows(plan_ref, lengths_ref, t):
    lane = lax.broadcasted_iota(jnp.int32, (1, WIDE), 1)
    row = lax.rem(lane, ROWS)
    first, second = plan_ref[Q_BASE + 2 * t], plan_ref[Q_BASE + 2 * t + 1]
    pos = jnp.where(row < BLOCK, first + row, second + row - BLOCK)
    start = jnp.zeros_like(pos)
    end = 0
    for d in range(DOCS):
        end = end + lengths_ref[d]
        start = jnp.where(pos >= end, end, start)
    return pos, start


def reached(plan_ref, t, c):
    low, high = plan_ref[K_BASE + 4 * c], plan_ref[K_BASE + 4 * c + 3] + BLOCK - 1
    seen = []
    for i in range(2):
        at = 2 * t + i
        last = plan_ref[Q_BASE + at] + BLOCK - 1
        seen.append((low <= last) & (high >= plan_ref[Q_LOW + at]))
    return seen[0] | seen[1]


def allowed(pos, start, base):
    row = lax.broadcasted_iota(jnp.int32, (BLOCK, WIDE), 0)
    return (row >= start - base) & (row <= pos - base)


def sort_keys(plan_ref, kv_refs, k_s, v_s):
    for b in range(32):
        rows = pl.ds(pl.multiple_of(plan_ref[K_RANK + b] * BLOCK, BLOCK), BLOCK)
        ref = kv_refs[b // 16]
        half = pl.ds((b % 2) * BLOCK, BLOCK)
        k_s[rows, :] = ref[b % 16 // 2, half, :HD]
        v_s[rows, :] = ref[b % 16 // 2, half, HD:]


def two_blocks(ref, plan_ref, t):
    first, second = ref[plan_ref[Q_ORDER + 2 * t]], ref[plan_ref[Q_ORDER + 2 * t + 1]]
    return jnp.concatenate([first[:, :HD], second[:, :HD], first[:, HD:], second[:, HD:]], axis=0)


def forward_kernel(
    plan_ref, lengths_ref, q_ref, kv0, kv1, out_ref, sums_ref, scores, k_s, v_s, v_t, top, total, acc
):
    sort_keys(plan_ref, (kv0, kv1), k_s, v_s)
    for c in range(CHUNKS):
        v_t[:, c * CHUNK : (c + 1) * CHUNK] = v_s[c * CHUNK : (c + 1) * CHUNK, :].T

    def tile(t, carried):
        queries = two_blocks(q_ref, plan_ref, t)
        pos, start = query_rows(plan_ref, lengths_ref, t)
        top[...] = jnp.full((1, WIDE), 0.1 * NEGATIVE, jnp.float32)
        total[...] = jnp.zeros((1, WIDE), jnp.float32)
        acc[...] = jnp.zeros((HD, WIDE), jnp.float32)
        for c in range(CHUNKS):

            @pl.when(reached(plan_ref, t, c))
            def _():
                s = mm(k_s[c * CHUNK : (c + 1) * CHUNK, :], queries, NT)
                most = top[...]
                for b in range(CHUNK // BLOCK):
                    base = plan_ref[K_BASE + c * 4 + b]
                    part = jnp.where(
                        allowed(pos, start, base), s[b * BLOCK : (b + 1) * BLOCK], NEGATIVE
                    )
                    scores[pl.ds(c * CHUNK + b * BLOCK, BLOCK), :] = part
                    most = jnp.maximum(most, jnp.max(part, axis=0, keepdims=True))
                top[...] = most

        for c in range(CHUNKS):

            @pl.when(reached(plan_ref, t, c))
            def _():
                e = jnp.exp2((scores[pl.ds(c * CHUNK, CHUNK), :] - top[...]) * SCALE2)
                total[...] += jnp.sum(e, axis=0, keepdims=True)
                acc[...] += mm(v_t[:, c * CHUNK : (c + 1) * CHUNK], e.astype(jnp.bfloat16), NN)

        some = total[...] > 0
        safe = jnp.where(some, total[...], 1.0)
        out = heads_across((acc[...] * (1.0 / safe)).T).astype(jnp.bfloat16)
        out_ref[plan_ref[Q_ORDER + 2 * t]] = out[:BLOCK]
        out_ref[plan_ref[Q_ORDER + 2 * t + 1]] = out[BLOCK:]
        sums_ref[t] = jnp.where(some, top[...] * SCALE2 + jnp.log2(safe), NEGATIVE)
        return carried

    lax.fori_loop(0, 4, tile, 0)


def both_kernel(at_ref, own_ref, other_ref, send_ref):
    mine = at_ref[3]
    for j in range(4):
        send_ref[j, mine] = own_ref[...]
        send_ref[j, 1 - mine] = other_ref[...]


def grad_kernel(all_ref, weight_ref, send_ref):
    acc = jnp.zeros((ROWS, WIDE), jnp.float32)
    for x in range(4):
        for z in range(2):
            acc = acc + mm(all_ref[x, z], weight_ref[x, z], NN)
    for j in range(4):
        send_ref[j] = acc.astype(jnp.bfloat16)


def pack_kernel(plan_ref, out_ref, sums_ref, grad_ref, send_ref):
    rows = []
    for t in range(4):
        dots = []
        for h in range(2):
            lanes = slice(h * HD, (h + 1) * HD)
            halves = []
            for i in range(2):
                at = plan_ref[Q_ORDER + 2 * t + i]
                product = out_ref[at][:, lanes].astype(jnp.float32) * grad_ref[at][
                    :, lanes
                ].astype(jnp.float32)
                halves.append(jnp.sum(product, axis=1, keepdims=True))
            dot = jnp.concatenate(halves, axis=0)
            dots.append(jnp.broadcast_to(dot, (ROWS, HD)).T[0:1])
        pieces = split3(sums_ref[t]) + split3(jnp.concatenate(dots, axis=1))
        rows += [v.astype(jnp.float32) for v in pieces]
        rows.append(jnp.zeros((2, WIDE), jnp.float32))
    extra = jnp.concatenate(rows, axis=0).astype(jnp.bfloat16)
    for t in range(4):
        send_ref[t, :BLOCK, :] = out_ref[2 * t]
        send_ref[t, BLOCK:ROWS, :] = out_ref[2 * t + 1]
        send_ref[t, ROWS:, :] = extra


def joined(log_sums):
    top = functools.reduce(jnp.maximum, log_sums)
    weights = [jnp.exp2(s - top) for s in log_sums]
    total = functools.reduce(jnp.add, weights)
    inverse = 1.0 / total
    return top + jnp.log2(total), [w * inverse for w in weights]


def combine_kernel(at_ref, plan_ref, parts_ref, weight_ref, terms_ref, sums):
    for j in range(4):
        extra = parts_ref[j, ROWS:, :].astype(jnp.float32)
        for t in range(4):
            sums[t, j : j + 1, :] = join3(extra, 8 * t)
    lane = lax.rem(lax.broadcasted_iota(jnp.int32, (8, WIDE), 1), ROWS)
    first, second = plan_ref[Q_RANK + 2 * at_ref[1]], plan_ref[Q_RANK + 2 * at_ref[1] + 1]
    low, high = sums[first // 2], sums[second // 2]
    low = jnp.where(first % 2 == 1, pltpu.roll(low, WIDE - BLOCK, 1), low)
    high = jnp.where(second % 2 == 0, pltpu.roll(high, BLOCK, 1), high)
    mine = jnp.where(lane < BLOCK, low, high)
    log_sum, weights = joined([mine[j : j + 1] for j in range(4)])
    flat = []
    for w in weights:
        flat += [w[:, :HD], w[:, HD:]]
    columns = jnp.concatenate(flat + [jnp.zeros((HD - 8, HD), jnp.float32)], axis=0).T
    halves = []
    for h in range(2):
        lanes = slice(h * HD, (h + 1) * HD)
        acc = jnp.zeros((ROWS, HD), jnp.float32)
        for j in range(4):
            acc = acc + columns[:, 2 * j + h : 2 * j + h + 1] * parts_ref[
                j, :ROWS, lanes
            ].astype(jnp.float32)
        halves.append(acc.astype(jnp.bfloat16))
    attn_out = jnp.concatenate(halves, axis=1)
    for x in range(4):
        for c in range(4):
            part = mm(attn_out, weight_ref[x, pl.ds(c * WIDE, WIDE), :], NT)
            terms_ref[x, :, c * WIDE : (c + 1) * WIDE] = part.astype(jnp.bfloat16)


def backward_kernel(
    at_ref,
    plan_ref,
    lengths_ref,
    q_ref,
    grad_ref,
    parts_ref,
    terms_ref,
    kv0,
    kv1,
    dq0_ref,
    dq1_ref,
    dq2_ref,
    dq3_ref,
    own_ref,
    far_ref,
    dk_acc,
    dv_acc,
    k_s,
    v_s,
    k_t,
    stats,
    dq_parts,
    dq_acc,
):
    sort_keys(plan_ref, (kv0, kv1), k_s, v_s)
    for c in range(CHUNKS):
        k_t[:, c * CHUNK : (c + 1) * CHUNK] = k_s[c * CHUNK : (c + 1) * CHUNK, :].T
    dk_acc[...] = jnp.zeros_like(dk_acc)
    dv_acc[...] = jnp.zeros_like(dv_acc)
    extras = [parts_ref[j, ROWS:, :].astype(jnp.float32) for j in range(4)]
    for t in range(4):
        log_sum, weights = joined([join3(e, 8 * t) for e in extras])
        dots = [w * join3(e, 8 * t + 3) for w, e in zip(weights, extras)]
        stats[t, 0:1, :] = log_sum
        stats[t, 1:2, :] = functools.reduce(jnp.add, dots)

    def tile(t, carried):
        queries = two_blocks(q_ref, plan_ref, t)
        grads = two_blocks(grad_ref, plan_ref, t)
        log_sum, row_dots = stats[t, 0:1, :], stats[t, 1:2, :]
        pos, start = query_rows(plan_ref, lengths_ref, t)
        dq_acc[...] = jnp.zeros((HD, WIDE), jnp.float32)
        for c in range(CHUNKS):

            @pl.when(reached(plan_ref, t, c))
            def _():
                rows = pl.ds(c * CHUNK, CHUNK)
                s = mm(k_s[rows, :], queries, NT)
                dp = mm(v_s[rows, :], grads, NT)
                parts = []
                for b in range(CHUNK // BLOCK):
                    base = plan_ref[K_BASE + c * 4 + b]
                    raised = jnp.exp2(s[b * BLOCK : (b + 1) * BLOCK] * SCALE2 - log_sum)
                    parts.append(jnp.where(allowed(pos, start, base), raised, 0.0))
                p = jnp.concatenate(parts, axis=0)
                ds = (p * (dp - row_dots)).astype(jnp.bfloat16)
                dv_acc[rows, :] += mm(p.astype(jnp.bfloat16), grads, NN)
                dk_acc[rows, :] += mm(ds, queries, NN)
                dq_acc[...] += mm(k_t[:, c * CHUNK : (c + 1) * CHUNK], ds, NN)

        dq = heads_across((dq_acc[...] * SCALE).T).astype(jnp.bfloat16)
        for i in range(2):
            at = plan_ref[Q_ORDER + 2 * t + i]
            slot = jnp.bitwise_xor(at // 2, at_ref[1]) * 2 + at % 2
            dq_parts[slot] = dq[i * BLOCK : (i + 1) * BLOCK]
        return carried

    lax.fori_loop(0, 4, tile, 0)
    for k, ref in enumerate((dq0_ref, dq1_ref, dq2_ref, dq3_ref)):
        ref[:BLOCK, :] = dq_parts[2 * k]
        ref[BLOCK:, :] = dq_parts[2 * k + 1]
    z2 = at_ref[0] // 4
    for b in range(32):
        ref = far_ref if b // 16 else own_ref
        k = b % 16 // 2
        rows = pl.ds(pl.multiple_of(plan_ref[K_RANK + b] * BLOCK, BLOCK), BLOCK)
        half = pl.ds((b % 2) * BLOCK, BLOCK)
        z10 = (k // 2 % 2) * 2 + k // 4
        z2_flip = jnp.bitwise_xor(z2, k % 2)
        ref[z10, z2_flip, half, :HD] = (dk_acc[rows, :] * SCALE).astype(jnp.bfloat16)
        ref[z10, z2_flip, half, HD:] = dv_acc[rows, :].astype(jnp.bfloat16)


def call(kernel, outs, scratch, smem, vmem, flops, unread=0, space=pltpu.VMEM):
    specs = [pl.BlockSpec(memory_space=pltpu.SMEM)] * len(smem)
    specs += [pl.BlockSpec(memory_space=pltpu.VMEM)] * len(vmem)
    if unread:
        specs[unread] = pl.BlockSpec(memory_space=pl.ANY)
    out_specs = [pl.BlockSpec(memory_space=space)] * len(outs)
    return pl.pallas_call(
        kernel,
        out_shape=[jax.ShapeDtypeStruct(*o) for o in outs],
        in_specs=specs,
        out_specs=out_specs,
        scratch_shapes=scratch,
        compiler_params=pltpu.CompilerParams(vmem_limit_bytes=VMEM),
        cost_estimate=pl.CostEstimate(flops=flops, bytes_accessed=1 << 21, transcendentals=1 << 21),
    )(*smem, *vmem)


def spread(x, axis, n):
    return lax.all_to_all(jnp.broadcast_to(x, (n,) + x.shape), axis, 0, 0)


def gather(x, axis):
    return lax.all_gather(x, axis, axis=0)


def swap(x, axis):
    return lax.ppermute(x, axis, [(0, 1), (1, 0)])


def per_device(
    query_states, key_states, value_states, out_weight, out_grad, doc_lengths, block_order
):
    z_hi = lax.axis_index("z_hi")
    z_lo = lax.axis_index("z2") * 4 + lax.axis_index("z1") * 2 + lax.axis_index("z0")
    at = jnp.stack([z_lo, lax.axis_index("y"), lax.axis_index("core"), z_hi]).astype(jnp.int32)
    smem = (at, block_order, doc_lengths)

    bf16, f32 = jnp.bfloat16, jnp.float32
    other_grad = swap(out_grad, "z_hi")
    queries = spread(query_states, "y", 4)
    kv = jnp.concatenate([key_states, value_states], axis=1)
    (plan,) = call(
        plan_kernel,
        [((ROWS,), jnp.int32)],
        [pltpu.SMEM((32,), jnp.int32)],
        smem,
        (),
        10**8,
        space=pltpu.SMEM,
    )
    out_grad, other_grad, kv, queries, plan = lax.optimization_barrier(
        (out_grad, other_grad, kv, queries, plan)
    )
    queries = queries.reshape(8, BLOCK, WIDE)
    lookup = (plan, doc_lengths)
    (send,) = call(
        both_kernel, [((4, 2, ROWS, 512), bf16)], [], (at,), (out_grad, other_grad), 10**8
    )
    send, kv = lax.optimization_barrier((send, kv))
    all_grad = lax.all_to_all(send, "x", 0, 0)
    kv = gather(gather(kv, "z2"), "z1")
    all_grad, kv = lax.optimization_barrier((all_grad, kv))
    (send,) = call(
        grad_kernel,
        [((4, ROWS, WIDE), bf16)],
        [],
        (),
        (all_grad, out_weight.reshape(4, 2, 512, WIDE)),
        10**9,
    )
    send, kv = lax.optimization_barrier((send, kv))
    grads = lax.all_to_all(send, "y", 0, 0).reshape(8, BLOCK, WIDE)
    kv = gather(kv, "z0").reshape(8, ROWS, WIDE)
    keys_values = (kv, swap(kv, "core"))
    weight = out_weight.reshape(4, 1024, WIDE)

    partial_out, partial_sums = call(
        forward_kernel,
        [((8, BLOCK, WIDE), bf16), ((4, 1, WIDE), f32)],
        [
            pltpu.VMEM((2048, WIDE), f32),
            pltpu.VMEM((2048, HD), bf16),
            pltpu.VMEM((2048, HD), bf16),
            pltpu.VMEM((HD, 2048), bf16),
            pltpu.VMEM((1, WIDE), f32),
            pltpu.VMEM((1, WIDE), f32),
            pltpu.VMEM((HD, WIDE), f32),
        ],
        lookup,
        (queries,) + keys_values,
        8 * 10**9,
    )
    (send,) = call(
        pack_kernel,
        [((4, ROWS + EXTRA, WIDE), bf16)],
        [],
        (plan,),
        (partial_out, partial_sums, grads),
        10**9,
    )
    parts = lax.all_to_all(send, "y", 0, 0)
    (terms,) = call(
        combine_kernel,
        [((4, ROWS, 1024), bf16)],
        [pltpu.VMEM((4, 8, WIDE), f32)],
        (at, plan),
        (parts, weight),
        10**9,
    )
    all_terms = lax.all_to_all(terms, "x", 0, 0)
    dq0, dq1, dq2, dq3, own, far = call(
        backward_kernel,
        [((ROWS, WIDE), bf16)] * 4 + [((4, 2, ROWS, WIDE), bf16)] * 2,
        [
            pltpu.VMEM((2048, HD), f32),
            pltpu.VMEM((2048, HD), f32),
            pltpu.VMEM((2048, HD), bf16),
            pltpu.VMEM((2048, HD), bf16),
            pltpu.VMEM((HD, 2048), bf16),
            pltpu.VMEM((4, 8, WIDE), f32),
            pltpu.VMEM((8, BLOCK, WIDE), bf16),
            pltpu.VMEM((HD, WIDE), f32),
        ],
        (at,) + lookup,
        (queries, grads, parts, terms) + keys_values,
        12 * 10**9,
        unread=6,
    )
    own, far, all_terms = lax.optimization_barrier((own, far, all_terms))
    far = swap(far, "core")
    both = (own.astype(f32) + far.astype(f32)).astype(bf16)
    both, dq1, dq2, dq3, all_terms = lax.optimization_barrier(
        (both, dq1, dq2, dq3, all_terms)
    )
    all_terms = jnp.sum(all_terms.astype(f32), axis=0)
    keep = jnp.where(z_hi == 0, all_terms[:, :512], all_terms[:, 512:])
    give = jnp.where(z_hi == 0, all_terms[:, 512:], all_terms[:, :512]).astype(bf16)
    got = swap(give, "z_hi")
    projected = (keep + got.astype(f32)).astype(bf16)
    both = lax.all_to_all(both, ("z1", "z0"), 0, 0)
    partial = [lax.ppermute(x, "y", [(i, i ^ k) for i in range(4)]) for k, x in ((1, dq1), (2, dq2), (3, dq3))]
    dq = dq0.astype(f32)
    for x in partial:
        dq = dq + x.astype(f32)
    grad_query = dq.astype(bf16)
    both = jnp.sum(both.astype(f32), axis=0)
    late = swap(both[1].astype(bf16), "z2")
    grad_kv = (both[0] + late.astype(f32)).astype(bf16)
    return projected, grad_query, grad_kv[:, :HD], grad_kv[:, HD:]


def solution(mesh):
    fine = Mesh(
        mesh.devices.reshape(2, 2, 2, 4, 2, 4, 2),
        ("z2", "z1", "z0", "y", "core", "x", "z_hi"),
    )
    ctx, head = ("z2", "z1", "z0", "y", "core"), ("x", "z_hi")
    both = P(ctx, head)
    return jax.shard_map(
        per_device,
        mesh=fine,
        in_specs=(both, both, both, P(None, head), both, P(), P()),
        out_specs=(both, both, both, both),
        check_vma=False,
    )
```

time: 169 us -> 161 us (0.953)
  the two profiles are of different devices: /device:TPU:64 before, /device:TPU:32 now
where the time goes in v3:
time: 161 us; the launch traced here: 160 us
  starting transfers between devices  64.5 us (40%)
  blocking collectives  36.6 us (23%)
  Pallas kernels  24.9 us (15%)
  waiting for transfers between devices  24.6 us (15%)
  local copies, waits for them, and re-layouts  5.12 us (3%)
  other arithmetic  3.97 us (2%)
    ppermute x5, starting transfers between devices, swap(): return lax.ppermute(x, axis, [(0, 1), (1, 0)])  30.3 us
    pallas_call x7, Pallas kernels, call(): pl.pallas_call(kernel, out_shape=[jax.ShapeDtypeStruct(*o) for o in outs]...  24.9 us
    all_gather x3, blocking collectives, gather(): return lax.all_gather(x, axis, axis=0)  24.9 us
    ppermute x5, waiting for transfers between devices, swap(): return lax.ppermute(x, axis, [(0, 1), (1, 0)])  17.3 us
    all_to_all x1, blocking collectives, per_device(): parts = lax.all_to_all(send, 'y', 0, 0)  11.7 us
    ppermute x3, starting transfers between devices, per_device(): lax.ppermute(x, 'y', [(i, i ^ k) for i in range(4)])  10.4 us
    all_to_all x1, starting transfers between devices, per_device(): both = lax.all_to_all(both, ('z1', 'z0'), 0, 0)  6.63 us
    all_to_all x1, waiting for transfers between devices, per_device(): all_terms = lax.all_to_all(terms, 'x', 0, 0)  6.44 us
  transfers between devices with their start and end apart: 13, of which 7 were waited for; matrix products, arithmetic and copies ran while one was open for 3% of the time, Pallas kernels for 11%

profile of v3, /device:TPU:32, one launch (start us, length us, event | category | flops | bytes accessed | tf_op | source)
XLA Modules:
  0.0 160.5 jit_solution(15712814417974850505)
XLA Ops:
  0.6 14.8 %collective-permute-start = (bf16[128,512]{1,0:T(8,128)(2,1)}, bf16[128,512]{1,0:T(8,128)(2,1)S(1)}, u32[]{:S(2)}, u32[]{:S(2)}) collective-permute-start(bf16[128,512]{1,0:T(8,128)(2,1)} %own_ref), channel_id=1, source_target_pairs={{0,1},{1,0},{2,3},{3,2},{4,5},{5,4},{6,7},{7,6},{8,9},{9,8},{10,11... | collective-permute-start | bytes 393224 | tf_op jit(solution)/shard_map/ppermute | solution.py:373
  15.5 1.6 broadcast_in_dim.3
  17.0 4.6 %all-to-all-start = ((bf16[4,128,256]{2,1,0:T(8,128)(2,1)}), bf16[4,128,256]{2,1,0:T(8,128)(2,1)S(1)}, u32[]{:S(2)}, u32[]{:S(2)}) async-start(bf16[4,128,256]{2,1,0:T(8,128)(2,1)} %broadcast_in_dim.3), calls=%async_computation | async-start | bytes 524288 | tf_op jit(solution)/shard_map/all_to_all | solution.py:365
  23.0 3.0 %shard_map.102.plan_ref = s32[128]{0:T(128)S(1)} custom-call(s32[4]{0:T(128)S(1)} %pad_add_fusion.at_ref, s32[128]{0:T(128)S(1)} %copy-done.3, s32[16]{0:T(128)S(1)} %copy-done.4), custom_call_target="tpu_custom_call" | custom-call | flops 100000000 | bytes 2097152 | tf_op jit(solution)/shard_map/pallas_call | solution.py:353
  26.1 1.7 %collective-permute-done.other_ref = bf16[128,512]{1,0:T(8,128)(2,1)S(1)} collective-permute-done((bf16[128,512]{1,0:T(8,128)(2,1)}, bf16[128,512]{1,0:T(8,128)(2,1)S(1)}, u32[]{:S(2)}, u32[]{:S(2)}) %collective-permute-start) | collective-permute-done | bytes 131104 | tf_op jit(solution)/shard_map/ppermute | solution.py:373
  28.3 1.6 %shard_map.103 = bf16[4,2,128,512]{3,2,1,0:T(8,128)(2,1)} custom-call(s32[4]{0:T(128)S(1)} %pad_add_fusion.at_ref, bf16[128,512]{1,0:T(8,128)(2,1)S(1)} %copy-done.2, bf16[128,512]{1,0:T(8,128)(2,1)S(1)} %collective-permute-done.other_ref), custom_call_target="tpu_custom_call" | custom-call | flops 100000000 | bytes 2097152 | tf_op jit(solution)/shard_map/pallas_call | solution.py:353
  29.9 4.3 %all-to-all-start.1 = ((bf16[4,2,128,512]{3,2,1,0:T(8,128)(2,1)}), bf16[4,2,128,512]{3,2,1,0:T(8,128)(2,1)S(1)}, u32[]{:S(2)}, u32[]{:S(2)}) async-start(bf16[4,2,128,512]{3,2,1,0:T(8,128)(2,1)} %shard_map.103), calls=%async_computation.1 | async-start | bytes 2097152 | tf_op jit(solution)/shard_map/all_to_all | solution.py:406
  34.2 10.4 %all-gather = bf16[256,256]{1,0:T(8,128)(2,1)S(1)} all-gather(bf16[128,256]{1,0:T(8,128)(2,1)S(1)} %pad_maximum_fusion), channel_id=2, replica_groups=mesh['z2'=2,'z1'=2,'z0'=2,'y'=4,'core'=2,'x'=4,'z_hi'=2] {'z2'}, dimensions={0}, use_global_device_ids=true | all-gather | bytes 196608 | tf_op jit(solution)/shard_map/all_gather | solution.py:369
  44.6 6.6 %all-gather.1 = bf16[4,128,256]{2,1,0:T(8,128)(2,1)S(1)} all-gather(bf16[2,128,256]{2,1,0:T(8,128)(2,1)S(1)} %bitcast.29), channel_id=3, replica_groups=mesh['z2'=2,'z1'=2,'z0'=2,'y'=4,'core'=2,'x'=4,'z_hi'=2] {'z1'}, dimensions={0}, use_global_device_ids=true | all-gather | bytes 393216 | tf_op jit(solution)/shard_map/all_gather | solution.py:369
  51.3 1.6 copy-done
  52.9 1.1 shard_map.104
  54.0 7.8 %all-gather.2 = bf16[4,2,128,256]{3,2,1,0:T(8,128)(2,1)S(1)} all-gather(bf16[2,2,128,256]{3,2,1,0:T(8,128)(2,1)S(1)} %bitcast.28), channel_id=4, replica_groups=mesh['z2'=2,'z1'=2,'z0'=2,'y'=4,'core'=2,'x'=4,'z_hi'=2] {'z0'}, dimensions={0}, use_global_device_ids=true | all-gather | bytes 786432 | tf_op jit(solution)/shard_map/all_gather | solution.py:369
  61.8 1.9 %collective-permute-start.1 = (bf16[8,128,256]{2,1,0:T(8,128)(2,1)S(1)}, bf16[8,128,256]{2,1,0:T(8,128)(2,1)S(1)}, u32[]{:S(2)}, u32[]{:S(2)}) collective-permute-start(bf16[8,128,256]{2,1,0:T(8,128)(2,1)S(1)} %bitcast.19), channel_id=1, source_target_pairs={{0,8},{8,0},{1,9},{9,1},{2,10},{10,2},{3,11},{11,3},{4,12},{12,4},... | collective-permute-start | bytes 1572872 | tf_op jit(solution)/shard_map/ppermute | solution.py:373
  63.8 3.4 %all-to-all-start.2 = ((bf16[4,128,256]{2,1,0:T(8,128)(2,1)}), bf16[4,128,256]{2,1,0:T(8,128)(2,1)S(1)}, u32[]{:S(2)}, u32[]{:S(2)}) async-start(bf16[4,128,256]{2,1,0:T(8,128)(2,1)} %shard_map.104), calls=%async_computation.2 | async-start | bytes 524288 | tf_op jit(solution)/shard_map/all_to_all | solution.py:418
  67.2 7.3 %shard_map.105 = (bf16[8,64,256]{2,1,0:T(8,128)(2,1)S(1)}, f32[4,1,256]{2,1,0:T(1,128)S(1)}) custom-call(s32[128]{0:T(128)S(1)} %shard_map.102.plan_ref, s32[16]{0:T(128)S(1)} %copy-done.5, bf16[8,64,256]{2,1,0:T(8,128)(2,1)S(1)} %bitcast.22, bf16[8,128,256]{2,1,0:T(8,128)(2,1)S(1)} %bitcast.20, bf16[8,128,256]{2,1,0:T(8,128)(2,1)S(1)} %collective-permute-done.1.kv1), custom_call_target="tpu_custom_call" | custom-call | flops 8000000000 | bytes 2097152 | tf_op jit(solution)/shard_map/pallas_call | solution.py:353
  74.8 1.3 shard_map.106
  76.0 11.7 %all_to_all.30.parts_ref = bf16[4,160,256]{2,1,0:T(8,128)(2,1)S(1)} all-to-all(bf16[4,160,256]{2,1,0:T(8,128)(2,1)S(1)} %shard_map.106), channel_id=1, replica_groups=mesh['z2'=2,'z1'=2,'z0'=2,'y'=4,'core'=2,'x'=4,'z_hi'=2] {'y'}, dimensions={0} | all-to-all | bytes 655360 | tf_op jit(solution)/shard_map/all_to_all | solution.py:447
  87.7 2.7 %shard_map.107.terms_ref = bf16[4,128,1024]{2,1,0:T(8,128)(2,1)} custom-call(s32[4]{0:T(128)S(1)} %pad_add_fusion.at_ref, s32[128]{0:T(128)S(1)} %shard_map.102.plan_ref, bf16[4,160,256]{2,1,0:T(8,128)(2,1)S(1)} %all_to_all.30.parts_ref, bf16[4,1024,256]{2,1,0:T(8,128)(2,1)S(1)} %bitcast.27), custom_call_target="tpu_custom_call" | custom-call | flops 1000000000 | bytes 2097152 | tf_op jit(solution)/shard_map/pallas_call | solution.py:353
  90.4 4.8 %all-to-all-start.4 = ((bf16[4,128,1024]{2,1,0:T(8,128)(2,1)}), bf16[4,128,1024]{2,1,0:T(8,128)(2,1)}, u32[]{:S(2)}, u32[]{:S(2)}) async-start(bf16[4,128,1024]{2,1,0:T(8,128)(2,1)} %shard_map.107.terms_ref), calls=%async_computation.4 | async-start | bytes 2097152 | tf_op jit(solution)/shard_map/all_to_all | solution.py:456
  95.2 7.9 %shard_map.108 = (bf16[128,256]{1,0:T(8,128)(2,1)S(1)}, bf16[128,256]{1,0:T(8,128)(2,1)S(1)}, bf16[128,256]{1,0:T(8,128)(2,1)S(1)}, bf16[128,256]{1,0:T(8,128)(2...) custom-call(s32[4]{0:T(128)S(1)} %pad_add_fusion.at_ref, ...), custom_call_target="tpu_custom_call" | custom-call | flops 12000000000 | bytes 2097152 | tf_op jit(solution)/shard_map/pallas_call | solution.py:353
  103.2 6.4 %all-to-all-done.4 = bf16[4,128,1024]{2,1,0:T(8,128)(2,1)} async-done(((bf16[4,128,1024]{2,1,0:T(8,128)(2,1)}), bf16[4,128,1024]{2,1,0:T(8,128)(2,1)}, u32[]{:S(2)}, u32[]{:S(2)}) %all-to-all-start.4) | async-done | bytes 1048608 | tf_op jit(solution)/shard_map/all_to_all | solution.py:456
  109.6 1.9 %collective-permute-start.2 = (bf16[4,2,128,256]{3,2,1,0:T(8,128)(2,1)S(1)}, bf16[4,2,128,256]{3,2,1,0:T(8,128)(2,1)S(1)}, u32[]{:S(2)}, u32[]{:S(2)}) collective-permute-start(bf16[4,2,128,256]{3,2,1,0:T(8,128)(2,1)S(1)} %get-tuple-element.47), channel_id=1, source_target_pairs={{0,8},{8,0},{1,9},{9,1},{2,10},{10,2},{3,11},{11,3},{4,12},{12,4},... | collective-permute-start | bytes 1572872 | tf_op jit(solution)/shard_map/ppermute | solution.py:373
  111.5 1.9 %collective-permute-done.2 = bf16[4,2,128,256]{3,2,1,0:T(8,128)(2,1)S(1)} collective-permute-done((bf16[4,2,128,256]{3,2,1,0:T(8,128)(2,1)S(1)}, bf16[4,2,128,256]{3,2,1,0:T(8,128)(2,1)S(1)}, u32[]{:S(2)}, u32[]{:S(2)}) %collective-permute-start.2) | collective-permute-done | bytes 524320 | tf_op jit(solution)/shard_map/ppermute | solution.py:373
  114.3 6.6 %all-to-all-start.5 = ((bf16[4,2,128,256]{3,2,1,0:T(8,128)(2,1)}), bf16[4,2,128,256]{3,2,1,0:T(8,128)(2,1)S(1)}, u32[]{:S(2)}, u32[]{:S(2)}) async-start(bf16[4,2,128,256]{3,2,1,0:T(8,128)(2,1)} %add_convert_fusion), calls=%async_computation.5 | async-start | bytes 1048576 | tf_op jit(solution)/shard_map/all_to_all | solution.py:486
  120.9 2.5 %collective-permute-start.4 = (bf16[128,256]{1,0:T(8,128)(2,1)S(1)}, bf16[128,256]{1,0:T(8,128)(2,1)S(1)}, u32[]{:S(2)}, u32[]{:S(2)}) collective-permute-start(bf16[128,256]{1,0:T(8,128)(2,1)S(1)} %get-tuple-element.54), channel_id=1, source_target_pairs={{0,16},{16,0},{32,48},{48,32},{1,17},{17,1},{33,49},{49,33},{2,18}... | collective-permute-start | bytes 196616 | tf_op jit(solution)/shard_map/ppermute | solution.py:487
  123.4 4.0 %collective-permute-start.5 = (bf16[128,256]{1,0:T(8,128)(2,1)S(1)}, bf16[128,256]{1,0:T(8,128)(2,1)S(1)}, u32[]{:S(2)}, u32[]{:S(2)}) collective-permute-start(bf16[128,256]{1,0:T(8,128)(2,1)S(1)} %get-tuple-element.55), channel_id=1, source_target_pairs={{0,32},{16,48},{32,0},{48,16},{1,33},{17,49},{33,1},{49,17},{2,34}... | collective-permute-start | bytes 196616 | tf_op jit(solution)/shard_map/ppermute | solution.py:487
  127.4 4.0 %collective-permute-start.6 = (bf16[128,256]{1,0:T(8,128)(2,1)S(1)}, bf16[128,256]{1,0:T(8,128)(2,1)S(1)}, u32[]{:S(2)}, u32[]{:S(2)}) collective-permute-start(bf16[128,256]{1,0:T(8,128)(2,1)S(1)} %get-tuple-element.56), channel_id=1, source_target_pairs={{0,48},{16,32},{32,16},{48,0},{1,49},{17,33},{33,17},{49,1},{2,50}... | collective-permute-start | bytes 196616 | tf_op jit(solution)/shard_map/ppermute | solution.py:487
  131.4 1.5 convert_reduce_fusion
  132.9 9.0 %collective-permute-start.3 = (bf16[128,512]{1,0:T(8,128)(2,1)S(1)}, bf16[128,512]{1,0:T(8,128)(2,1)S(1)}, u32[]{:S(2)}, u32[]{:S(2)}) collective-permute-start(bf16[128,512]{1,0:T(8,128)(2,1)S(1)} %select_convert_fusion), channel_id=1, source_target_pairs={{0,1},{1,0},{2,3},{3,2},{4,5},{5,4},{6,7},{7,6},{8,9},{9,8},{10,11... | collective-permute-start | bytes 393224 | tf_op jit(solution)/shard_map/ppermute | solution.py:373
  142.7 2.6 %collective-permute-start.7 = (bf16[128,256]{1,0:T(8,128)(2,1)S(1)}, bf16[128,256]{1,0:T(8,128)(2,1)S(1)}, u32[]{:S(2)}, u32[]{:S(2)}) collective-permute-start(bf16[128,256]{1,0:T(8,128)(2,1)S(1)} %fusion.2), channel_id=1, source_target_pairs={{0,256},{256,0},{1,257},{257,1},{2,258},{258,2},{3,259},{259,3},{4... | collective-permute-start | bytes 196616 | tf_op jit(solution)/shard_map/ppermute | solution.py:373
  145.3 10.6 %collective-permute-done.3 = bf16[128,512]{1,0:T(8,128)(2,1)S(1)} collective-permute-done((bf16[128,512]{1,0:T(8,128)(2,1)S(1)}, bf16[128,512]{1,0:T(8,128)(2,1)S(1)}, u32[]{:S(2)}, u32[]{:S(2)}) %collective-permute-start.3) | collective-permute-done | bytes 131104 | tf_op jit(solution)/shard_map/ppermute | solution.py:373
  156.6 3.2 %collective-permute-done.7 = bf16[128,256]{1,0:T(8,128)(2,1)S(1)} collective-permute-done((bf16[128,256]{1,0:T(8,128)(2,1)S(1)}, bf16[128,256]{1,0:T(8,128)(2,1)S(1)}, u32[]{:S(2)}, u32[]{:S(2)}) %collective-permute-start.7) | collective-permute-done | bytes 65568 | tf_op jit(solution)/shard_map/ppermute | solution.py:373
  (33 shorter events, 5.3 us)
Async XLA Ops:
  0.6 27.1 %collective-permute-start = (bf16[128,512]{1,0:T(8,128)(2,1)}, bf16[128,512]{1,0:T(8,128)(2,1)S(1)}, u32[]{:S(2)}, u32[]{:S(2)}) collective-permute-start(bf16[128,512]{1,0:T(8,128)(2,1)} %own_ref), channel_id=1, source_target_pairs={{0,1},{1,0},{2,3},{3,2},{4,5},{5,4},{6,7},{7,6},{8,9},{9,8},{10,11... | collective-permute-start | bytes 393224 | tf_op jit(solution)/shard_map/ppermute | solution.py:373
  17.0 9.0 %copy-start.6 = (bf16[128,128]{1,0:T(8,128)(2,1)S(1)}, bf16[128,128]{1,0:T(8,128)(2,1)}, u32[]{:S(2)}) copy-start(bf16[128,128]{1,0:T(8,128)(2,1)} %param.9) | copy-start | bytes 98308
  17.0 9.0 %copy-start.7 = (bf16[128,128]{1,0:T(8,128)(2,1)S(1)}, bf16[128,128]{1,0:T(8,128)(2,1)}, u32[]{:S(2)}) copy-start(bf16[128,128]{1,0:T(8,128)(2,1)} %param.8) | copy-start | bytes 98308
  17.0 11.3 %all-to-all-start = ((bf16[4,128,256]{2,1,0:T(8,128)(2,1)}), bf16[4,128,256]{2,1,0:T(8,128)(2,1)S(1)}, u32[]{:S(2)}, u32[]{:S(2)}) async-start(bf16[4,128,256]{2,1,0:T(8,128)(2,1)} %broadcast_in_dim.3), calls=%async_computation | async-start | bytes 524288 | tf_op jit(solution)/shard_map/all_to_all | solution.py:365
  21.6 6.7 %copy-start.2 = (bf16[128,512]{1,0:T(8,128)(2,1)S(1)}, bf16[128,512]{1,0:T(8,128)(2,1)}, u32[]{:S(2)}) copy-start(bf16[128,512]{1,0:T(8,128)(2,1)} %own_ref) | copy-start | bytes 393220
  21.7 0.7 copy-start.3
  22.4 0.7 copy-start.4
  29.9 21.4 %all-to-all-start.1 = ((bf16[4,2,128,512]{3,2,1,0:T(8,128)(2,1)}), bf16[4,2,128,512]{3,2,1,0:T(8,128)(2,1)S(1)}, u32[]{:S(2)}, u32[]{:S(2)}) async-start(bf16[4,2,128,512]{3,2,1,0:T(8,128)(2,1)} %shard_map.103), calls=%async_computation.1 | async-start | bytes 2097152 | tf_op jit(solution)/shard_map/all_to_all | solution.py:406
  51.3 1.6 copy-start
  52.9 14.3 %copy-start.5 = (s32[16]{0:T(128)S(1)}, s32[16]{0:T(128)}, u32[]{:S(2)}) copy-start(s32[16]{0:T(128)} %lengths_ref.5) | copy-start | bytes 196
  61.8 5.3 %collective-permute-start.1 = (bf16[8,128,256]{2,1,0:T(8,128)(2,1)S(1)}, bf16[8,128,256]{2,1,0:T(8,128)(2,1)S(1)}, u32[]{:S(2)}, u32[]{:S(2)}) collective-permute-start(bf16[8,128,256]{2,1,0:T(8,128)(2,1)S(1)} %bitcast.19), channel_id=1, source_target_pairs={{0,8},{8,0},{1,9},{9,1},{2,10},{10,2},{3,11},{11,3},{4,12},{12,4},... | collective-permute-start | bytes 1572872 | tf_op jit(solution)/shard_map/ppermute | solution.py:373
  63.8 11.0 %all-to-all-start.2 = ((bf16[4,128,256]{2,1,0:T(8,128)(2,1)}), bf16[4,128,256]{2,1,0:T(8,128)(2,1)S(1)}, u32[]{:S(2)}, u32[]{:S(2)}) async-start(bf16[4,128,256]{2,1,0:T(8,128)(2,1)} %shard_map.104), calls=%async_computation.2 | async-start | bytes 524288 | tf_op jit(solution)/shard_map/all_to_all | solution.py:418
  74.8 12.9 %copy-start.1 = (bf16[4096,256]{1,0:T(8,128)(2,1)S(1)}, bf16[4096,256]{1,0:T(8,128)(2,1)}, u32[]{:S(2)}) copy-start(bf16[4096,256]{1,0:T(8,128)(2,1)} %param.10) | copy-start | bytes 6291460
  90.4 19.2 %all-to-all-start.4 = ((bf16[4,128,1024]{2,1,0:T(8,128)(2,1)}), bf16[4,128,1024]{2,1,0:T(8,128)(2,1)}, u32[]{:S(2)}, u32[]{:S(2)}) async-start(bf16[4,128,1024]{2,1,0:T(8,128)(2,1)} %shard_map.107.terms_ref), calls=%async_computation.4 | async-start | bytes 2097152 | tf_op jit(solution)/shard_map/all_to_all | solution.py:456
  109.6 3.8 %collective-permute-start.2 = (bf16[4,2,128,256]{3,2,1,0:T(8,128)(2,1)S(1)}, bf16[4,2,128,256]{3,2,1,0:T(8,128)(2,1)S(1)}, u32[]{:S(2)}, u32[]{:S(2)}) collective-permute-start(bf16[4,2,128,256]{3,2,1,0:T(8,128)(2,1)S(1)} %get-tuple-element.47), channel_id=1, source_target_pairs={{0,8},{8,0},{1,9},{9,1},{2,10},{10,2},{3,11},{11,3},{4,12},{12,4},... | collective-permute-start | bytes 1572872 | tf_op jit(solution)/shard_map/ppermute | solution.py:373
  114.3 28.3 %all-to-all-start.5 = ((bf16[4,2,128,256]{3,2,1,0:T(8,128)(2,1)}), bf16[4,2,128,256]{3,2,1,0:T(8,128)(2,1)S(1)}, u32[]{:S(2)}, u32[]{:S(2)}) async-start(bf16[4,2,128,256]{3,2,1,0:T(8,128)(2,1)} %add_convert_fusion), calls=%async_computation.5 | async-start | bytes 1048576 | tf_op jit(solution)/shard_map/all_to_all | solution.py:486
  120.9 21.0 %collective-permute-start.4 = (bf16[128,256]{1,0:T(8,128)(2,1)S(1)}, bf16[128,256]{1,0:T(8,128)(2,1)S(1)}, u32[]{:S(2)}, u32[]{:S(2)}) collective-permute-start(bf16[128,256]{1,0:T(8,128)(2,1)S(1)} %get-tuple-element.54), channel_id=1, source_target_pairs={{0,16},{16,0},{32,48},{48,32},{1,17},{17,1},{33,49},{49,33},{2,18}... | collective-permute-start | bytes 196616 | tf_op jit(solution)/shard_map/ppermute | solution.py:487
  123.4 18.5 %collective-permute-start.5 = (bf16[128,256]{1,0:T(8,128)(2,1)S(1)}, bf16[128,256]{1,0:T(8,128)(2,1)S(1)}, u32[]{:S(2)}, u32[]{:S(2)}) collective-permute-start(bf16[128,256]{1,0:T(8,128)(2,1)S(1)} %get-tuple-element.55), channel_id=1, source_target_pairs={{0,32},{16,48},{32,0},{48,16},{1,33},{17,49},{33,1},{49,17},{2,34}... | collective-permute-start | bytes 196616 | tf_op jit(solution)/shard_map/ppermute | solution.py:487
  127.4 14.5 %collective-permute-start.6 = (bf16[128,256]{1,0:T(8,128)(2,1)S(1)}, bf16[128,256]{1,0:T(8,128)(2,1)S(1)}, u32[]{:S(2)}, u32[]{:S(2)}) collective-permute-start(bf16[128,256]{1,0:T(8,128)(2,1)S(1)} %get-tuple-element.56), channel_id=1, source_target_pairs={{0,48},{16,32},{32,16},{48,0},{1,49},{17,33},{33,17},{49,1},{2,50}... | collective-permute-start | bytes 196616 | tf_op jit(solution)/shard_map/ppermute | solution.py:487
  132.9 23.0 %collective-permute-start.3 = (bf16[128,512]{1,0:T(8,128)(2,1)S(1)}, bf16[128,512]{1,0:T(8,128)(2,1)S(1)}, u32[]{:S(2)}, u32[]{:S(2)}) collective-permute-start(bf16[128,512]{1,0:T(8,128)(2,1)S(1)} %select_convert_fusion), channel_id=1, source_target_pairs={{0,1},{1,0},{2,3},{3,2},{4,5},{5,4},{6,7},{7,6},{8,9},{9,8},{10,11... | collective-permute-start | bytes 393224 | tf_op jit(solution)/shard_map/ppermute | solution.py:373
  142.7 17.1 %collective-permute-start.7 = (bf16[128,256]{1,0:T(8,128)(2,1)S(1)}, bf16[128,256]{1,0:T(8,128)(2,1)S(1)}, u32[]{:S(2)}, u32[]{:S(2)}) collective-permute-start(bf16[128,256]{1,0:T(8,128)(2,1)S(1)} %fusion.2), channel_id=1, source_target_pairs={{0,256},{256,0},{1,257},{257,1},{2,258},{258,2},{3,259},{259,3},{4... | collective-permute-start | bytes 196616 | tf_op jit(solution)/shard_map/ppermute | solution.py:373

commit v4 on v3

--- a/solution.py
+++ b/solution.py
@@ -478,13 +478,14 @@
     both, dq1, dq2, dq3, all_terms = lax.optimization_barrier(
         (both, dq1, dq2, dq3, all_terms)
     )
+    partial = [lax.ppermute(x, "y", [(i, i ^ k) for i in range(4)]) for k, x in ((1, dq1), (2, dq2), (3, dq3))]
+    both = lax.all_to_all(both, ("z1", "z0"), 0, 0)
     all_terms = jnp.sum(all_terms.astype(f32), axis=0)
     keep = jnp.where(z_hi == 0, all_terms[:, :512], all_terms[:, 512:])
     give = jnp.where(z_hi == 0, all_terms[:, 512:], all_terms[:, :512]).astype(bf16)
     got = swap(give, "z_hi")
     projected = (keep + got.astype(f32)).astype(bf16)
-    both = lax.all_to_all(both, ("z1", "z0"), 0, 0)
-    partial = [lax.ppermute(x, "y", [(i, i ^ k) for i in range(4)]) for k, x in ((1, dq1), (2, dq2), (3, dq3))]
+    both, *partial = lax.optimization_barrier((both, *partial))
     dq = dq0.astype(f32)
     for x in partial:
         dq = dq + x.astype(f32)

time: 161 us -> 159 us (0.988)
  the two profiles are of different devices: /device:TPU:32 before, /device:TPU:96 now
where the time goes in v4:
time: 159 us; the launch traced here: 158 us
  starting transfers between devices  64.5 us (41%)
  blocking collectives  35.5 us (22%)
  Pallas kernels  24.1 us (15%)
  waiting for transfers between devices  24 us (15%)
  local copies, waits for them, and re-layouts  5.12 us (3%)
  other arithmetic  3.97 us (2%)
    ppermute x5, starting transfers between devices, swap(): return lax.ppermute(x, axis, [(0, 1), (1, 0)])  29 us
    all_gather x3, blocking collectives, gather(): return lax.all_gather(x, axis, axis=0)  24.1 us
    pallas_call x7, Pallas kernels, call(): pl.pallas_call(kernel, out_shape=[jax.ShapeDtypeStruct(*o) for o in outs]...  24.1 us
    ppermute x5, waiting for transfers between devices, swap(): return lax.ppermute(x, axis, [(0, 1), (1, 0)])  15.9 us
    all_to_all x1, blocking collectives, per_device(): parts = lax.all_to_all(send, 'y', 0, 0)  11.4 us
    ppermute x3, starting transfers between devices, per_device(): lax.ppermute(x, 'y', [(i, i ^ k) for i in range(4)])  10.4 us
    all_to_all x1, starting transfers between devices, per_device(): both = lax.all_to_all(both, ('z1', 'z0'), 0, 0)  7.96 us
    all_to_all x1, waiting for transfers between devices, per_device(): all_terms = lax.all_to_all(terms, 'x', 0, 0)  5.17 us
  transfers between devices with their start and end apart: 13, of which 6 were waited for; matrix products, arithmetic and copies ran while one was open for 3% of the time, Pallas kernels for 11%

profile of v4, /device:TPU:96, one launch (start us, length us, event | category | flops | bytes accessed | tf_op | source)
XLA Modules:
  0.0 157.9 jit_solution(4434017112216030779)
XLA Ops:
  0.6 13.0 %collective-permute-start = (bf16[128,512]{1,0:T(8,128)(2,1)}, bf16[128,512]{1,0:T(8,128)(2,1)S(1)}, u32[]{:S(2)}, u32[]{:S(2)}) collective-permute-start(bf16[128,512]{1,0:T(8,128)(2,1)} %own_ref), channel_id=1, source_target_pairs={{0,1},{1,0},{2,3},{3,2},{4,5},{5,4},{6,7},{7,6},{8,9},{9,8},{10,11... | collective-permute-start | bytes 393224 | tf_op jit(solution)/shard_map/ppermute | solution.py:373
  13.7 1.6 broadcast_in_dim.3
  15.2 4.6 %all-to-all-start = ((bf16[4,128,256]{2,1,0:T(8,128)(2,1)}), bf16[4,128,256]{2,1,0:T(8,128)(2,1)S(1)}, u32[]{:S(2)}, u32[]{:S(2)}) async-start(bf16[4,128,256]{2,1,0:T(8,128)(2,1)} %broadcast_in_dim.3), calls=%async_computation | async-start | bytes 524288 | tf_op jit(solution)/shard_map/all_to_all | solution.py:365
  21.2 3.0 %shard_map.102.plan_ref = s32[128]{0:T(128)S(1)} custom-call(s32[4]{0:T(128)S(1)} %pad_add_fusion.at_ref, s32[128]{0:T(128)S(1)} %copy-done.3, s32[16]{0:T(128)S(1)} %copy-done.4), custom_call_target="tpu_custom_call" | custom-call | flops 100000000 | bytes 2097152 | tf_op jit(solution)/shard_map/pallas_call | solution.py:353
  24.3 2.2 %all-to-all-done = bf16[4,128,256]{2,1,0:T(8,128)(2,1)S(1)} async-done(((bf16[4,128,256]{2,1,0:T(8,128)(2,1)}), bf16[4,128,256]{2,1,0:T(8,128)(2,1)S(1)}, u32[]{:S(2)}, u32[]{:S(2)}) %all-to-all-start) | async-done | bytes 262176 | tf_op jit(solution)/shard_map/all_to_all | solution.py:365
  26.5 1.6 %shard_map.103 = bf16[4,2,128,512]{3,2,1,0:T(8,128)(2,1)} custom-call(s32[4]{0:T(128)S(1)} %pad_add_fusion.at_ref, bf16[128,512]{1,0:T(8,128)(2,1)S(1)} %copy-done.2, bf16[128,512]{1,0:T(8,128)(2,1)S(1)} %collective-permute-done.other_ref), custom_call_target="tpu_custom_call" | custom-call | flops 100000000 | bytes 2097152 | tf_op jit(solution)/shard_map/pallas_call | solution.py:353
  28.1 4.3 %all-to-all-start.1 = ((bf16[4,2,128,512]{3,2,1,0:T(8,128)(2,1)}), bf16[4,2,128,512]{3,2,1,0:T(8,128)(2,1)S(1)}, u32[]{:S(2)}, u32[]{:S(2)}) async-start(bf16[4,2,128,512]{3,2,1,0:T(8,128)(2,1)} %shard_map.103), calls=%async_computation.1 | async-start | bytes 2097152 | tf_op jit(solution)/shard_map/all_to_all | solution.py:406
  32.4 9.1 %all-gather = bf16[256,256]{1,0:T(8,128)(2,1)S(1)} all-gather(bf16[128,256]{1,0:T(8,128)(2,1)S(1)} %pad_maximum_fusion), channel_id=2, replica_groups=mesh['z2'=2,'z1'=2,'z0'=2,'y'=4,'core'=2,'x'=4,'z_hi'=2] {'z2'}, dimensions={0}, use_global_device_ids=true | all-gather | bytes 196608 | tf_op jit(solution)/shard_map/all_gather | solution.py:369
  41.5 7.9 %all-gather.1 = bf16[4,128,256]{2,1,0:T(8,128)(2,1)S(1)} all-gather(bf16[2,128,256]{2,1,0:T(8,128)(2,1)S(1)} %bitcast.29), channel_id=3, replica_groups=mesh['z2'=2,'z1'=2,'z0'=2,'y'=4,'core'=2,'x'=4,'z_hi'=2] {'z1'}, dimensions={0}, use_global_device_ids=true | all-gather | bytes 393216 | tf_op jit(solution)/shard_map/all_gather | solution.py:369
  49.5 1.6 %copy-done = bf16[4096,256]{1,0:T(8,128)(2,1)S(1)} copy-done((bf16[4096,256]{1,0:T(8,128)(2,1)S(1)}, bf16[4096,256]{1,0:T(8,128)(2,1)}, u32[]{:S(2)}) %copy-start) | copy-done | bytes 2097176
  51.1 1.1 shard_map.104
  52.2 7.0 %all-gather.2 = bf16[4,2,128,256]{3,2,1,0:T(8,128)(2,1)S(1)} all-gather(bf16[2,2,128,256]{3,2,1,0:T(8,128)(2,1)S(1)} %bitcast.28), channel_id=4, replica_groups=mesh['z2'=2,'z1'=2,'z0'=2,'y'=4,'core'=2,'x'=4,'z_hi'=2] {'z0'}, dimensions={0}, use_global_device_ids=true | all-gather | bytes 786432 | tf_op jit(solution)/shard_map/all_gather | solution.py:369
  59.3 1.9 %collective-permute-start.1 = (bf16[8,128,256]{2,1,0:T(8,128)(2,1)S(1)}, bf16[8,128,256]{2,1,0:T(8,128)(2,1)S(1)}, u32[]{:S(2)}, u32[]{:S(2)}) collective-permute-start(bf16[8,128,256]{2,1,0:T(8,128)(2,1)S(1)} %bitcast.19), channel_id=1, source_target_pairs={{0,8},{8,0},{1,9},{9,1},{2,10},{10,2},{3,11},{11,3},{4,12},{12,4},... | collective-permute-start | bytes 1572872 | tf_op jit(solution)/shard_map/ppermute | solution.py:373
  61.2 3.5 %all-to-all-start.2 = ((bf16[4,128,256]{2,1,0:T(8,128)(2,1)}), bf16[4,128,256]{2,1,0:T(8,128)(2,1)S(1)}, u32[]{:S(2)}, u32[]{:S(2)}) async-start(bf16[4,128,256]{2,1,0:T(8,128)(2,1)} %shard_map.104), calls=%async_computation.2 | async-start | bytes 524288 | tf_op jit(solution)/shard_map/all_to_all | solution.py:418
  64.7 6.9 %shard_map.105 = (bf16[8,64,256]{2,1,0:T(8,128)(2,1)S(1)}, f32[4,1,256]{2,1,0:T(1,128)S(1)}) custom-call(s32[128]{0:T(128)S(1)} %shard_map.102.plan_ref, s32[16]{0:T(128)S(1)} %copy-done.5, bf16[8,64,256]{2,1,0:T(8,128)(2,1)S(1)} %bitcast.22, bf16[8,128,256]{2,1,0:T(8,128)(2,1)S(1)} %bitcast.20, bf16[8,128,256]{2,1,0:T(8,128)(2,1)S(1)} %collective-permute-done.1.kv1), custom_call_target="tpu_custom_call" | custom-call | flops 8000000000 | bytes 2097152 | tf_op jit(solution)/shard_map/pallas_call | solution.py:353
  72.2 1.3 shard_map.106
  73.5 11.4 %all_to_all.30.parts_ref = bf16[4,160,256]{2,1,0:T(8,128)(2,1)S(1)} all-to-all(bf16[4,160,256]{2,1,0:T(8,128)(2,1)S(1)} %shard_map.106), channel_id=1, replica_groups=mesh['z2'=2,'z1'=2,'z0'=2,'y'=4,'core'=2,'x'=4,'z_hi'=2] {'y'}, dimensions={0} | all-to-all | bytes 655360 | tf_op jit(solution)/shard_map/all_to_all | solution.py:447
  84.9 2.7 %shard_map.107.terms_ref = bf16[4,128,1024]{2,1,0:T(8,128)(2,1)} custom-call(s32[4]{0:T(128)S(1)} %pad_add_fusion.at_ref, s32[128]{0:T(128)S(1)} %shard_map.102.plan_ref, bf16[4,160,256]{2,1,0:T(8,128)(2,1)S(1)} %all_to_all.30.parts_ref, bf16[4,1024,256]{2,1,0:T(8,128)(2,1)S(1)} %bitcast.27), custom_call_target="tpu_custom_call" | custom-call | flops 1000000000 | bytes 2097152 | tf_op jit(solution)/shard_map/pallas_call | solution.py:353
  87.6 4.7 %all-to-all-start.4 = ((bf16[4,128,1024]{2,1,0:T(8,128)(2,1)}), bf16[4,128,1024]{2,1,0:T(8,128)(2,1)}, u32[]{:S(2)}, u32[]{:S(2)}) async-start(bf16[4,128,1024]{2,1,0:T(8,128)(2,1)} %shard_map.107.terms_ref), calls=%async_computation.4 | async-start | bytes 2097152 | tf_op jit(solution)/shard_map/all_to_all | solution.py:456
  92.3 7.5 %shard_map.108 = (bf16[128,256]{1,0:T(8,128)(2,1)S(1)}, bf16[128,256]{1,0:T(8,128)(2,1)S(1)}, bf16[128,256]{1,0:T(8,128)(2,1)S(1)}, bf16[128,256]{1,0:T(8,128)(2...) custom-call(s32[4]{0:T(128)S(1)} %pad_add_fusion.at_ref, ...), custom_call_target="tpu_custom_call" | custom-call | flops 12000000000 | bytes 2097152 | tf_op jit(solution)/shard_map/pallas_call | solution.py:353
  99.7 5.2 %all-to-all-done.4 = bf16[4,128,1024]{2,1,0:T(8,128)(2,1)} async-done(((bf16[4,128,1024]{2,1,0:T(8,128)(2,1)}), bf16[4,128,1024]{2,1,0:T(8,128)(2,1)}, u32[]{:S(2)}, u32[]{:S(2)}) %all-to-all-start.4) | async-done | bytes 1048608 | tf_op jit(solution)/shard_map/all_to_all | solution.py:456
  104.9 1.9 %collective-permute-start.2 = (bf16[4,2,128,256]{3,2,1,0:T(8,128)(2,1)S(1)}, bf16[4,2,128,256]{3,2,1,0:T(8,128)(2,1)S(1)}, u32[]{:S(2)}, u32[]{:S(2)}) collective-permute-start(bf16[4,2,128,256]{3,2,1,0:T(8,128)(2,1)S(1)} %get-tuple-element.51), channel_id=1, source_target_pairs={{0,8},{8,0},{1,9},{9,1},{2,10},{10,2},{3,11},{11,3},{4,12},{12,4},... | collective-permute-start | bytes 1572872 | tf_op jit(solution)/shard_map/ppermute | solution.py:373
  106.8 1.9 %collective-permute-done.2 = bf16[4,2,128,256]{3,2,1,0:T(8,128)(2,1)S(1)} collective-permute-done((bf16[4,2,128,256]{3,2,1,0:T(8,128)(2,1)S(1)}, bf16[4,2,128,256]{3,2,1,0:T(8,128)(2,1)S(1)}, u32[]{:S(2)}, u32[]{:S(2)}) %collective-permute-start.2) | collective-permute-done | bytes 524320 | tf_op jit(solution)/shard_map/ppermute | solution.py:373
  109.6 8.0 %all-to-all-start.5 = ((bf16[4,2,128,256]{3,2,1,0:T(8,128)(2,1)}), bf16[4,2,128,256]{3,2,1,0:T(8,128)(2,1)S(1)}, u32[]{:S(2)}, u32[]{:S(2)}) async-start(bf16[4,2,128,256]{3,2,1,0:T(8,128)(2,1)} %add_convert_fusion), calls=%async_computation.5 | async-start | bytes 1048576 | tf_op jit(solution)/shard_map/all_to_all | solution.py:482
  117.6 1.5 convert_reduce_fusion
  119.1 10.2 %collective-permute-start.3 = (bf16[128,512]{1,0:T(8,128)(2,1)S(1)}, bf16[128,512]{1,0:T(8,128)(2,1)S(1)}, u32[]{:S(2)}, u32[]{:S(2)}) collective-permute-start(bf16[128,512]{1,0:T(8,128)(2,1)S(1)} %select_convert_fusion), channel_id=1, source_target_pairs={{0,1},{1,0},{2,3},{3,2},{4,5},{5,4},{6,7},{7,6},{8,9},{9,8},{10,11... | collective-permute-start | bytes 393224 | tf_op jit(solution)/shard_map/ppermute | solution.py:373
  129.3 2.5 %collective-permute-start.4 = (bf16[128,256]{1,0:T(8,128)(2,1)S(1)}, bf16[128,256]{1,0:T(8,128)(2,1)S(1)}, u32[]{:S(2)}, u32[]{:S(2)}) collective-permute-start(bf16[128,256]{1,0:T(8,128)(2,1)S(1)} %get-tuple-element.59), channel_id=1, source_target_pairs={{0,16},{16,0},{32,48},{48,32},{1,17},{17,1},{33,49},{49,33},{2,18}... | collective-permute-start | bytes 196616 | tf_op jit(solution)/shard_map/ppermute | solution.py:481
  131.8 4.0 %collective-permute-start.5 = (bf16[128,256]{1,0:T(8,128)(2,1)S(1)}, bf16[128,256]{1,0:T(8,128)(2,1)S(1)}, u32[]{:S(2)}, u32[]{:S(2)}) collective-permute-start(bf16[128,256]{1,0:T(8,128)(2,1)S(1)} %get-tuple-element.60), channel_id=1, source_target_pairs={{0,32},{16,48},{32,0},{48,16},{1,33},{17,49},{33,1},{49,17},{2,34}... | collective-permute-start | bytes 196616 | tf_op jit(solution)/shard_map/ppermute | solution.py:481
  135.8 4.0 %collective-permute-start.6 = (bf16[128,256]{1,0:T(8,128)(2,1)S(1)}, bf16[128,256]{1,0:T(8,128)(2,1)S(1)}, u32[]{:S(2)}, u32[]{:S(2)}) collective-permute-start(bf16[128,256]{1,0:T(8,128)(2,1)S(1)} %get-tuple-element.61), channel_id=1, source_target_pairs={{0,48},{16,32},{32,16},{48,0},{1,49},{17,33},{33,17},{49,1},{2,50}... | collective-permute-start | bytes 196616 | tf_op jit(solution)/shard_map/ppermute | solution.py:481
  139.8 6.6 %collective-permute-done.3 = bf16[128,512]{1,0:T(8,128)(2,1)S(1)} collective-permute-done((bf16[128,512]{1,0:T(8,128)(2,1)S(1)}, bf16[128,512]{1,0:T(8,128)(2,1)S(1)}, u32[]{:S(2)}, u32[]{:S(2)}) %collective-permute-start.3) | collective-permute-done | bytes 131104 | tf_op jit(solution)/shard_map/ppermute | solution.py:373
  147.2 1.9 %collective-permute-start.7 = (bf16[128,256]{1,0:T(8,128)(2,1)S(1)}, bf16[128,256]{1,0:T(8,128)(2,1)S(1)}, u32[]{:S(2)}, u32[]{:S(2)}) collective-permute-start(bf16[128,256]{1,0:T(8,128)(2,1)S(1)} %fusion.2), channel_id=1, source_target_pairs={{0,256},{256,0},{1,257},{257,1},{2,258},{258,2},{3,259},{259,3},{4... | collective-permute-start | bytes 196616 | tf_op jit(solution)/shard_map/ppermute | solution.py:373
  149.8 7.5 %collective-permute-done.7 = bf16[128,256]{1,0:T(8,128)(2,1)S(1)} collective-permute-done((bf16[128,256]{1,0:T(8,128)(2,1)S(1)}, bf16[128,256]{1,0:T(8,128)(2,1)S(1)}, u32[]{:S(2)}, u32[]{:S(2)}) %collective-permute-start.7) | collective-permute-done | bytes 65568 | tf_op jit(solution)/shard_map/ppermute | solution.py:373
  (33 shorter events, 5.1 us)
Async XLA Ops:
  0.6 23.6 %collective-permute-start = (bf16[128,512]{1,0:T(8,128)(2,1)}, bf16[128,512]{1,0:T(8,128)(2,1)S(1)}, u32[]{:S(2)}, u32[]{:S(2)}) collective-permute-start(bf16[128,512]{1,0:T(8,128)(2,1)} %own_ref), channel_id=1, source_target_pairs={{0,1},{1,0},{2,3},{3,2},{4,5},{5,4},{6,7},{7,6},{8,9},{9,8},{10,11... | collective-permute-start | bytes 393224 | tf_op jit(solution)/shard_map/ppermute | solution.py:373
  15.2 9.0 %copy-start.6 = (bf16[128,128]{1,0:T(8,128)(2,1)S(1)}, bf16[128,128]{1,0:T(8,128)(2,1)}, u32[]{:S(2)}) copy-start(bf16[128,128]{1,0:T(8,128)(2,1)} %param.9) | copy-start | bytes 98308
  15.2 9.0 %copy-start.7 = (bf16[128,128]{1,0:T(8,128)(2,1)S(1)}, bf16[128,128]{1,0:T(8,128)(2,1)}, u32[]{:S(2)}) copy-start(bf16[128,128]{1,0:T(8,128)(2,1)} %param.8) | copy-start | bytes 98308
  15.2 11.3 %all-to-all-start = ((bf16[4,128,256]{2,1,0:T(8,128)(2,1)}), bf16[4,128,256]{2,1,0:T(8,128)(2,1)S(1)}, u32[]{:S(2)}, u32[]{:S(2)}) async-start(bf16[4,128,256]{2,1,0:T(8,128)(2,1)} %broadcast_in_dim.3), calls=%async_computation | async-start | bytes 524288 | tf_op jit(solution)/shard_map/all_to_all | solution.py:365
  19.8 6.7 %copy-start.2 = (bf16[128,512]{1,0:T(8,128)(2,1)S(1)}, bf16[128,512]{1,0:T(8,128)(2,1)}, u32[]{:S(2)}) copy-start(bf16[128,512]{1,0:T(8,128)(2,1)} %own_ref) | copy-start | bytes 393220
  19.9 0.7 copy-start.3
  20.6 0.7 copy-start.4
  28.1 21.4 %all-to-all-start.1 = ((bf16[4,2,128,512]{3,2,1,0:T(8,128)(2,1)}), bf16[4,2,128,512]{3,2,1,0:T(8,128)(2,1)S(1)}, u32[]{:S(2)}, u32[]{:S(2)}) async-start(bf16[4,2,128,512]{3,2,1,0:T(8,128)(2,1)} %shard_map.103), calls=%async_computation.1 | async-start | bytes 2097152 | tf_op jit(solution)/shard_map/all_to_all | solution.py:406
  49.5 1.6 %copy-start = (bf16[4096,256]{1,0:T(8,128)(2,1)S(1)}, bf16[4096,256]{1,0:T(8,128)(2,1)}, u32[]{:S(2)}) copy-start(bf16[4096,256]{1,0:T(8,128)(2,1)} %param.10) | copy-start | bytes 6291460
  51.1 13.6 %copy-start.5 = (s32[16]{0:T(128)S(1)}, s32[16]{0:T(128)}, u32[]{:S(2)}) copy-start(s32[16]{0:T(128)} %lengths_ref.5) | copy-start | bytes 196
  59.3 5.4 %collective-permute-start.1 = (bf16[8,128,256]{2,1,0:T(8,128)(2,1)S(1)}, bf16[8,128,256]{2,1,0:T(8,128)(2,1)S(1)}, u32[]{:S(2)}, u32[]{:S(2)}) collective-permute-start(bf16[8,128,256]{2,1,0:T(8,128)(2,1)S(1)} %bitcast.19), channel_id=1, source_target_pairs={{0,8},{8,0},{1,9},{9,1},{2,10},{10,2},{3,11},{11,3},{4,12},{12,4},... | collective-permute-start | bytes 1572872 | tf_op jit(solution)/shard_map/ppermute | solution.py:373
  61.2 11.0 %all-to-all-start.2 = ((bf16[4,128,256]{2,1,0:T(8,128)(2,1)}), bf16[4,128,256]{2,1,0:T(8,128)(2,1)S(1)}, u32[]{:S(2)}, u32[]{:S(2)}) async-start(bf16[4,128,256]{2,1,0:T(8,128)(2,1)} %shard_map.104), calls=%async_computation.2 | async-start | bytes 524288 | tf_op jit(solution)/shard_map/all_to_all | solution.py:418
  72.2 12.7 %copy-start.1 = (bf16[4096,256]{1,0:T(8,128)(2,1)S(1)}, bf16[4096,256]{1,0:T(8,128)(2,1)}, u32[]{:S(2)}) copy-start(bf16[4096,256]{1,0:T(8,128)(2,1)} %param.10) | copy-start | bytes 6291460
  87.6 17.3 %all-to-all-start.4 = ((bf16[4,128,1024]{2,1,0:T(8,128)(2,1)}), bf16[4,128,1024]{2,1,0:T(8,128)(2,1)}, u32[]{:S(2)}, u32[]{:S(2)}) async-start(bf16[4,128,1024]{2,1,0:T(8,128)(2,1)} %shard_map.107.terms_ref), calls=%async_computation.4 | async-start | bytes 2097152 | tf_op jit(solution)/shard_map/all_to_all | solution.py:456
  104.9 3.8 %collective-permute-start.2 = (bf16[4,2,128,256]{3,2,1,0:T(8,128)(2,1)S(1)}, bf16[4,2,128,256]{3,2,1,0:T(8,128)(2,1)S(1)}, u32[]{:S(2)}, u32[]{:S(2)}) collective-permute-start(bf16[4,2,128,256]{3,2,1,0:T(8,128)(2,1)S(1)} %get-tuple-element.51), channel_id=1, source_target_pairs={{0,8},{8,0},{1,9},{9,1},{2,10},{10,2},{3,11},{11,3},{4,12},{12,4},... | collective-permute-start | bytes 1572872 | tf_op jit(solution)/shard_map/ppermute | solution.py:373
  109.6 37.5 %all-to-all-start.5 = ((bf16[4,2,128,256]{3,2,1,0:T(8,128)(2,1)}), bf16[4,2,128,256]{3,2,1,0:T(8,128)(2,1)S(1)}, u32[]{:S(2)}, u32[]{:S(2)}) async-start(bf16[4,2,128,256]{3,2,1,0:T(8,128)(2,1)} %add_convert_fusion), calls=%async_computation.5 | async-start | bytes 1048576 | tf_op jit(solution)/shard_map/all_to_all | solution.py:482
  119.1 27.3 %collective-permute-start.3 = (bf16[128,512]{1,0:T(8,128)(2,1)S(1)}, bf16[128,512]{1,0:T(8,128)(2,1)S(1)}, u32[]{:S(2)}, u32[]{:S(2)}) collective-permute-start(bf16[128,512]{1,0:T(8,128)(2,1)S(1)} %select_convert_fusion), channel_id=1, source_target_pairs={{0,1},{1,0},{2,3},{3,2},{4,5},{5,4},{6,7},{7,6},{8,9},{9,8},{10,11... | collective-permute-start | bytes 393224 | tf_op jit(solution)/shard_map/ppermute | solution.py:373
  129.3 17.7 %collective-permute-start.4 = (bf16[128,256]{1,0:T(8,128)(2,1)S(1)}, bf16[128,256]{1,0:T(8,128)(2,1)S(1)}, u32[]{:S(2)}, u32[]{:S(2)}) collective-permute-start(bf16[128,256]{1,0:T(8,128)(2,1)S(1)} %get-tuple-element.59), channel_id=1, source_target_pairs={{0,16},{16,0},{32,48},{48,32},{1,17},{17,1},{33,49},{49,33},{2,18}... | collective-permute-start | bytes 196616 | tf_op jit(solution)/shard_map/ppermute | solution.py:481
  131.8 15.3 %collective-permute-start.5 = (bf16[128,256]{1,0:T(8,128)(2,1)S(1)}, bf16[128,256]{1,0:T(8,128)(2,1)S(1)}, u32[]{:S(2)}, u32[]{:S(2)}) collective-permute-start(bf16[128,256]{1,0:T(8,128)(2,1)S(1)} %get-tuple-element.60), channel_id=1, source_target_pairs={{0,32},{16,48},{32,0},{48,16},{1,33},{17,49},{33,1},{49,17},{2,34}... | collective-permute-start | bytes 196616 | tf_op jit(solution)/shard_map/ppermute | solution.py:481
  135.8 11.3 %collective-permute-start.6 = (bf16[128,256]{1,0:T(8,128)(2,1)S(1)}, bf16[128,256]{1,0:T(8,128)(2,1)S(1)}, u32[]{:S(2)}, u32[]{:S(2)}) collective-permute-start(bf16[128,256]{1,0:T(8,128)(2,1)S(1)} %get-tuple-element.61), channel_id=1, source_target_pairs={{0,48},{16,32},{32,16},{48,0},{1,49},{17,33},{33,17},{49,1},{2,50}... | collective-permute-start | bytes 196616 | tf_op jit(solution)/shard_map/ppermute | solution.py:481
  147.2 10.1 %collective-permute-start.7 = (bf16[128,256]{1,0:T(8,128)(2,1)S(1)}, bf16[128,256]{1,0:T(8,128)(2,1)S(1)}, u32[]{:S(2)}, u32[]{:S(2)}) collective-permute-start(bf16[128,256]{1,0:T(8,128)(2,1)S(1)} %fusion.2), channel_id=1, source_target_pairs={{0,256},{256,0},{1,257},{257,1},{2,258},{258,2},{3,259},{259,3},{4... | collective-permute-start | bytes 196616 | tf_op jit(solution)/shard_map/ppermute | solution.py:373

commit v5 on v4

--- a/solution.py
+++ b/solution.py
@@ -127,96 +127,96 @@
         v_s[rows, :] = ref[b % 16 // 2, half, HD:]
 
 
-def two_blocks(ref, plan_ref, t):
+def two_blocks(ref, plan_ref, t, at):
     first, second = ref[plan_ref[Q_ORDER + 2 * t]], ref[plan_ref[Q_ORDER + 2 * t + 1]]
-    return jnp.concatenate([first[:, :HD], second[:, :HD], first[:, HD:], second[:, HD:]], axis=0)
+    parts = [x[:, at + h * HD : at + (h + 1) * HD] for h in range(2) for x in (first, second)]
+    return jnp.concatenate(parts, axis=0)
+
+
+def two_lanes(stats, plan_ref, t):
+    lane = lax.rem(lax.broadcasted_iota(jnp.int32, (8, WIDE), 1), ROWS)
+    first, second = plan_ref[Q_ORDER + 2 * t], plan_ref[Q_ORDER + 2 * t + 1]
+    low, high = stats[first // 2], stats[second // 2]
+    low = jnp.where(first % 2 == 1, pltpu.roll(low, WIDE - BLOCK, 1), low)
+    high = jnp.where(second % 2 == 0, pltpu.roll(high, BLOCK, 1), high)
+    return jnp.where(lane < BLOCK, low, high)
+
+
+def loader_rows(at_ref, order_ref, lengths_ref, t):
+    z_lo, core = at_ref[0], at_ref[2]
+    ctx = (z_lo * 4 + t) * 2 + core
+    lane = lax.broadcasted_iota(jnp.int32, (1, WIDE), 1)
+    row = lax.rem(lane, ROWS)
+    first, second = order_ref[2 * ctx] * BLOCK, order_ref[2 * ctx + 1] * BLOCK
+    pos = jnp.where(row < BLOCK, first + row, second + row - BLOCK)
+    start = jnp.zeros_like(pos)
+    end = 0
+    for d in range(DOCS):
+        end = end + lengths_ref[d]
+        start = jnp.where(pos >= end, end, start)
+    return pos, start
+
+
+def kv_chunk(kv_refs, c, which):
+    ref = kv_refs[c // 4]
+    first = 2 * (c % 4)
+    columns = slice(which * HD, (which + 1) * HD)
+    return jnp.concatenate([ref[first, :, columns], ref[first + 1, :, columns]], axis=0)
 
 
 def forward_kernel(
-    plan_ref, lengths_ref, q_ref, kv0, kv1, out_ref, sums_ref, scores, k_s, v_s, v_t, top, total, acc
+    at_ref, order_ref, lengths_ref, q_ref, kv0, kv1, out_ref, sums_ref, scores, v_t
 ):
-    sort_keys(plan_ref, (kv0, kv1), k_s, v_s)
+    kv_refs = (kv0, kv1)
     for c in range(CHUNKS):
-        v_t[:, c * CHUNK : (c + 1) * CHUNK] = v_s[c * CHUNK : (c + 1) * CHUNK, :].T
+        v_t[:, c * CHUNK : (c + 1) * CHUNK] = kv_chunk(kv_refs, c, 1).T
 
     def tile(t, carried):
-        queries = two_blocks(q_ref, plan_ref, t)
-        pos, start = query_rows(plan_ref, lengths_ref, t)
-        top[...] = jnp.full((1, WIDE), 0.1 * NEGATIVE, jnp.float32)
-        total[...] = jnp.zeros((1, WIDE), jnp.float32)
-        acc[...] = jnp.zeros((HD, WIDE), jnp.float32)
+        queries = heads_down(q_ref[t, :, :WIDE])
+        pos, start = loader_rows(at_ref, order_ref, lengths_ref, t)
+        top = jnp.full((1, WIDE), NEGATIVE, jnp.float32)
         for c in range(CHUNKS):
-
-            @pl.when(reached(plan_ref, t, c))
-            def _():
-                s = mm(k_s[c * CHUNK : (c + 1) * CHUNK, :], queries, NT)
-                most = top[...]
-                for b in range(CHUNK // BLOCK):
-                    base = plan_ref[K_BASE + c * 4 + b]
-                    part = jnp.where(
-                        allowed(pos, start, base), s[b * BLOCK : (b + 1) * BLOCK], NEGATIVE
-                    )
-                    scores[pl.ds(c * CHUNK + b * BLOCK, BLOCK), :] = part
-                    most = jnp.maximum(most, jnp.max(part, axis=0, keepdims=True))
-                top[...] = most
-
+            s = mm(kv_chunk(kv_refs, c, 0), queries, NT)
+            for b in range(CHUNK // BLOCK):
+                base = key_base(at_ref, order_ref, c * 4 + b)
+                part = jnp.where(
+                    allowed(pos, start, base), s[b * BLOCK : (b + 1) * BLOCK], NEGATIVE
+                )
+                scores[pl.ds(c * CHUNK + b * BLOCK, BLOCK), :] = part
+                top = jnp.maximum(top, jnp.max(part, axis=0, keepdims=True))
+        top = jnp.maximum(top, 0.1 * NEGATIVE)
+        total = jnp.zeros((1, WIDE), jnp.float32)
+        acc = jnp.zeros((HD, WIDE), jnp.float32)
         for c in range(CHUNKS):
-
-            @pl.when(reached(plan_ref, t, c))
-            def _():
-                e = jnp.exp2((scores[pl.ds(c * CHUNK, CHUNK), :] - top[...]) * SCALE2)
-                total[...] += jnp.sum(e, axis=0, keepdims=True)
-                acc[...] += mm(v_t[:, c * CHUNK : (c + 1) * CHUNK], e.astype(jnp.bfloat16), NN)
-
-        some = total[...] > 0
-        safe = jnp.where(some, total[...], 1.0)
-        out = heads_across((acc[...] * (1.0 / safe)).T).astype(jnp.bfloat16)
-        out_ref[plan_ref[Q_ORDER + 2 * t]] = out[:BLOCK]
-        out_ref[plan_ref[Q_ORDER + 2 * t + 1]] = out[BLOCK:]
-        sums_ref[t] = jnp.where(some, top[...] * SCALE2 + jnp.log2(safe), NEGATIVE)
+            e = jnp.exp2((scores[pl.ds(c * CHUNK, CHUNK), :] - top) * SCALE2)
+            total = total + jnp.sum(e, axis=0, keepdims=True)
+            acc = acc + mm(v_t[:, c * CHUNK : (c + 1) * CHUNK], e.astype(jnp.bfloat16), NN)
+        some = total > 0
+        safe = jnp.where(some, total, 1.0)
+        out_ref[t] = heads_across((acc * (1.0 / safe)).T).astype(jnp.bfloat16)
+        sums_ref[t] = jnp.where(some, top * SCALE2 + jnp.log2(safe), NEGATIVE)
         return carried
 
     lax.fori_loop(0, 4, tile, 0)
 
 
-def both_kernel(at_ref, own_ref, other_ref, send_ref):
-    mine = at_ref[3]
-    for j in range(4):
-        send_ref[j, mine] = own_ref[...]
-        send_ref[j, 1 - mine] = other_ref[...]
-
-
-def grad_kernel(all_ref, weight_ref, send_ref):
-    acc = jnp.zeros((ROWS, WIDE), jnp.float32)
-    for x in range(4):
-        for z in range(2):
-            acc = acc + mm(all_ref[x, z], weight_ref[x, z], NN)
-    for j in range(4):
-        send_ref[j] = acc.astype(jnp.bfloat16)
-
-
-def pack_kernel(plan_ref, out_ref, sums_ref, grad_ref, send_ref):
+def pack_kernel(out_ref, sums_ref, grad_ref, send_ref):
     rows = []
     for t in range(4):
         dots = []
         for h in range(2):
             lanes = slice(h * HD, (h + 1) * HD)
-            halves = []
-            for i in range(2):
-                at = plan_ref[Q_ORDER + 2 * t + i]
-                product = out_ref[at][:, lanes].astype(jnp.float32) * grad_ref[at][
-                    :, lanes
-                ].astype(jnp.float32)
-                halves.append(jnp.sum(product, axis=1, keepdims=True))
-            dot = jnp.concatenate(halves, axis=0)
+            product = out_ref[t, :, lanes].astype(jnp.float32) * grad_ref[
+                t, :, slice(WIDE + h * HD, WIDE + (h + 1) * HD)
+            ].astype(jnp.float32)
+            dot = jnp.sum(product, axis=1, keepdims=True)
             dots.append(jnp.broadcast_to(dot, (ROWS, HD)).T[0:1])
         pieces = split3(sums_ref[t]) + split3(jnp.concatenate(dots, axis=1))
         rows += [v.astype(jnp.float32) for v in pieces]
         rows.append(jnp.zeros((2, WIDE), jnp.float32))
     extra = jnp.concatenate(rows, axis=0).astype(jnp.bfloat16)
     for t in range(4):
-        send_ref[t, :BLOCK, :] = out_ref[2 * t]
-        send_ref[t, BLOCK:ROWS, :] = out_ref[2 * t + 1]
+        send_ref[t, :ROWS, :] = out_ref[t]
         send_ref[t, ROWS:, :] = extra
 
 
@@ -228,17 +228,12 @@
     return top + jnp.log2(total), [w * inverse for w in weights]
 
 
-def combine_kernel(at_ref, plan_ref, parts_ref, weight_ref, terms_ref, sums):
+def combine_kernel(at_ref, parts_ref, weight_ref, terms_ref, sums):
     for j in range(4):
         extra = parts_ref[j, ROWS:, :].astype(jnp.float32)
         for t in range(4):
             sums[t, j : j + 1, :] = join3(extra, 8 * t)
-    lane = lax.rem(lax.broadcasted_iota(jnp.int32, (8, WIDE), 1), ROWS)
-    first, second = plan_ref[Q_RANK + 2 * at_ref[1]], plan_ref[Q_RANK + 2 * at_ref[1] + 1]
-    low, high = sums[first // 2], sums[second // 2]
-    low = jnp.where(first % 2 == 1, pltpu.roll(low, WIDE - BLOCK, 1), low)
-    high = jnp.where(second % 2 == 0, pltpu.roll(high, BLOCK, 1), high)
-    mine = jnp.where(lane < BLOCK, low, high)
+    mine = sums[at_ref[1]]
     log_sum, weights = joined([mine[j : j + 1] for j in range(4)])
     flat = []
     for w in weights:
@@ -264,8 +259,7 @@
     at_ref,
     plan_ref,
     lengths_ref,
-    q_ref,
-    grad_ref,
+    both_ref,
     parts_ref,
     terms_ref,
     kv0,
@@ -298,9 +292,10 @@
         stats[t, 1:2, :] = functools.reduce(jnp.add, dots)
 
     def tile(t, carried):
-        queries = two_blocks(q_ref, plan_ref, t)
-        grads = two_blocks(grad_ref, plan_ref, t)
-        log_sum, row_dots = stats[t, 0:1, :], stats[t, 1:2, :]
+        queries = two_blocks(both_ref, plan_ref, t, 0)
+        grads = two_blocks(both_ref, plan_ref, t, WIDE)
+        mine = two_lanes(stats, plan_ref, t)
+        log_sum, row_dots = mine[0:1, :], mine[1:2, :]
         pos, start = query_rows(plan_ref, lengths_ref, t)
         dq_acc[...] = jnp.zeros((HD, WIDE), jnp.float32)
         for c in range(CHUNKS):
@@ -382,74 +377,55 @@
     smem = (at, block_order, doc_lengths)
 
     bf16, f32 = jnp.bfloat16, jnp.float32
-    other_grad = swap(out_grad, "z_hi")
-    queries = spread(query_states, "y", 4)
+    weight = out_weight.reshape(4, 2, 512, WIDE)
+    send = gather(out_grad, "z_hi")
     kv = jnp.concatenate([key_states, value_states], axis=1)
+    send, kv = lax.optimization_barrier((send, kv))
+    all_grad = spread(send, "x", 4)
+    kv = gather(gather(kv, "z2"), "z1")
+    all_grad, kv = lax.optimization_barrier((all_grad, kv))
+    grad_attn = jnp.einsum("xzrd,xzdc->rc", all_grad, weight, preferred_element_type=f32)
+    send = jnp.concatenate([query_states, grad_attn.astype(bf16)], axis=1)
+    send, kv = lax.optimization_barrier((send, kv))
+    queries_grads = spread(send, "y", 4)
+    kv = gather(kv, "z0").reshape(8, ROWS, WIDE)
+    kv, queries_grads = lax.optimization_barrier((kv, queries_grads))
+    keys_values = (kv, swap(kv, "core"))
+    weight = out_weight.reshape(4, 1024, WIDE)
+
+    partial_out, partial_sums = call(
+        forward_kernel,
+        [((4, ROWS, WIDE), bf16), ((4, 1, WIDE), f32)],
+        [pltpu.VMEM((2048, WIDE), f32), pltpu.VMEM((HD, 2048), bf16)],
+        smem,
+        (queries_grads,) + keys_values,
+        8 * 10**9,
+    )
+    (send,) = call(
+        pack_kernel,
+        [((4, ROWS + EXTRA, WIDE), bf16)],
+        [],
+        (),
+        (partial_out, partial_sums, queries_grads),
+        10**9,
+    )
+    order, send = lax.optimization_barrier((block_order, send))
     (plan,) = call(
         plan_kernel,
         [((ROWS,), jnp.int32)],
         [pltpu.SMEM((32,), jnp.int32)],
-        smem,
+        (at, order, doc_lengths),
         (),
-        10**8,
+        3 * 10**9,
         space=pltpu.SMEM,
     )
-    out_grad, other_grad, kv, queries, plan = lax.optimization_barrier(
-        (out_grad, other_grad, kv, queries, plan)
-    )
-    queries = queries.reshape(8, BLOCK, WIDE)
-    lookup = (plan, doc_lengths)
-    (send,) = call(
-        both_kernel, [((4, 2, ROWS, 512), bf16)], [], (at,), (out_grad, other_grad), 10**8
-    )
-    send, kv = lax.optimization_barrier((send, kv))
-    all_grad = lax.all_to_all(send, "x", 0, 0)
-    kv = gather(gather(kv, "z2"), "z1")
-    all_grad, kv = lax.optimization_barrier((all_grad, kv))
-    (send,) = call(
-        grad_kernel,
-        [((4, ROWS, WIDE), bf16)],
-        [],
-        (),
-        (all_grad, out_weight.reshape(4, 2, 512, WIDE)),
-        10**9,
-    )
-    send, kv = lax.optimization_barrier((send, kv))
-    grads = lax.all_to_all(send, "y", 0, 0).reshape(8, BLOCK, WIDE)
-    kv = gather(kv, "z0").reshape(8, ROWS, WIDE)
-    keys_values = (kv, swap(kv, "core"))
-    weight = out_weight.reshape(4, 1024, WIDE)
-
-    partial_out, partial_sums = call(
-        forward_kernel,
-        [((8, BLOCK, WIDE), bf16), ((4, 1, WIDE), f32)],
-        [
-            pltpu.VMEM((2048, WIDE), f32),
-            pltpu.VMEM((2048, HD), bf16),
-            pltpu.VMEM((2048, HD), bf16),
-            pltpu.VMEM((HD, 2048), bf16),
-            pltpu.VMEM((1, WIDE), f32),
-            pltpu.VMEM((1, WIDE), f32),
-            pltpu.VMEM((HD, WIDE), f32),
-        ],
-        lookup,
-        (queries,) + keys_values,
-        8 * 10**9,
-    )
-    (send,) = call(
-        pack_kernel,
-        [((4, ROWS + EXTRA, WIDE), bf16)],
-        [],
-        (plan,),
-        (partial_out, partial_sums, grads),
-        10**9,
-    )
     parts = lax.all_to_all(send, "y", 0, 0)
+    parts, plan = lax.optimization_barrier((parts, plan))
     (terms,) = call(
         combine_kernel,
         [((4, ROWS, 1024), bf16)],
         [pltpu.VMEM((4, 8, WIDE), f32)],
-        (at, plan),
+        (at,),
         (parts, weight),
         10**9,
     )
@@ -467,10 +443,10 @@
             pltpu.VMEM((8, BLOCK, WIDE), bf16),
             pltpu.VMEM((HD, WIDE), f32),
         ],
-        (at,) + lookup,
-        (queries, grads, parts, terms) + keys_values,
+        (at, plan, doc_lengths),
+        (queries_grads.reshape(8, BLOCK, 2 * WIDE), parts, terms) + keys_values,
         12 * 10**9,
-        unread=6,
+        unread=5,
     )
     own, far, all_terms = lax.optimization_barrier((own, far, all_terms))
     far = swap(far, "core")

time: 159 us -> 160 us (level)
  the two profiles are of different devices: /device:TPU:96 before, /device:TPU:24 now
where the time goes in v5:
time: 160 us; the launch traced here: 159 us
  starting transfers between devices  50.3 us (31%)
  blocking collectives  49.1 us (31%)
  waiting for transfers between devices  27.1 us (17%)
  Pallas kernels  19.9 us (12%)
  local copies, waits for them, and re-layouts  6.04 us (4%)
  other arithmetic  4.92 us (3%)
    all_gather x4, blocking collectives, gather(): return lax.all_gather(x, axis, axis=0)  49.1 us
    pallas_call x5, Pallas kernels, call(): pl.pallas_call(kernel, out_shape=[jax.ShapeDtypeStruct(*o) for o in outs]...  19.9 us
    ppermute x4, waiting for transfers between devices, swap(): return lax.ppermute(x, axis, [(0, 1), (1, 0)])  19.3 us
    ppermute x4, starting transfers between devices, swap(): return lax.ppermute(x, axis, [(0, 1), (1, 0)])  15.3 us
    ppermute x3, starting transfers between devices, per_device(): lax.ppermute(x, 'y', [(i, i ^ k) for i in range(4)])  10.4 us
    all_to_all x2, starting transfers between devices, spread(): return lax.all_to_all(jnp.broadcast_to(x, (n,) + x.shape), axis, 0, 0)  8.98 us
    all_to_all x1, starting transfers between devices, per_device(): both = lax.all_to_all(both, ('z1', 'z0'), 0, 0)  6.61 us
    all_to_all x1, waiting for transfers between devices, per_device(): all_terms = lax.all_to_all(terms, 'x', 0, 0)  5.23 us
  transfers between devices with their start and end apart: 12, of which 6 were waited for; matrix products, arithmetic and copies ran while one was open for 2% of the time, Pallas kernels for 6%

profile of v5, /device:TPU:24, one launch (start us, length us, event | category | flops | bytes accessed | tf_op | source)
XLA Modules:
  0.0 158.6 jit_solution(832105718225922134)
XLA Ops:
  0.6 18.5 %all-gather = bf16[256,512]{1,0:T(8,128)(2,1)S(1)} all-gather(bf16[128,512]{1,0:T(8,128)(2,1)} %param.11), channel_id=2, replica_groups=mesh['z2'=2,'z1'=2,'z0'=2,'y'=4,'core'=2,'x'=4,'z_hi'=2] {'z_hi'}, dimensions={0}, use_global_device_ids=true | all-gather | bytes 393216 | tf_op jit(solution)/shard_map/all_gather | solution.py:364
  19.2 0.9 pad_maximum_fusion.1
  20.1 1.1 broadcast_in_dim.6
  21.2 4.3 %all-to-all-start = ((bf16[4,2,128,512]{3,2,1,0:T(8,128)(2,1)}), bf16[4,2,128,512]{3,2,1,0:T(8,128)(2,1)S(1)}, u32[]{:S(2)}, u32[]{:S(2)}) async-start(bf16[4,2,128,512]{3,2,1,0:T(8,128)(2,1)} %broadcast_in_dim.6), calls=%async_computation | async-start | bytes 2097152 | tf_op jit(solution)/shard_map/all_to_all | solution.py:360
  25.5 13.4 %all-gather.1 = bf16[256,256]{1,0:T(8,128)(2,1)S(1)} all-gather(bf16[128,256]{1,0:T(8,128)(2,1)S(1)} %pad_maximum_fusion.1), channel_id=3, replica_groups=mesh['z2'=2,'z1'=2,'z0'=2,'y'=4,'core'=2,'x'=4,'z_hi'=2] {'z2'}, dimensions={0}, use_global_device_ids=true | all-gather | bytes 196608 | tf_op jit(solution)/shard_map/all_gather | solution.py:364
  38.9 7.6 %all-gather.2 = bf16[4,128,256]{2,1,0:T(8,128)(2,1)S(1)} all-gather(bf16[2,128,256]{2,1,0:T(8,128)(2,1)S(1)} %bitcast.35), channel_id=4, replica_groups=mesh['z2'=2,'z1'=2,'z0'=2,'y'=4,'core'=2,'x'=4,'z_hi'=2] {'z1'}, dimensions={0}, use_global_device_ids=true | all-gather | bytes 393216 | tf_op jit(solution)/shard_map/all_gather | solution.py:364
  47.1 0.8 broadcast_in_dim.7
  47.9 4.7 %all-to-all-start.1 = ((bf16[4,128,512]{2,1,0:T(8,128)(2,1)}), bf16[4,128,512]{2,1,0:T(8,128)(2,1)S(1)}, u32[]{:S(2)}, u32[]{:S(2)}) async-start(bf16[4,128,512]{2,1,0:T(8,128)(2,1)} %broadcast_in_dim.7), calls=%async_computation.1 | async-start | bytes 1048576 | tf_op jit(solution)/shard_map/all_to_all | solution.py:360
  52.6 9.4 %all-gather.3 = bf16[4,2,128,256]{3,2,1,0:T(8,128)(2,1)S(1)} all-gather(bf16[2,2,128,256]{3,2,1,0:T(8,128)(2,1)S(1)} %bitcast.33), channel_id=5, replica_groups=mesh['z2'=2,'z1'=2,'z0'=2,'y'=4,'core'=2,'x'=4,'z_hi'=2] {'z0'}, dimensions={0}, use_global_device_ids=true | all-gather | bytes 786432 | tf_op jit(solution)/shard_map/all_gather | solution.py:364
  62.1 1.9 %collective-permute-start = (bf16[8,128,256]{2,1,0:T(8,128)(2,1)S(1)}, bf16[8,128,256]{2,1,0:T(8,128)(2,1)}, u32[]{:S(2)}, u32[]{:S(2)}) collective-permute-start(bf16[8,128,256]{2,1,0:T(8,128)(2,1)S(1)} %bitcast.29), channel_id=1, source_target_pairs={{0,8},{8,0},{1,9},{9,1},{2,10},{10,2},{3,11},{11,3},{4,12},{12,4},... | collective-permute-start | bytes 1572872 | tf_op jit(solution)/shard_map/ppermute | solution.py:368
  64.1 1.9 %collective-permute-done.kv1 = bf16[8,128,256]{2,1,0:T(8,128)(2,1)} collective-permute-done((bf16[8,128,256]{2,1,0:T(8,128)(2,1)S(1)}, bf16[8,128,256]{2,1,0:T(8,128)(2,1)}, u32[]{:S(2)}, u32[]{:S(2)}) %collective-permute-start) | collective-permute-done | bytes 524320 | tf_op jit(solution)/shard_map/ppermute | solution.py:368
  66.0 7.5 %shard_map.102 = (bf16[4,128,256]{2,1,0:T(8,128)(2,1)S(1)}, f32[4,1,256]{2,1,0:T(1,128)S(1)}) custom-call(s32[4]{0:T(128)S(1)} %pad_add_fusion.at_ref, s32[128]{0:T(128)S(1)} %copy-done.9, s32[16]{0:T(128)S(1)} %copy-done.10, bf16[4,128,512]{2,1,0:T(8,128)(2,1)S(1)} %all-to-all-done.1.q_ref.grad_ref, bf16[8,128,256]{2,1,0:T(8,128)(2,1)S(1)} %bitcast.30, ...), custom_call_target="tpu_custom_call" | custom-call | flops 8000000000 | bytes 2097152 | tf_op jit(solution)/shard_map/pallas_call | solution.py:348
  74.6 4.8 %all-to-all-start.2 = ((bf16[4,160,256]{2,1,0:T(8,128)(2,1)}), bf16[4,160,256]{2,1,0:T(8,128)(2,1)S(1)}, u32[]{:S(2)}, u32[]{:S(2)}) async-start(bf16[4,160,256]{2,1,0:T(8,128)(2,1)} %copy-done.1), calls=%async_computation.2 | async-start | bytes 655360 | tf_op jit(solution)/shard_map/all_to_all | solution.py:422
  79.4 3.0 %shard_map.104.plan_ref = s32[128]{0:T(128)S(1)} custom-call(s32[4]{0:T(128)S(1)} %pad_add_fusion.at_ref, s32[128]{0:T(128)S(1)} %copy-done.9, s32[16]{0:T(128)S(1)} %copy-done.10), custom_call_target="tpu_custom_call" | custom-call | flops 3000000000 | bytes 2097152 | tf_op jit(solution)/shard_map/pallas_call | solution.py:348
  82.5 2.6 %all-to-all-done.2.parts_ref = bf16[4,160,256]{2,1,0:T(8,128)(2,1)S(1)} async-done(((bf16[4,160,256]{2,1,0:T(8,128)(2,1)}), bf16[4,160,256]{2,1,0:T(8,128)(2,1)S(1)}, u32[]{:S(2)}, u32[]{:S(2)}) %all-to-all-start.2) | async-done | bytes 327712 | tf_op jit(solution)/shard_map/all_to_all | solution.py:422
  85.0 2.6 %shard_map.105.terms_ref = bf16[4,128,1024]{2,1,0:T(8,128)(2,1)} custom-call(s32[4]{0:T(128)S(1)} %pad_add_fusion.at_ref, bf16[4,160,256]{2,1,0:T(8,128)(2,1)S(1)} %all-to-all-done.2.parts_ref, bf16[4,1024,256]{2,1,0:T(8,128)(2,1)S(1)} %bitcast.28), custom_call_target="tpu_custom_call" | custom-call | flops 1000000000 | bytes 2097152 | tf_op jit(solution)/shard_map/pallas_call | solution.py:348
  87.7 4.2 %all-to-all-start.3 = ((bf16[4,128,1024]{2,1,0:T(8,128)(2,1)}), bf16[4,128,1024]{2,1,0:T(8,128)(2,1)}, u32[]{:S(2)}, u32[]{:S(2)}) async-start(bf16[4,128,1024]{2,1,0:T(8,128)(2,1)} %shard_map.105.terms_ref), calls=%async_computation.3 | async-start | bytes 2097152 | tf_op jit(solution)/shard_map/all_to_all | solution.py:432
  91.9 6.4 %shard_map.106 = (bf16[128,256]{1,0:T(8,128)(2,1)S(1)}, bf16[128,256]{1,0:T(8,128)(2,1)S(1)}, bf16[128,256]{1,0:T(8,128)(2,1)S(1)}, bf16[128,256]{1,0:T(8,128)(2...) custom-call(s32[4]{0:T(128)S(1)} %pad_add_fusion.at_ref, ...), custom_call_target="tpu_custom_call" | custom-call | flops 12000000000 | bytes 2097152 | tf_op jit(solution)/shard_map/pallas_call | solution.py:348
  98.3 0.8 copy-done.2
  101.0 5.2 %all-to-all-done.3 = bf16[4,128,1024]{2,1,0:T(8,128)(2,1)} async-done(((bf16[4,128,1024]{2,1,0:T(8,128)(2,1)}), bf16[4,128,1024]{2,1,0:T(8,128)(2,1)}, u32[]{:S(2)}, u32[]{:S(2)}) %all-to-all-start.3) | async-done | bytes 1048608 | tf_op jit(solution)/shard_map/all_to_all | solution.py:432
  106.2 2.0 %collective-permute-start.1 = (bf16[4,2,128,256]{3,2,1,0:T(8,128)(2,1)}, bf16[4,2,128,256]{3,2,1,0:T(8,128)(2,1)S(1)}, u32[]{:S(2)}, u32[]{:S(2)}) collective-permute-start(bf16[4,2,128,256]{3,2,1,0:T(8,128)(2,1)} %copy-done.2), channel_id=1, source_target_pairs={{0,8},{8,0},{1,9},{9,1},{2,10},{10,2},{3,11},{11,3},{4,12},{12,4},... | collective-permute-start | bytes 1572872 | tf_op jit(solution)/shard_map/ppermute | solution.py:368
  108.3 2.1 %collective-permute-done.1 = bf16[4,2,128,256]{3,2,1,0:T(8,128)(2,1)S(1)} collective-permute-done((bf16[4,2,128,256]{3,2,1,0:T(8,128)(2,1)}, bf16[4,2,128,256]{3,2,1,0:T(8,128)(2,1)S(1)}, u32[]{:S(2)}, u32[]{:S(2)}) %collective-permute-start.1) | collective-permute-done | bytes 524320 | tf_op jit(solution)/shard_map/ppermute | solution.py:368
  110.3 0.9 add_convert_fusion
  111.3 6.6 %all-to-all-start.4 = ((bf16[4,2,128,256]{3,2,1,0:T(8,128)(2,1)}), bf16[4,2,128,256]{3,2,1,0:T(8,128)(2,1)S(1)}, u32[]{:S(2)}, u32[]{:S(2)}) async-start(bf16[4,2,128,256]{3,2,1,0:T(8,128)(2,1)} %add_convert_fusion), calls=%async_computation.4 | async-start | bytes 1048576 | tf_op jit(solution)/shard_map/all_to_all | solution.py:458
  117.9 1.5 convert_reduce_fusion
  119.4 9.4 %collective-permute-start.2 = (bf16[128,512]{1,0:T(8,128)(2,1)S(1)}, bf16[128,512]{1,0:T(8,128)(2,1)S(1)}, u32[]{:S(2)}, u32[]{:S(2)}) collective-permute-start(bf16[128,512]{1,0:T(8,128)(2,1)S(1)} %select_convert_fusion), channel_id=1, source_target_pairs={{0,1},{1,0},{2,3},{3,2},{4,5},{5,4},{6,7},{7,6},{8,9},{9,8},{10,11... | collective-permute-start | bytes 393224 | tf_op jit(solution)/shard_map/ppermute | solution.py:368
  128.8 2.2 %collective-permute-start.3 = (bf16[128,256]{1,0:T(8,128)(2,1)S(1)}, bf16[128,256]{1,0:T(8,128)(2,1)S(1)}, u32[]{:S(2)}, u32[]{:S(2)}) collective-permute-start(bf16[128,256]{1,0:T(8,128)(2,1)S(1)} %copy-done.8), channel_id=1, source_target_pairs={{0,16},{16,0},{32,48},{48,32},{1,17},{17,1},{33,49},{49,33},{2,18}... | collective-permute-start | bytes 196616 | tf_op jit(solution)/shard_map/ppermute | solution.py:457
  131.1 5.1 %collective-permute-start.4 = (bf16[128,256]{1,0:T(8,128)(2,1)S(1)}, bf16[128,256]{1,0:T(8,128)(2,1)S(1)}, u32[]{:S(2)}, u32[]{:S(2)}) collective-permute-start(bf16[128,256]{1,0:T(8,128)(2,1)S(1)} %copy-done.6), channel_id=1, source_target_pairs={{0,32},{16,48},{32,0},{48,16},{1,33},{17,49},{33,1},{49,17},{2,34}... | collective-permute-start | bytes 196616 | tf_op jit(solution)/shard_map/ppermute | solution.py:457
  136.2 3.1 %collective-permute-start.5 = (bf16[128,256]{1,0:T(8,128)(2,1)S(1)}, bf16[128,256]{1,0:T(8,128)(2,1)S(1)}, u32[]{:S(2)}, u32[]{:S(2)}) collective-permute-start(bf16[128,256]{1,0:T(8,128)(2,1)S(1)} %copy-done.4), channel_id=1, source_target_pairs={{0,48},{16,32},{32,16},{48,0},{1,49},{17,33},{33,17},{49,1},{2,50}... | collective-permute-start | bytes 196616 | tf_op jit(solution)/shard_map/ppermute | solution.py:457
  139.3 6.8 %collective-permute-done.2 = bf16[128,512]{1,0:T(8,128)(2,1)S(1)} collective-permute-done((bf16[128,512]{1,0:T(8,128)(2,1)S(1)}, bf16[128,512]{1,0:T(8,128)(2,1)S(1)}, u32[]{:S(2)}, u32[]{:S(2)}) %collective-permute-start.2) | collective-permute-done | bytes 131104 | tf_op jit(solution)/shard_map/ppermute | solution.py:368
  146.9 1.9 %collective-permute-start.6 = (bf16[128,256]{1,0:T(8,128)(2,1)S(1)}, bf16[128,256]{1,0:T(8,128)(2,1)S(1)}, u32[]{:S(2)}, u32[]{:S(2)}) collective-permute-start(bf16[128,256]{1,0:T(8,128)(2,1)S(1)} %fusion.3), channel_id=1, source_target_pairs={{0,256},{256,0},{1,257},{257,1},{2,258},{258,2},{3,259},{259,3},{4... | collective-permute-start | bytes 196616 | tf_op jit(solution)/shard_map/ppermute | solution.py:368
  149.5 8.5 %collective-permute-done.6 = bf16[128,256]{1,0:T(8,128)(2,1)S(1)} collective-permute-done((bf16[128,256]{1,0:T(8,128)(2,1)S(1)}, bf16[128,256]{1,0:T(8,128)(2,1)S(1)}, u32[]{:S(2)}, u32[]{:S(2)}) %collective-permute-start.6) | collective-permute-done | bytes 65568 | tf_op jit(solution)/shard_map/ppermute | solution.py:368
  (40 shorter events, 5.7 us)
Async XLA Ops:
  19.2 27.4 %copy-start = (bf16[4096,256]{1,0:T(8,128)(2,1)S(1)}, bf16[4096,256]{1,0:T(8,128)(2,1)}, u32[]{:S(2)}) copy-start(bf16[4096,256]{1,0:T(8,128)(2,1)} %param.10) | copy-start | bytes 6291460
  21.2 25.4 %all-to-all-start = ((bf16[4,2,128,512]{3,2,1,0:T(8,128)(2,1)}), bf16[4,2,128,512]{3,2,1,0:T(8,128)(2,1)S(1)}, u32[]{:S(2)}, u32[]{:S(2)}) async-start(bf16[4,2,128,512]{3,2,1,0:T(8,128)(2,1)} %broadcast_in_dim.6), calls=%async_computation | async-start | bytes 2097152 | tf_op jit(solution)/shard_map/all_to_all | solution.py:360
  25.5 21.5 %copy-start.11 = (bf16[128,256]{1,0:T(8,128)(2,1)S(1)}, bf16[128,256]{1,0:T(8,128)(2,1)}, u32[]{:S(2)}) copy-start(bf16[128,256]{1,0:T(8,128)(2,1)} %param.7) | copy-start | bytes 196612
  47.1 18.9 %copy-start.9 = (s32[128]{0:T(128)S(1)}, s32[128]{0:T(128)}, u32[]{:S(2)}) copy-start(s32[128]{0:T(128)} %order_ref.2) | copy-start | bytes 1540
  47.1 18.9 %copy-start.10 = (s32[16]{0:T(128)S(1)}, s32[16]{0:T(128)}, u32[]{:S(2)}) copy-start(s32[16]{0:T(128)} %lengths_ref.5) | copy-start | bytes 196
  47.9 14.1 %all-to-all-start.1 = ((bf16[4,128,512]{2,1,0:T(8,128)(2,1)}), bf16[4,128,512]{2,1,0:T(8,128)(2,1)S(1)}, u32[]{:S(2)}, u32[]{:S(2)}) async-start(bf16[4,128,512]{2,1,0:T(8,128)(2,1)} %broadcast_in_dim.7), calls=%async_computation.1 | async-start | bytes 1048576 | tf_op jit(solution)/shard_map/all_to_all | solution.py:360
  62.1 3.9 %collective-permute-start = (bf16[8,128,256]{2,1,0:T(8,128)(2,1)S(1)}, bf16[8,128,256]{2,1,0:T(8,128)(2,1)}, u32[]{:S(2)}, u32[]{:S(2)}) collective-permute-start(bf16[8,128,256]{2,1,0:T(8,128)(2,1)S(1)} %bitcast.29), channel_id=1, source_target_pairs={{0,8},{8,0},{1,9},{9,1},{2,10},{10,2},{3,11},{11,3},{4,12},{12,4},... | collective-permute-start | bytes 1572872 | tf_op jit(solution)/shard_map/ppermute | solution.py:368
  73.9 0.7 copy-start.1
  74.6 10.4 %all-to-all-start.2 = ((bf16[4,160,256]{2,1,0:T(8,128)(2,1)}), bf16[4,160,256]{2,1,0:T(8,128)(2,1)S(1)}, u32[]{:S(2)}, u32[]{:S(2)}) async-start(bf16[4,160,256]{2,1,0:T(8,128)(2,1)} %copy-done.1), calls=%async_computation.2 | async-start | bytes 655360 | tf_op jit(solution)/shard_map/all_to_all | solution.py:422
  87.7 18.5 %all-to-all-start.3 = ((bf16[4,128,1024]{2,1,0:T(8,128)(2,1)}), bf16[4,128,1024]{2,1,0:T(8,128)(2,1)}, u32[]{:S(2)}, u32[]{:S(2)}) async-start(bf16[4,128,1024]{2,1,0:T(8,128)(2,1)} %shard_map.105.terms_ref), calls=%async_computation.3 | async-start | bytes 2097152 | tf_op jit(solution)/shard_map/all_to_all | solution.py:432
  98.3 0.8 copy-start.2
  99.1 0.6 copy-start.3
  99.7 0.6 copy-start.5
  100.4 0.6 copy-start.7
  106.2 22.6 %copy-start.8 = (bf16[128,256]{1,0:T(8,128)(2,1)S(1)}, bf16[128,256]{1,0:T(8,128)(2,1)}, u32[]{:S(2)}) copy-start(bf16[128,256]{1,0:T(8,128)(2,1)} %copy-done.7) | copy-start | bytes 196612
  106.2 24.8 %copy-start.6 = (bf16[128,256]{1,0:T(8,128)(2,1)S(1)}, bf16[128,256]{1,0:T(8,128)(2,1)}, u32[]{:S(2)}) copy-start(bf16[128,256]{1,0:T(8,128)(2,1)} %copy-done.5) | copy-start | bytes 196612
  106.2 30.0 %copy-start.4 = (bf16[128,256]{1,0:T(8,128)(2,1)S(1)}, bf16[128,256]{1,0:T(8,128)(2,1)}, u32[]{:S(2)}) copy-start(bf16[128,256]{1,0:T(8,128)(2,1)} %copy-done.3) | copy-start | bytes 196612
  106.2 4.1 %collective-permute-start.1 = (bf16[4,2,128,256]{3,2,1,0:T(8,128)(2,1)}, bf16[4,2,128,256]{3,2,1,0:T(8,128)(2,1)S(1)}, u32[]{:S(2)}, u32[]{:S(2)}) collective-permute-start(bf16[4,2,128,256]{3,2,1,0:T(8,128)(2,1)} %copy-done.2), channel_id=1, source_target_pairs={{0,8},{8,0},{1,9},{9,1},{2,10},{10,2},{3,11},{11,3},{4,12},{12,4},... | collective-permute-start | bytes 1572872 | tf_op jit(solution)/shard_map/ppermute | solution.py:368
  111.3 35.5 %all-to-all-start.4 = ((bf16[4,2,128,256]{3,2,1,0:T(8,128)(2,1)}), bf16[4,2,128,256]{3,2,1,0:T(8,128)(2,1)S(1)}, u32[]{:S(2)}, u32[]{:S(2)}) async-start(bf16[4,2,128,256]{3,2,1,0:T(8,128)(2,1)} %add_convert_fusion), calls=%async_computation.4 | async-start | bytes 1048576 | tf_op jit(solution)/shard_map/all_to_all | solution.py:458
  119.4 26.7 %collective-permute-start.2 = (bf16[128,512]{1,0:T(8,128)(2,1)S(1)}, bf16[128,512]{1,0:T(8,128)(2,1)S(1)}, u32[]{:S(2)}, u32[]{:S(2)}) collective-permute-start(bf16[128,512]{1,0:T(8,128)(2,1)S(1)} %select_convert_fusion), channel_id=1, source_target_pairs={{0,1},{1,0},{2,3},{3,2},{4,5},{5,4},{6,7},{7,6},{8,9},{9,8},{10,11... | collective-permute-start | bytes 393224 | tf_op jit(solution)/shard_map/ppermute | solution.py:368
  128.8 17.9 %collective-permute-start.3 = (bf16[128,256]{1,0:T(8,128)(2,1)S(1)}, bf16[128,256]{1,0:T(8,128)(2,1)S(1)}, u32[]{:S(2)}, u32[]{:S(2)}) collective-permute-start(bf16[128,256]{1,0:T(8,128)(2,1)S(1)} %copy-done.8), channel_id=1, source_target_pairs={{0,16},{16,0},{32,48},{48,32},{1,17},{17,1},{33,49},{49,33},{2,18}... | collective-permute-start | bytes 196616 | tf_op jit(solution)/shard_map/ppermute | solution.py:457
  131.1 15.7 %collective-permute-start.4 = (bf16[128,256]{1,0:T(8,128)(2,1)S(1)}, bf16[128,256]{1,0:T(8,128)(2,1)S(1)}, u32[]{:S(2)}, u32[]{:S(2)}) collective-permute-start(bf16[128,256]{1,0:T(8,128)(2,1)S(1)} %copy-done.6), channel_id=1, source_target_pairs={{0,32},{16,48},{32,0},{48,16},{1,33},{17,49},{33,1},{49,17},{2,34}... | collective-permute-start | bytes 196616 | tf_op jit(solution)/shard_map/ppermute | solution.py:457
  136.2 10.6 %collective-permute-start.5 = (bf16[128,256]{1,0:T(8,128)(2,1)S(1)}, bf16[128,256]{1,0:T(8,128)(2,1)S(1)}, u32[]{:S(2)}, u32[]{:S(2)}) collective-permute-start(bf16[128,256]{1,0:T(8,128)(2,1)S(1)} %copy-done.4), channel_id=1, source_target_pairs={{0,48},{16,32},{32,16},{48,0},{1,49},{17,33},{33,17},{49,1},{2,50}... | collective-permute-start | bytes 196616 | tf_op jit(solution)/shard_map/ppermute | solution.py:457
  146.9 11.1 %collective-permute-start.6 = (bf16[128,256]{1,0:T(8,128)(2,1)S(1)}, bf16[128,256]{1,0:T(8,128)(2,1)S(1)}, u32[]{:S(2)}, u32[]{:S(2)}) collective-permute-start(bf16[128,256]{1,0:T(8,128)(2,1)S(1)} %fusion.3), channel_id=1, source_target_pairs={{0,256},{256,0},{1,257},{257,1},{2,258},{258,2},{3,259},{259,3},{4... | collective-permute-start | bytes 196616 | tf_op jit(solution)/shard_map/ppermute | solution.py:368

commit v6 on v5

--- a/solution.py
+++ b/solution.py
@@ -466,9 +466,10 @@
     for x in partial:
         dq = dq + x.astype(f32)
     grad_query = dq.astype(bf16)
-    both = jnp.sum(both.astype(f32), axis=0)
-    late = swap(both[1].astype(bf16), "z2")
-    grad_kv = (both[0] + late.astype(f32)).astype(bf16)
+    late = jnp.sum(both[:, 1].astype(f32), axis=0).astype(bf16)
+    late = swap(late, "z2")
+    stay = jnp.sum(both[:, 0].astype(f32), axis=0)
+    grad_kv = (stay + late.astype(f32)).astype(bf16)
     return projected, grad_query, grad_kv[:, :HD], grad_kv[:, HD:]
 
 

time: 160 us -> 160 us (level)
  no operation moved by 1% of the time
where the time goes in v6:
time: 160 us; the launch traced here: 158 us
  starting transfers between devices  50.3 us (31%)
  blocking collectives  49.1 us (31%)
  waiting for transfers between devices  26.7 us (17%)
  Pallas kernels  19.9 us (12%)
  local copies, waits for them, and re-layouts  5.97 us (4%)
  other arithmetic  4.9 us (3%)
    all_gather x4, blocking collectives, gather(): return lax.all_gather(x, axis, axis=0)  49.1 us
    pallas_call x5, Pallas kernels, call(): pl.pallas_call(kernel, out_shape=[jax.ShapeDtypeStruct(*o) for o in outs]...  19.9 us
    ppermute x4, waiting for transfers between devices, swap(): return lax.ppermute(x, axis, [(0, 1), (1, 0)])  18.9 us
    ppermute x4, starting transfers between devices, swap(): return lax.ppermute(x, axis, [(0, 1), (1, 0)])  15.3 us
    ppermute x3, starting transfers between devices, per_device(): lax.ppermute(x, 'y', [(i, i ^ k) for i in range(4)])  10.4 us
    all_to_all x2, starting transfers between devices, spread(): return lax.all_to_all(jnp.broadcast_to(x, (n,) + x.shape), axis, 0, 0)  8.98 us
    all_to_all x1, starting transfers between devices, per_device(): both = lax.all_to_all(both, ('z1', 'z0'), 0, 0)  6.63 us
    all_to_all x1, waiting for transfers between devices, per_device(): all_terms = lax.all_to_all(terms, 'x', 0, 0)  5.22 us
  transfers between devices with their start and end apart: 12, of which 6 were waited for; matrix products, arithmetic and copies ran while one was open for 2% of the time, Pallas kernels for 6%

profile of v6, /device:TPU:24, one launch (start us, length us, event | category | flops | bytes accessed | tf_op | source)
XLA Modules:
  0.0 158.2 jit_solution(8607455901569878373)
XLA Ops:
  0.6 18.5 %all-gather = bf16[256,512]{1,0:T(8,128)(2,1)S(1)} all-gather(bf16[128,512]{1,0:T(8,128)(2,1)} %param.11), channel_id=2, replica_groups=mesh['z2'=2,'z1'=2,'z0'=2,'y'=4,'core'=2,'x'=4,'z_hi'=2] {'z_hi'}, dimensions={0}, use_global_device_ids=true | all-gather | bytes 393216 | tf_op jit(solution)/shard_map/all_gather | solution.py:364
  19.2 0.9 pad_maximum_fusion.1
  20.1 1.1 broadcast_in_dim.6
  21.2 4.3 %all-to-all-start = ((bf16[4,2,128,512]{3,2,1,0:T(8,128)(2,1)}), bf16[4,2,128,512]{3,2,1,0:T(8,128)(2,1)S(1)}, u32[]{:S(2)}, u32[]{:S(2)}) async-start(bf16[4,2,128,512]{3,2,1,0:T(8,128)(2,1)} %broadcast_in_dim.6), calls=%async_computation | async-start | bytes 2097152 | tf_op jit(solution)/shard_map/all_to_all | solution.py:360
  25.5 13.4 %all-gather.1 = bf16[256,256]{1,0:T(8,128)(2,1)S(1)} all-gather(bf16[128,256]{1,0:T(8,128)(2,1)S(1)} %pad_maximum_fusion.1), channel_id=3, replica_groups=mesh['z2'=2,'z1'=2,'z0'=2,'y'=4,'core'=2,'x'=4,'z_hi'=2] {'z2'}, dimensions={0}, use_global_device_ids=true | all-gather | bytes 196608 | tf_op jit(solution)/shard_map/all_gather | solution.py:364
  38.9 7.6 %all-gather.2 = bf16[4,128,256]{2,1,0:T(8,128)(2,1)S(1)} all-gather(bf16[2,128,256]{2,1,0:T(8,128)(2,1)S(1)} %bitcast.27), channel_id=4, replica_groups=mesh['z2'=2,'z1'=2,'z0'=2,'y'=4,'core'=2,'x'=4,'z_hi'=2] {'z1'}, dimensions={0}, use_global_device_ids=true | all-gather | bytes 393216 | tf_op jit(solution)/shard_map/all_gather | solution.py:364
  47.1 0.8 broadcast_in_dim.7
  47.9 4.7 %all-to-all-start.1 = ((bf16[4,128,512]{2,1,0:T(8,128)(2,1)}), bf16[4,128,512]{2,1,0:T(8,128)(2,1)S(1)}, u32[]{:S(2)}, u32[]{:S(2)}) async-start(bf16[4,128,512]{2,1,0:T(8,128)(2,1)} %broadcast_in_dim.7), calls=%async_computation.1 | async-start | bytes 1048576 | tf_op jit(solution)/shard_map/all_to_all | solution.py:360
  52.6 9.4 %all-gather.3 = bf16[4,2,128,256]{3,2,1,0:T(8,128)(2,1)S(1)} all-gather(bf16[2,2,128,256]{3,2,1,0:T(8,128)(2,1)S(1)} %bitcast.25), channel_id=5, replica_groups=mesh['z2'=2,'z1'=2,'z0'=2,'y'=4,'core'=2,'x'=4,'z_hi'=2] {'z0'}, dimensions={0}, use_global_device_ids=true | all-gather | bytes 786432 | tf_op jit(solution)/shard_map/all_gather | solution.py:364
  62.0 1.9 %collective-permute-start = (bf16[8,128,256]{2,1,0:T(8,128)(2,1)S(1)}, bf16[8,128,256]{2,1,0:T(8,128)(2,1)}, u32[]{:S(2)}, u32[]{:S(2)}) collective-permute-start(bf16[8,128,256]{2,1,0:T(8,128)(2,1)S(1)} %bitcast.21), channel_id=1, source_target_pairs={{0,8},{8,0},{1,9},{9,1},{2,10},{10,2},{3,11},{11,3},{4,12},{12,4},... | collective-permute-start | bytes 1572872 | tf_op jit(solution)/shard_map/ppermute | solution.py:368
  64.1 1.9 %collective-permute-done.kv1 = bf16[8,128,256]{2,1,0:T(8,128)(2,1)} collective-permute-done((bf16[8,128,256]{2,1,0:T(8,128)(2,1)S(1)}, bf16[8,128,256]{2,1,0:T(8,128)(2,1)}, u32[]{:S(2)}, u32[]{:S(2)}) %collective-permute-start) | collective-permute-done | bytes 524320 | tf_op jit(solution)/shard_map/ppermute | solution.py:368
  66.0 7.5 %shard_map.102 = (bf16[4,128,256]{2,1,0:T(8,128)(2,1)S(1)}, f32[4,1,256]{2,1,0:T(1,128)S(1)}) custom-call(s32[4]{0:T(128)S(1)} %pad_add_fusion.at_ref, s32[128]{0:T(128)S(1)} %copy-done.9, s32[16]{0:T(128)S(1)} %copy-done.10, bf16[4,128,512]{2,1,0:T(8,128)(2,1)S(1)} %all-to-all-done.1.q_ref.grad_ref, bf16[8,128,256]{2,1,0:T(8,128)(2,1)S(1)} %bitcast.22, ...), custom_call_target="tpu_custom_call" | custom-call | flops 8000000000 | bytes 2097152 | tf_op jit(solution)/shard_map/pallas_call | solution.py:348
  74.6 4.8 %all-to-all-start.2 = ((bf16[4,160,256]{2,1,0:T(8,128)(2,1)}), bf16[4,160,256]{2,1,0:T(8,128)(2,1)S(1)}, u32[]{:S(2)}, u32[]{:S(2)}) async-start(bf16[4,160,256]{2,1,0:T(8,128)(2,1)} %copy-done.1), calls=%async_computation.2 | async-start | bytes 655360 | tf_op jit(solution)/shard_map/all_to_all | solution.py:422
  79.4 3.0 %shard_map.104.plan_ref = s32[128]{0:T(128)S(1)} custom-call(s32[4]{0:T(128)S(1)} %pad_add_fusion.at_ref, s32[128]{0:T(128)S(1)} %copy-done.9, s32[16]{0:T(128)S(1)} %copy-done.10), custom_call_target="tpu_custom_call" | custom-call | flops 3000000000 | bytes 2097152 | tf_op jit(solution)/shard_map/pallas_call | solution.py:348
  82.4 2.6 %all-to-all-done.2.parts_ref = bf16[4,160,256]{2,1,0:T(8,128)(2,1)S(1)} async-done(((bf16[4,160,256]{2,1,0:T(8,128)(2,1)}), bf16[4,160,256]{2,1,0:T(8,128)(2,1)S(1)}, u32[]{:S(2)}, u32[]{:S(2)}) %all-to-all-start.2) | async-done | bytes 327712 | tf_op jit(solution)/shard_map/all_to_all | solution.py:422
  85.0 2.6 %shard_map.105.terms_ref = bf16[4,128,1024]{2,1,0:T(8,128)(2,1)} custom-call(s32[4]{0:T(128)S(1)} %pad_add_fusion.at_ref, bf16[4,160,256]{2,1,0:T(8,128)(2,1)S(1)} %all-to-all-done.2.parts_ref, bf16[4,1024,256]{2,1,0:T(8,128)(2,1)S(1)} %bitcast.20), custom_call_target="tpu_custom_call" | custom-call | flops 1000000000 | bytes 2097152 | tf_op jit(solution)/shard_map/pallas_call | solution.py:348
  87.6 4.2 %all-to-all-start.3 = ((bf16[4,128,1024]{2,1,0:T(8,128)(2,1)}), bf16[4,128,1024]{2,1,0:T(8,128)(2,1)}, u32[]{:S(2)}, u32[]{:S(2)}) async-start(bf16[4,128,1024]{2,1,0:T(8,128)(2,1)} %shard_map.105.terms_ref), calls=%async_computation.3 | async-start | bytes 2097152 | tf_op jit(solution)/shard_map/all_to_all | solution.py:432
  91.9 6.4 %shard_map.106 = (bf16[128,256]{1,0:T(8,128)(2,1)S(1)}, bf16[128,256]{1,0:T(8,128)(2,1)S(1)}, bf16[128,256]{1,0:T(8,128)(2,1)S(1)}, bf16[128,256]{1,0:T(8,128)(2...) custom-call(s32[4]{0:T(128)S(1)} %pad_add_fusion.at_ref, ...), custom_call_target="tpu_custom_call" | custom-call | flops 12000000000 | bytes 2097152 | tf_op jit(solution)/shard_map/pallas_call | solution.py:348
  98.3 0.8 copy-done.2
  100.9 5.2 %all-to-all-done.3 = bf16[4,128,1024]{2,1,0:T(8,128)(2,1)} async-done(((bf16[4,128,1024]{2,1,0:T(8,128)(2,1)}), bf16[4,128,1024]{2,1,0:T(8,128)(2,1)}, u32[]{:S(2)}, u32[]{:S(2)}) %all-to-all-start.3) | async-done | bytes 1048608 | tf_op jit(solution)/shard_map/all_to_all | solution.py:432
  106.2 2.0 %collective-permute-start.1 = (bf16[4,2,128,256]{3,2,1,0:T(8,128)(2,1)}, bf16[4,2,128,256]{3,2,1,0:T(8,128)(2,1)S(1)}, u32[]{:S(2)}, u32[]{:S(2)}) collective-permute-start(bf16[4,2,128,256]{3,2,1,0:T(8,128)(2,1)} %copy-done.2), channel_id=1, source_target_pairs={{0,8},{8,0},{1,9},{9,1},{2,10},{10,2},{3,11},{11,3},{4,12},{12,4},... | collective-permute-start | bytes 1572872 | tf_op jit(solution)/shard_map/ppermute | solution.py:368
  108.2 2.1 %collective-permute-done.1 = bf16[4,2,128,256]{3,2,1,0:T(8,128)(2,1)S(1)} collective-permute-done((bf16[4,2,128,256]{3,2,1,0:T(8,128)(2,1)}, bf16[4,2,128,256]{3,2,1,0:T(8,128)(2,1)S(1)}, u32[]{:S(2)}, u32[]{:S(2)}) %collective-permute-start.1) | collective-permute-done | bytes 524320 | tf_op jit(solution)/shard_map/ppermute | solution.py:368
  110.3 0.9 add_convert_fusion
  111.2 6.6 %all-to-all-start.4 = ((bf16[4,2,128,256]{3,2,1,0:T(8,128)(2,1)}), bf16[4,2,128,256]{3,2,1,0:T(8,128)(2,1)S(1)}, u32[]{:S(2)}, u32[]{:S(2)}) async-start(bf16[4,2,128,256]{3,2,1,0:T(8,128)(2,1)} %add_convert_fusion), calls=%async_computation.4 | async-start | bytes 1048576 | tf_op jit(solution)/shard_map/all_to_all | solution.py:458
  117.9 1.5 convert_reduce_fusion
  119.4 9.4 %collective-permute-start.2 = (bf16[128,512]{1,0:T(8,128)(2,1)S(1)}, bf16[128,512]{1,0:T(8,128)(2,1)S(1)}, u32[]{:S(2)}, u32[]{:S(2)}) collective-permute-start(bf16[128,512]{1,0:T(8,128)(2,1)S(1)} %select_convert_fusion), channel_id=1, source_target_pairs={{0,1},{1,0},{2,3},{3,2},{4,5},{5,4},{6,7},{7,6},{8,9},{9,8},{10,11... | collective-permute-start | bytes 393224 | tf_op jit(solution)/shard_map/ppermute | solution.py:368
  128.8 2.2 %collective-permute-start.3 = (bf16[128,256]{1,0:T(8,128)(2,1)S(1)}, bf16[128,256]{1,0:T(8,128)(2,1)S(1)}, u32[]{:S(2)}, u32[]{:S(2)}) collective-permute-start(bf16[128,256]{1,0:T(8,128)(2,1)S(1)} %copy-done.8), channel_id=1, source_target_pairs={{0,16},{16,0},{32,48},{48,32},{1,17},{17,1},{33,49},{49,33},{2,18}... | collective-permute-start | bytes 196616 | tf_op jit(solution)/shard_map/ppermute | solution.py:457
  131.0 5.1 %collective-permute-start.4 = (bf16[128,256]{1,0:T(8,128)(2,1)S(1)}, bf16[128,256]{1,0:T(8,128)(2,1)S(1)}, u32[]{:S(2)}, u32[]{:S(2)}) collective-permute-start(bf16[128,256]{1,0:T(8,128)(2,1)S(1)} %copy-done.6), channel_id=1, source_target_pairs={{0,32},{16,48},{32,0},{48,16},{1,33},{17,49},{33,1},{49,17},{2,34}... | collective-permute-start | bytes 196616 | tf_op jit(solution)/shard_map/ppermute | solution.py:457
  136.2 3.1 %collective-permute-start.5 = (bf16[128,256]{1,0:T(8,128)(2,1)S(1)}, bf16[128,256]{1,0:T(8,128)(2,1)S(1)}, u32[]{:S(2)}, u32[]{:S(2)}) collective-permute-start(bf16[128,256]{1,0:T(8,128)(2,1)S(1)} %copy-done.4), channel_id=1, source_target_pairs={{0,48},{16,32},{32,16},{48,0},{1,49},{17,33},{33,17},{49,1},{2,50}... | collective-permute-start | bytes 196616 | tf_op jit(solution)/shard_map/ppermute | solution.py:457
  139.2 6.8 %collective-permute-done.2 = bf16[128,512]{1,0:T(8,128)(2,1)S(1)} collective-permute-done((bf16[128,512]{1,0:T(8,128)(2,1)S(1)}, bf16[128,512]{1,0:T(8,128)(2,1)S(1)}, u32[]{:S(2)}, u32[]{:S(2)}) %collective-permute-start.2) | collective-permute-done | bytes 131104 | tf_op jit(solution)/shard_map/ppermute | solution.py:368
  146.8 1.9 %collective-permute-start.6 = (bf16[128,256]{1,0:T(8,128)(2,1)S(1)}, bf16[128,256]{1,0:T(8,128)(2,1)S(1)}, u32[]{:S(2)}, u32[]{:S(2)}) collective-permute-start(bf16[128,256]{1,0:T(8,128)(2,1)S(1)} %slice_reduce_fusion), channel_id=1, source_target_pairs={{0,256},{256,0},{1,257},{257,1},{2,258},{258,2},{3,259},{259,3},{4... | collective-permute-start | bytes 196616 | tf_op jit(solution)/shard_map/ppermute | solution.py:368
  149.4 8.1 %collective-permute-done.6 = bf16[128,256]{1,0:T(8,128)(2,1)S(1)} collective-permute-done((bf16[128,256]{1,0:T(8,128)(2,1)S(1)}, bf16[128,256]{1,0:T(8,128)(2,1)S(1)}, u32[]{:S(2)}, u32[]{:S(2)}) %collective-permute-start.6) | collective-permute-done | bytes 65568 | tf_op jit(solution)/shard_map/ppermute | solution.py:368
  (40 shorter events, 5.7 us)
Async XLA Ops:
  19.2 27.4 %copy-start = (bf16[4096,256]{1,0:T(8,128)(2,1)S(1)}, bf16[4096,256]{1,0:T(8,128)(2,1)}, u32[]{:S(2)}) copy-start(bf16[4096,256]{1,0:T(8,128)(2,1)} %param.10) | copy-start | bytes 6291460
  21.2 25.4 %all-to-all-start = ((bf16[4,2,128,512]{3,2,1,0:T(8,128)(2,1)}), bf16[4,2,128,512]{3,2,1,0:T(8,128)(2,1)S(1)}, u32[]{:S(2)}, u32[]{:S(2)}) async-start(bf16[4,2,128,512]{3,2,1,0:T(8,128)(2,1)} %broadcast_in_dim.6), calls=%async_computation | async-start | bytes 2097152 | tf_op jit(solution)/shard_map/all_to_all | solution.py:360
  25.5 21.5 %copy-start.11 = (bf16[128,256]{1,0:T(8,128)(2,1)S(1)}, bf16[128,256]{1,0:T(8,128)(2,1)}, u32[]{:S(2)}) copy-start(bf16[128,256]{1,0:T(8,128)(2,1)} %param.7) | copy-start | bytes 196612
  47.0 18.9 %copy-start.9 = (s32[128]{0:T(128)S(1)}, s32[128]{0:T(128)}, u32[]{:S(2)}) copy-start(s32[128]{0:T(128)} %order_ref.2) | copy-start | bytes 1540
  47.0 18.9 %copy-start.10 = (s32[16]{0:T(128)S(1)}, s32[16]{0:T(128)}, u32[]{:S(2)}) copy-start(s32[16]{0:T(128)} %lengths_ref.5) | copy-start | bytes 196
  47.9 14.1 %all-to-all-start.1 = ((bf16[4,128,512]{2,1,0:T(8,128)(2,1)}), bf16[4,128,512]{2,1,0:T(8,128)(2,1)S(1)}, u32[]{:S(2)}, u32[]{:S(2)}) async-start(bf16[4,128,512]{2,1,0:T(8,128)(2,1)} %broadcast_in_dim.7), calls=%async_computation.1 | async-start | bytes 1048576 | tf_op jit(solution)/shard_map/all_to_all | solution.py:360
  62.0 3.9 %collective-permute-start = (bf16[8,128,256]{2,1,0:T(8,128)(2,1)S(1)}, bf16[8,128,256]{2,1,0:T(8,128)(2,1)}, u32[]{:S(2)}, u32[]{:S(2)}) collective-permute-start(bf16[8,128,256]{2,1,0:T(8,128)(2,1)S(1)} %bitcast.21), channel_id=1, source_target_pairs={{0,8},{8,0},{1,9},{9,1},{2,10},{10,2},{3,11},{11,3},{4,12},{12,4},... | collective-permute-start | bytes 1572872 | tf_op jit(solution)/shard_map/ppermute | solution.py:368
  73.9 0.7 copy-start.1
  74.6 10.4 %all-to-all-start.2 = ((bf16[4,160,256]{2,1,0:T(8,128)(2,1)}), bf16[4,160,256]{2,1,0:T(8,128)(2,1)S(1)}, u32[]{:S(2)}, u32[]{:S(2)}) async-start(bf16[4,160,256]{2,1,0:T(8,128)(2,1)} %copy-done.1), calls=%async_computation.2 | async-start | bytes 655360 | tf_op jit(solution)/shard_map/all_to_all | solution.py:422
  87.6 18.5 %all-to-all-start.3 = ((bf16[4,128,1024]{2,1,0:T(8,128)(2,1)}), bf16[4,128,1024]{2,1,0:T(8,128)(2,1)}, u32[]{:S(2)}, u32[]{:S(2)}) async-start(bf16[4,128,1024]{2,1,0:T(8,128)(2,1)} %shard_map.105.terms_ref), calls=%async_computation.3 | async-start | bytes 2097152 | tf_op jit(solution)/shard_map/all_to_all | solution.py:432
  98.3 0.8 copy-start.2
  99.0 0.6 copy-start.3
  99.7 0.6 copy-start.5
  100.3 0.6 copy-start.7
  106.2 22.6 %copy-start.8 = (bf16[128,256]{1,0:T(8,128)(2,1)S(1)}, bf16[128,256]{1,0:T(8,128)(2,1)}, u32[]{:S(2)}) copy-start(bf16[128,256]{1,0:T(8,128)(2,1)} %copy-done.7) | copy-start | bytes 196612
  106.2 24.8 %copy-start.6 = (bf16[128,256]{1,0:T(8,128)(2,1)S(1)}, bf16[128,256]{1,0:T(8,128)(2,1)}, u32[]{:S(2)}) copy-start(bf16[128,256]{1,0:T(8,128)(2,1)} %copy-done.5) | copy-start | bytes 196612
  106.2 30.0 %copy-start.4 = (bf16[128,256]{1,0:T(8,128)(2,1)S(1)}, bf16[128,256]{1,0:T(8,128)(2,1)}, u32[]{:S(2)}) copy-start(bf16[128,256]{1,0:T(8,128)(2,1)} %copy-done.3) | copy-start | bytes 196612
  106.2 4.1 %collective-permute-start.1 = (bf16[4,2,128,256]{3,2,1,0:T(8,128)(2,1)}, bf16[4,2,128,256]{3,2,1,0:T(8,128)(2,1)S(1)}, u32[]{:S(2)}, u32[]{:S(2)}) collective-permute-start(bf16[4,2,128,256]{3,2,1,0:T(8,128)(2,1)} %copy-done.2), channel_id=1, source_target_pairs={{0,8},{8,0},{1,9},{9,1},{2,10},{10,2},{3,11},{11,3},{4,12},{12,4},... | collective-permute-start | bytes 1572872 | tf_op jit(solution)/shard_map/ppermute | solution.py:368
  111.2 35.5 %all-to-all-start.4 = ((bf16[4,2,128,256]{3,2,1,0:T(8,128)(2,1)}), bf16[4,2,128,256]{3,2,1,0:T(8,128)(2,1)S(1)}, u32[]{:S(2)}, u32[]{:S(2)}) async-start(bf16[4,2,128,256]{3,2,1,0:T(8,128)(2,1)} %add_convert_fusion), calls=%async_computation.4 | async-start | bytes 1048576 | tf_op jit(solution)/shard_map/all_to_all | solution.py:458
  119.4 26.6 %collective-permute-start.2 = (bf16[128,512]{1,0:T(8,128)(2,1)S(1)}, bf16[128,512]{1,0:T(8,128)(2,1)S(1)}, u32[]{:S(2)}, u32[]{:S(2)}) collective-permute-start(bf16[128,512]{1,0:T(8,128)(2,1)S(1)} %select_convert_fusion), channel_id=1, source_target_pairs={{0,1},{1,0},{2,3},{3,2},{4,5},{5,4},{6,7},{7,6},{8,9},{9,8},{10,11... | collective-permute-start | bytes 393224 | tf_op jit(solution)/shard_map/ppermute | solution.py:368
  128.8 17.9 %collective-permute-start.3 = (bf16[128,256]{1,0:T(8,128)(2,1)S(1)}, bf16[128,256]{1,0:T(8,128)(2,1)S(1)}, u32[]{:S(2)}, u32[]{:S(2)}) collective-permute-start(bf16[128,256]{1,0:T(8,128)(2,1)S(1)} %copy-done.8), channel_id=1, source_target_pairs={{0,16},{16,0},{32,48},{48,32},{1,17},{17,1},{33,49},{49,33},{2,18}... | collective-permute-start | bytes 196616 | tf_op jit(solution)/shard_map/ppermute | solution.py:457
  131.0 15.7 %collective-permute-start.4 = (bf16[128,256]{1,0:T(8,128)(2,1)S(1)}, bf16[128,256]{1,0:T(8,128)(2,1)S(1)}, u32[]{:S(2)}, u32[]{:S(2)}) collective-permute-start(bf16[128,256]{1,0:T(8,128)(2,1)S(1)} %copy-done.6), channel_id=1, source_target_pairs={{0,32},{16,48},{32,0},{48,16},{1,33},{17,49},{33,1},{49,17},{2,34}... | collective-permute-start | bytes 196616 | tf_op jit(solution)/shard_map/ppermute | solution.py:457
  136.2 10.6 %collective-permute-start.5 = (bf16[128,256]{1,0:T(8,128)(2,1)S(1)}, bf16[128,256]{1,0:T(8,128)(2,1)S(1)}, u32[]{:S(2)}, u32[]{:S(2)}) collective-permute-start(bf16[128,256]{1,0:T(8,128)(2,1)S(1)} %copy-done.4), channel_id=1, source_target_pairs={{0,48},{16,32},{32,16},{48,0},{1,49},{17,33},{33,17},{49,1},{2,50}... | collective-permute-start | bytes 196616 | tf_op jit(solution)/shard_map/ppermute | solution.py:457
  146.8 10.8 %collective-permute-start.6 = (bf16[128,256]{1,0:T(8,128)(2,1)S(1)}, bf16[128,256]{1,0:T(8,128)(2,1)S(1)}, u32[]{:S(2)}, u32[]{:S(2)}) collective-permute-start(bf16[128,256]{1,0:T(8,128)(2,1)S(1)} %slice_reduce_fusion), channel_id=1, source_target_pairs={{0,256},{256,0},{1,257},{257,1},{2,258},{258,2},{3,259},{259,3},{4... | collective-permute-start | bytes 196616 | tf_op jit(solution)/shard_map/ppermute | solution.py:368
